TPU v7x, 32 devices: a whole 2x2x4 slice. The times are simulated.
32 devices in a mesh: dp: 16 (over z, y, core), space: 2 (over x).
Axes of the slice: x: 2, y: 2, z: 4, core: 2. Of those that a mesh axis runs over, the one named last changes fastest.
Arguments:
- volumes: bfloat16 [16, 16, 8, 16, 256], P('dp', 'space'), may hold values from -6 to 6
- cotangent: bfloat16 [16, 16, 8, 16, 256], P('dp', 'space'), may hold values from -6 to 6
- first_weight: float32 [256, 6912], P('dp'), may hold values from -0.078125 to 0.078125
- second_weight: float32 [256, 6912], P('dp'), may hold values from -0.078125 to 0.078125
- first_noise: float32 [256, 6912], P('dp'), may hold values from -6 to 6
- second_noise: float32 [256, 6912], P('dp'), may hold values from -6 to 6
Outputs:
- outputs: bfloat16 [16, 16, 8, 16, 256], P('dp', 'space')
- input_grads: bfloat16 [16, 16, 8, 16, 256], P('dp', 'space')
- new_first: float32 [256, 6912], P('dp')
- new_second: float32 [256, 6912], P('dp')
All inputs are finite; a program needn't handle non-finite values.
Results may differ from a plain program's by a relative error of at most 0.014.
Values may be sent and summed in bfloat16 or wider, within the bound.
No kernel may reach another device: no remote copies, remote signals or barrier semaphores. Data moves between devices by JAX's collectives and lax.ppermute only.
A program may use at most 192 MiB of HBM per device.

v0:
```python
import functools
import math

import jax
import jax.numpy as jnp
from jax import lax
from jax.experimental import pallas as pl
from jax.experimental.pallas import tpu as pltpu
from jax.sharding import PartitionSpec as P

NOISE_COEF = 0.25
BF = jnp.bfloat16
F32 = jnp.float32
VMEM_LIMIT = 56 * 2**20


def dot(a, b):
    return jnp.dot(a, b, preferred_element_type=F32)


def dot_nt(a, b):
    return lax.dot_general(a, b, (((1,), (1,)), ((), ())), preferred_element_type=F32)


def reverse_bits(value, bits):
    total = jnp.zeros_like(value)
    for b in range(bits):
        total = total | (((value >> b) & 1) << (bits - 1 - b))
    return total


def relative_matrix(k, size, rows, bits):
    rel = lax.broadcasted_iota(jnp.int32, (size, size), 0)
    nat = lax.broadcasted_iota(jnp.int32, (size, size), 1)
    want = (k ^ reverse_bits(rel // rows, bits)) * rows + rel % rows
    return jnp.where(want == nat, 1.0, 0.0).astype(BF)


def member_matrix(h, channels, half):
    chan = lax.broadcasted_iota(jnp.int32, (channels, channels // 2), 0)
    hid = lax.broadcasted_iota(jnp.int32, (channels, channels // 2), 1)
    want = (hid // half) * (2 * half) + h * half + hid % half
    return jnp.where(want == chan, 1.0, 0.0).astype(BF)


def shift_matrix(cells, width):
    out = lax.broadcasted_iota(jnp.int32, (2 * cells, cells), 0)
    src = lax.broadcasted_iota(jnp.int32, (2 * cells, cells), 1)
    step = jnp.where(out < cells, -1, 1)
    cell = out % cells
    inside = (cell % width + step >= 0) & (cell % width + step < width)
    return jnp.where(inside & (src == cell + step), 1.0, 0.0).astype(BF)


def clear_border(t3, width, area):
    planes = t3.shape[1] - 2
    zero = jnp.zeros((3, planes + 2, width, t3.shape[3]), BF)
    t3[:, :, 0:width, :] = zero
    t3[:, :, width + area : 2 * width + area, :] = zero
    plane = jnp.zeros((3, area, t3.shape[3]), BF)
    t3[:, 0, width : width + area, :] = plane
    t3[:, planes + 1, width : width + area, :] = plane


def store_shifted(t3, plane, value, shifts, width, area):
    both = dot(shifts, value).astype(BF)
    channels = value.shape[1]
    rows = slice(width, width + area)
    t3[0, plane : plane + 2, rows, :] = both[: 2 * area].reshape(2, area, channels)
    t3[1, plane : plane + 2, rows, :] = value.reshape(2, area, channels)
    t3[2, plane : plane + 2, rows, :] = both[2 * area :].reshape(2, area, channels)


def window(t3, c, plane, count, b, width, area):
    block = t3[c, pl.ds(plane, count), b * width : b * width + area, :]
    return block.reshape(count * area, t3.shape[3])


def weights_kernel(half, idx, first, second, w1, w2):
    h = idx[1]
    channels = 2 * w1.shape[1] // 27
    hid = channels // 2
    select = member_matrix(h, channels, half)
    for a in range(3):
        for bc in range(9):
            t = a * 9 + bc
            u = bc * 3 + a
            taps = first[:, t * channels : (t + 1) * channels].astype(BF)
            w1[:, u * hid : (u + 1) * hid] = dot(taps, select).astype(BF)
    w2[...] = jnp.where(h == 0, second[0:half, :], second[half : 2 * half, :]).astype(BF)


def spread_kernel(dims, relative, idx, own, other, t3, *rest):
    slab, width, area, rows, bits = dims
    k, h = idx[0], idx[1]
    channels = t3.shape[3]
    clear_border(t3, width, area)
    shifts = shift_matrix(2 * area, width)
    if relative:
        matrix = relative_matrix(k, channels, rows, bits)
    for pair in range(slab):
        plane = 2 * pair
        member, inside = plane // slab, plane % slab
        mine = own[inside : inside + 2].reshape(2 * area, channels)
        theirs = other[inside : inside + 2].reshape(2 * area, channels)
        value = jnp.where(h == member, mine, theirs)
        if relative:
            rest[0][:, plane * area : (plane + 2) * area] = dot_nt(matrix, value).astype(BF)
            value = dot_nt(value, matrix).astype(BF)
        store_shifted(t3, plane + 1, value, shifts, width, area)


def planes_of(halo, planes):
    if halo:
        return [(p, 2) for p in range(0, planes + 2, 2)]
    return [(1 + p, planes // 2) for p in range(0, planes, planes // 2)]


def hidden_kernel(dims, halo, idx, x3, w1, a3, at, slope, z):
    slab, width, area, rows, bits = dims
    k = idx[0]
    hid = w1.shape[1] // 27
    planes = 2 * slab
    for plane, count in planes_of(halo, planes):
        total = None
        for b in range(3):
            for c in range(3):
                u = b * 3 + c
                part = dot(window(x3, c, plane, count, b, width, area), w1[:, u * 3 * hid : (u + 1) * 3 * hid])
                total = part if total is None else total + part
        z[plane : plane + count] = total.reshape(count, area, 3 * hid)
    if not halo:
        z[0] = jnp.zeros((area, 3 * hid), F32)
        z[planes + 1] = jnp.zeros((area, 3 * hid), F32)
    clear_border(a3, width, area)
    shifts = shift_matrix(2 * area, width)
    matrix = relative_matrix(k, hid, rows // 2, bits)
    for d in range(0, planes, 2):
        hidden = z[d : d + 2, :, 0:hid] + z[d + 1 : d + 3, :, hid : 2 * hid] + z[d + 2 : d + 4, :, 2 * hid : 3 * hid]
        hidden = hidden.reshape(2 * area, hid)
        sigma = jax.nn.sigmoid(hidden)
        active = (hidden * sigma).astype(BF)
        grad = (sigma * (1.0 + hidden * (1.0 - sigma))).astype(BF)
        at[:, d * area : (d + 2) * area] = dot_nt(matrix, active).astype(BF)
        slope[d : d + 2] = dot_nt(grad, matrix).astype(BF).reshape(2, area, hid)
        store_shifted(a3, d + 1, dot_nt(active, matrix).astype(BF), shifts, width, area)


def second_grad_kernel(dims, at, c3, keep, send):
    slab, width, area, rows, bits = dims
    channels = c3.shape[3]
    half = keep.shape[0]
    for a in range(3):
        for b in range(3):
            for c in range(3):
                t = (a * 3 + b) * 3 + c
                right = window(c3, 2 - c, 2 - a, 2 * slab, 2 - b, width, area)
                value = dot(at[...], right).astype(BF)
                keep[:, t * channels : (t + 1) * channels] = value[:half]
                send[:, t * channels : (t + 1) * channels] = value[half:]


def hidden_grad_kernel(dims, halo, idx, c3, w2, slope, g3, z):
    slab, width, area, rows, bits = dims
    k = idx[0]
    hid = w2.shape[0]
    channels = c3.shape[3]
    planes = 2 * slab
    for plane, count in planes_of(halo, planes):
        total = None
        for b in range(3):
            for c in range(3):
                taps = [(a * 3 + b) * 3 + c for a in range(3)]
                right = jnp.concatenate([w2[:, t * channels : (t + 1) * channels] for t in taps], axis=0)
                part = dot_nt(window(c3, 2 - c, plane, count, 2 - b, width, area), right)
                total = part if total is None else total + part
        z[plane : plane + count] = total.reshape(count, area, 3 * hid)
    if not halo:
        z[0] = jnp.zeros((area, 3 * hid), F32)
        z[planes + 1] = jnp.zeros((area, 3 * hid), F32)
    clear_border(g3, width, area)
    shifts = shift_matrix(2 * area, width)
    matrix = relative_matrix(k, hid, rows // 2, bits)
    for d in range(0, planes, 2):
        grad = z[d + 2 : d + 4, :, 0:hid] + z[d + 1 : d + 3, :, hid : 2 * hid] + z[d : d + 2, :, 2 * hid : 3 * hid]
        grad = grad.reshape(2 * area, hid)
        value = (grad * slope[d : d + 2].reshape(2 * area, hid).astype(F32)).astype(BF)
        store_shifted(g3, d + 1, dot(value, matrix).astype(BF), shifts, width, area)


def first_grad_kernel(dims, xt, g3, keep, send):
    slab, width, area, rows, bits = dims
    hid = g3.shape[3]
    half = keep.shape[0]
    taps = [(a, b, c) for b in range(3) for c in range(3) for a in range(3)]
    for u in range(0, 27, 2):
        blocks = [window(g3, 2 - c, 2 - a, 2 * slab, 2 - b, width, area) for a, b, c in taps[u : u + 2]]
        right = jnp.concatenate(blocks, axis=1)
        value = dot(xt[...], right).astype(BF)
        keep[:, u * hid : (u + len(blocks)) * hid] = value[:half]
        send[:, u * hid : (u + len(blocks)) * hid] = value[half:]


def outputs_kernel(dims, idx, a3, w2, base, keep, send):
    slab, width, area, rows, bits = dims
    h = idx[1]
    channels = w2.shape[1] // 27
    taps = [(a, b, c) for a in range(3) for b in range(3) for c in range(3)]
    for mine in (False, True):
        start = (h if mine else 1 - h) * slab
        total = None
        for t in range(0, 27, 2):
            left = [window(a3, c, start + a, slab, b, width, area) for a, b, c in taps[t : t + 2]]
            right = [w2[:, v * channels : (v + 1) * channels] for v in range(t, t + len(left))]
            part = dot(jnp.concatenate(left, axis=1), jnp.concatenate(right, axis=0))
            total = part if total is None else total + part
        total = total.reshape(slab, area, channels)
        if mine:
            keep[...] = base[...].astype(F32) + total
        else:
            send[...] = total.astype(BF)


def input_grads_kernel(dims, idx, g3, w1, base, keep, send):
    slab, width, area, rows, bits = dims
    k, h = idx[0], idx[1]
    hid = w1.shape[1] // 27
    channels = w1.shape[0]
    matrix = relative_matrix(k, channels, rows, bits)
    taps = [(a, b, c) for b in range(3) for c in range(3) for a in range(3)]
    for mine in (False, True):
        start = (h if mine else 1 - h) * slab
        total = None
        for u in range(0, 27, 2):
            left = [window(g3, 2 - c, start + 2 - a, slab, 2 - b, width, area) for a, b, c in taps[u : u + 2]]
            part = dot_nt(jnp.concatenate(left, axis=1), w1[:, u * hid : (u + len(left)) * hid])
            total = part if total is None else total + part
        high = total.astype(BF)
        natural = dot(high, matrix)
        if mine:
            low = (total - high.astype(F32)).astype(BF)
            natural = natural + dot(low, matrix)
            keep[...] = base[...].astype(F32) + natural.reshape(slab, area, channels)
        else:
            send[...] = natural.astype(BF).reshape(slab, area, channels)


def update_kernel(half, rate, idx, own1, other1, own2, other2, first, second, noise1, noise2, new1, new2):
    h = idx[1]
    hid = own1.shape[1] // 27
    channels = 2 * hid
    mine = member_matrix(h, channels, half)
    theirs = member_matrix(1 - h, channels, half)
    for a in range(3):
        for bc in range(9):
            t = a * 9 + bc
            u = bc * 3 + a
            cols = slice(t * channels, (t + 1) * channels)
            part = slice(u * hid, (u + 1) * hid)
            grad = dot_nt(own1[:, part], mine) + dot_nt(other1[:, part], theirs)
            new1[:, cols] = first[:, cols] - rate * grad + NOISE_COEF * noise1[:, cols]
    mine2 = own2[...].astype(F32)
    theirs2 = other2[...].astype(F32)
    low = jnp.where(h == 0, mine2, theirs2)
    high = jnp.where(h == 0, theirs2, mine2)
    new2[0:half, :] = second[0:half, :] - rate * low + NOISE_COEF * noise2[0:half, :]
    new2[half : 2 * half, :] = (
        second[half : 2 * half, :] - rate * high + NOISE_COEF * noise2[half : 2 * half, :]
    )


def run(kernel, args, outs, name, flops, scalars=1, scratch=()):
    moved = sum(math.prod(a.shape) * a.dtype.itemsize for a in (*args, *outs))
    smem = pl.BlockSpec(memory_space=pltpu.SMEM)
    vmem = pl.BlockSpec(memory_space=pltpu.VMEM)
    return pl.pallas_call(
        kernel,
        out_shape=tuple(outs),
        in_specs=[smem] * scalars + [vmem] * (len(args) - scalars),
        out_specs=tuple([vmem] * len(outs)),
        scratch_shapes=list(scratch),
        compiler_params=pltpu.CompilerParams(vmem_limit_bytes=VMEM_LIMIT),
        cost_estimate=pl.CostEstimate(flops=flops, bytes_accessed=moved, transcendentals=0),
        name=name,
    )(*args)


def trade(array, axis, bit):
    size = lax.axis_size(axis)
    return lax.ppermute(array, axis, [(i, i ^ bit) for i in range(size)])


def gather(array, bits):
    for b in range(bits - 1, -1, -1):
        array = jnp.concatenate([array, trade(array, "dp", 1 << b)], axis=0)
    return array


def add(a, b):
    return (a.astype(F32) + b.astype(F32)).astype(BF)


def scatter(keep, send, bits):
    for b in range(bits):
        came = trade(send, "dp", 1 << b)
        if b == bits - 1:
            keep = add(keep, came)
        else:
            half = keep.shape[0] // 2
            keep, send = add(keep[:half], came[:half]), add(keep[half:], came[half:])
    pairs = lax.axis_size("space") // 2
    step = 1
    while step < pairs:
        keep = add(keep, trade(keep, "space", 2 * step))
        step *= 2
    return keep


def with_halo(t3):
    size = lax.axis_size("space")
    if size == 2:
        return t3
    last = t3.shape[1] - 1
    before = lax.ppermute(t3[:, last - 1], "space", [(i, i + 2) for i in range(size - 2)])
    after = lax.ppermute(t3[:, 1], "space", [(i + 2, i) for i in range(size - 2)])
    return t3.at[:, 0].set(before).at[:, last].set(after)


def body(volumes, cotangent, first_weight, second_weight, first_noise, second_noise):
    _, slab, height, width, channels = volumes.shape
    area = height * width
    hid = channels // 2
    devices = lax.axis_size("dp")
    members = lax.axis_size("space")
    rows = channels // devices
    half = rows // 2
    bits = devices.bit_length() - 1
    dims = (slab, width, area, rows, bits)
    halo = members > 2
    planes = 2 * slab
    cells = planes * area
    heavy = 2 * cells * 27 * channels * hid
    idx = jnp.stack([lax.axis_index("dp"), lax.axis_index("space") % 2]).astype(jnp.int32)
    volume = volumes.reshape(slab, area, channels)
    upstream = cotangent.reshape(slab, area, channels)
    shape = jax.ShapeDtypeStruct

    def padded(count):
        return shape((3, planes + 2, area + 2 * width, count), BF)

    w1, w2 = run(
        functools.partial(weights_kernel, half),
        (idx, first_weight, second_weight),
        (shape((rows, 27 * hid), BF), shape((half, 27 * channels), BF)),
        "weights",
        2 * rows * 27 * channels * hid,
    )
    w1 = gather(w1, bits)
    other_volume = trade(volume, "space", 1)
    x3, xt = run(
        functools.partial(spread_kernel, dims, True),
        (idx, volume, other_volume),
        (padded(channels), shape((channels, cells), BF)),
        "spread_volumes",
        8 * cells * channels * channels,
    )
    x3 = with_halo(x3)
    other_upstream = trade(upstream, "space", 1)
    (c3,) = run(
        functools.partial(spread_kernel, dims, False),
        (idx, upstream, other_upstream),
        (padded(channels),),
        "spread_cotangent",
        4 * cells * channels * channels,
    )
    c3 = with_halo(c3)
    w2 = gather(w2, bits)
    scratch = [pltpu.VMEM((planes + 2, area, 3 * hid), F32)]
    a3, at, slope = run(
        functools.partial(hidden_kernel, dims, halo),
        (idx, x3, w1),
        (padded(hid), shape((hid, cells), BF), shape((planes, area, hid), BF)),
        "hidden",
        heavy,
        scratch=scratch,
    )
    a3 = with_halo(a3)
    keep2, send2 = run(
        functools.partial(second_grad_kernel, dims),
        (at, c3),
        (shape((hid // 2, 27 * channels), BF),) * 2,
        "second_grad",
        heavy,
        scalars=0,
    )
    share2 = scatter(keep2, send2, bits)
    (g3,) = run(
        functools.partial(hidden_grad_kernel, dims, halo),
        (idx, c3, w2, slope),
        (padded(hid),),
        "hidden_grad",
        heavy,
        scratch=scratch,
    )
    g3 = with_halo(g3)
    keep1, send1 = run(
        functools.partial(first_grad_kernel, dims),
        (xt, g3),
        (shape((channels // 2, 27 * hid), BF),) * 2,
        "first_grad",
        heavy,
        scalars=0,
    )
    share1 = scatter(keep1, send1, bits)
    parts = (shape((slab, area, channels), F32), shape((slab, area, channels), BF))
    own_out, send_out = run(
        functools.partial(outputs_kernel, dims), (idx, a3, w2, volume), parts, "outputs", heavy
    )
    came_out = trade(send_out, "space", 1)
    own_in, send_in = run(
        functools.partial(input_grads_kernel, dims), (idx, g3, w1, upstream), parts, "input_grads", heavy
    )
    came_in = trade(send_in, "space", 1)
    outputs = (own_out + came_out.astype(F32)).astype(BF).reshape(volumes.shape)
    input_grads = (own_in + came_in.astype(F32)).astype(BF).reshape(volumes.shape)
    other2 = trade(share2, "space", 1)
    other1 = trade(share1, "space", 1)
    rate = 1.0 / math.sqrt(slab * area * devices * members)
    new_first, new_second = run(
        functools.partial(update_kernel, half, rate),
        (idx, share1, other1, share2, other2, first_weight, second_weight, first_noise, second_noise),
        (shape(first_weight.shape, F32),) * 2,
        "update",
        4 * rows * 27 * channels * hid,
    )
    return (outputs, input_grads, new_first, new_second)


def solution(mesh):
    cells = P("dp", "space", None, None, None)
    rows = P("dp", None)
    return jax.shard_map(
        body,
        mesh=mesh,
        in_specs=(cells, cells, rows, rows, rows, rows),
        out_specs=(cells, cells, rows, rows),
        check_vma=False,
    )
```

profile of v0, /device:TPU:0, one launch (start us, length us, event | category | flops | bytes accessed | tf_op | source)
XLA Modules:
  0.0 153.1 jit_solution(11324871469347189552)
XLA Ops:
  0.6 3.0 %collective-permute-start = (bf16[8,128,256]{2,1,0:T(8,128)(2,1)}, bf16[8,128,256]{2,1,0:T(8,128)(2,1)S(1)}, u32[]{:S(2)}, u32[]{:S(2)}) collective-permute-start(bf16[8,128,256]{2,1,0:T(8,128)(2,1)} %bitcast.11), channel_id=1, source_target_pairs={{0,1},{1,0},{2,3},{3,2},{4,5},{5,4},{6,7},{7,6},{8,9},{9,8},{10,11... | collective-permute-start | bytes 1572872 | tf_op jit(solution)/shard_map/ppermute | solution.py:290
  3.6 0.6 pad_add_fusion.idx
  4.2 2.2 %weights.1 = (bf16[16,3456]{1,0:T(8,128)(2,1)}, bf16[8,6912]{1,0:T(8,128)(2,1)}) custom-call(s32[2]{0:T(128)} %pad_add_fusion.idx, f32[16,6912]{1,0:T(8,128)} %first.3, f32[16,6912]{1,0:T(8,128)} %second.3), custom_call_target="tpu_custom_call" | custom-call | flops 28311552 | bytes 1105928 | tf_op jit(solution)/shard_map/weights/pallas_call | solution.py:276
  6.4 2.6 %collective-permute-start.1 = (bf16[16,3456]{1,0:T(8,128)(2,1)}, bf16[16,3456]{1,0:T(8,128)(2,1)S(1)}, u32[]{:S(2)}, u32[]{:S(2)}) collective-permute-start(bf16[16,3456]{1,0:T(8,128)(2,1)} %get-tuple-element.22), channel_id=1, source_target_pairs={{0,16},{2,18},{4,20},{6,22},{8,24},{10,26},{12,28},{14,30},{16,0},... | collective-permute-start | bytes 331784 | tf_op jit(solution)/shard_map/ppermute | solution.py:290
  9.0 0.3 collective-permute-start.5
  9.3 0.3 collective-permute-start.10
  9.6 0.9 constant_dynamic-update-slice_fusion.9
  10.5 0.9 constant_dynamic-update-slice_fusion.4
  11.4 6.5 %collective-permute-done.1 = bf16[16,3456]{1,0:T(8,128)(2,1)S(1)} collective-permute-done((bf16[16,3456]{1,0:T(8,128)(2,1)}, bf16[16,3456]{1,0:T(8,128)(2,1)S(1)}, u32[]{:S(2)}, u32[]{:S(2)}) %collective-permute-start.1) | collective-permute-done | bytes 110624 | tf_op jit(solution)/shard_map/ppermute | solution.py:290
  17.9 0.9 pad_maximum_fusion.4
  18.9 0.1 collective-permute-start.2
  18.9 0.2 collective-permute-done.5
  19.1 0.9 pad_maximum_fusion.5
  20.1 1.9 %collective-permute-start.6 = (bf16[16,6912]{1,0:T(8,128)(2,1)S(1)}, bf16[16,6912]{1,0:T(8,128)(2,1)S(1)}, u32[]{:S(2)}, u32[]{:S(2)}) collective-permute-start(bf16[16,6912]{1,0:T(8,128)(2,1)S(1)} %pad_maximum_fusion.5), channel_id=1, source_target_pairs={{0,8},{2,10},{4,12},{6,14},{8,0},{10,2},{12,4},{14,6},{16,24},{18,... | collective-permute-start | bytes 663560 | tf_op jit(solution)/shard_map/ppermute | solution.py:290
  22.0 4.6 %collective-permute-done.2 = bf16[32,3456]{1,0:T(8,128)(2,1)S(1)} collective-permute-done((bf16[32,3456]{1,0:T(8,128)(2,1)S(1)}, bf16[32,3456]{1,0:T(8,128)(2,1)S(1)}, u32[]{:S(2)}, u32[]{:S(2)}) %collective-permute-start.2) | collective-permute-done | bytes 221216 | tf_op jit(solution)/shard_map/ppermute | solution.py:290
  26.6 1.6 %collective-permute-start.3 = (bf16[64,3456]{1,0:T(8,128)(2,1)S(1)}, bf16[64,3456]{1,0:T(8,128)(2,1)S(1)}, u32[]{:S(2)}, u32[]{:S(2)}) collective-permute-start(bf16[64,3456]{1,0:T(8,128)(2,1)S(1)} %pad_maximum_fusion.2), channel_id=1, source_target_pairs={{0,4},{2,6},{4,0},{6,2},{8,12},{10,14},{12,8},{14,10},{16,20},{18,... | collective-permute-start | bytes 1327112 | tf_op jit(solution)/shard_map/ppermute | solution.py:290
  28.2 0.7 collective-permute-done.6
  29.0 1.6 %collective-permute-start.7 = (bf16[32,6912]{1,0:T(8,128)(2,1)S(1)}, bf16[32,6912]{1,0:T(8,128)(2,1)S(1)}, u32[]{:S(2)}, u32[]{:S(2)}) collective-permute-start(bf16[32,6912]{1,0:T(8,128)(2,1)S(1)} %pad_maximum_fusion.3), channel_id=1, source_target_pairs={{0,4},{2,6},{4,0},{6,2},{8,12},{10,14},{12,8},{14,10},{16,20},{18,... | collective-permute-start | bytes 1327112 | tf_op jit(solution)/shard_map/ppermute | solution.py:290
  30.6 0.0 copy-start.6
  30.6 0.8 copy-done.6
  31.4 4.0 %spread_cotangent.1.c3 = bf16[3,18,160,256]{3,2,1,0:T(8,128)(2,1)} custom-call(s32[2]{0:T(128)} %pad_add_fusion.idx, bf16[8,128,256]{2,1,0:T(8,128)(2,1)} %bitcast.9, bf16[8,128,256]{2,1,0:T(8,128)(2,1)} %copy-done.6), custom_call_target="tpu_custom_call" | custom-call | flops 536870912 | bytes 5472264 | tf_op jit(solution)/shard_map/spread_cotangent/pallas_call | solution.py:276
  35.5 0.8 copy-done.13
  36.2 4.8 %spread_volumes.1 = (bf16[3,18,160,256]{3,2,1,0:T(8,128)(2,1)}, bf16[256,2048]{1,0:T(8,128)(2,1)}) custom-call(s32[2]{0:T(128)} %pad_add_fusion.idx, bf16[8,128,256]{2,1,0:T(8,128)(2,1)} %bitcast.12, bf16[8,128,256]{2,1,0:T(8,128)(2,1)} %copy-done.13), custom_call_target="tpu_custom_call" | custom-call | flops 1073741824 | bytes 6520840 | tf_op jit(solution)/shard_map/spread_volumes/pallas_call | solution.py:276
  41.1 0.1 pad_maximum_fusion
  41.2 0.1 collective-permute-start.4
  41.3 2.5 %collective-permute-done.7 = bf16[32,6912]{1,0:T(8,128)(2,1)S(1)} collective-permute-done((bf16[32,6912]{1,0:T(8,128)(2,1)S(1)}, bf16[32,6912]{1,0:T(8,128)(2,1)S(1)}, u32[]{:S(2)}, u32[]{:S(2)}) %collective-permute-start.7) | collective-permute-done | bytes 442400 | tf_op jit(solution)/shard_map/ppermute | solution.py:290
  43.8 0.1 pad_maximum_fusion.1
  43.8 0.1 collective-permute-start.8
  44.0 0.1 constant_dynamic-update-slice_fusion.w1
  44.1 1.3 copy-done.11
  45.4 10.7 %hidden.1 = (bf16[3,18,160,128]{3,2,1,0:T(8,128)(2,1)}, bf16[128,2048]{1,0:T(8,128)(2,1)}, bf16[16,128,128]{2,1,0:T(8,128)(2,1)}) custom-call(s32[2]{0:T(128)} %pad_add_fusion.idx, bf16[3,18,160,256]{3,2,1,0:T(8,128)(2,1)} %get-tuple-element.21.x3, bf16[256,3456]{1,0:T(8,128)(2,1)} %copy-done.11), custom_call_target="tpu_custom_call" | custom-call | flops 3623878656 | bytes 9453576 | tf_op jit(solution)/shard_map/hidden/pallas_call | solution.py:276
  56.2 0.1 constant_dynamic-update-slice_fusion.5.w2
  56.2 1.3 copy-done.12
  57.5 7.3 %outputs.1 = (f32[8,128,256]{2,1,0:T(8,128)}, bf16[8,128,256]{2,1,0:T(8,128)(2,1)}) custom-call(s32[2]{0:T(128)} %pad_add_fusion.idx, bf16[3,18,160,128]{3,2,1,0:T(8,128)(2,1)} %get-tuple-element.23.a3, bf16[128,6912]{1,0:T(8,128)(2,1)} %copy-done.12, bf16[8,128,256]{2,1,0:T(8,128)(2,1)} %bitcast.13), custom_call_target="tpu_custom_call" | custom-call | flops 3623878656 | bytes 6078472 | tf_op jit(solution)/shard_map/outputs/pallas_call | solution.py:276
  64.8 0.6 collective-permute-start.9
  65.4 10.6 %hidden_grad.1.g3 = bf16[3,18,160,128]{3,2,1,0:T(8,128)(2,1)} custom-call(s32[2]{0:T(128)} %pad_add_fusion.idx, bf16[3,18,160,256]{3,2,1,0:T(8,128)(2,1)} %spread_cotangent.1.c3, bf16[128,6912]{1,0:T(8,128)(2,1)} %copy-done.12, bf16[16,128,128]{2,1,0:T(8,128)(2,1)} %get-tuple-element.27.slope), custom_call_target="tpu_custom_call" | custom-call | flops 3623878656 | bytes 8929288 | tf_op jit(solution)/shard_map/hidden_grad/pallas_call | solution.py:276
  76.1 7.1 %first_grad.1 = (bf16[128,3456]{1,0:T(8,128)(2,1)}, bf16[128,3456]{1,0:T(8,128)(2,1)}) custom-call(bf16[256,2048]{1,0:T(8,128)(2,1)} %get-tuple-element.30.xt, bf16[3,18,160,128]{3,2,1,0:T(8,128)(2,1)} %hidden_grad.1.g3), custom_call_target="tpu_custom_call" | custom-call | flops 3623878656 | bytes 5029888 | tf_op jit(solution)/shard_map/first_grad/pallas_call | solution.py:276
  83.2 0.2 collective-permute-start.12
  83.4 11.5 %input_grads.1 = (f32[8,128,256]{2,1,0:T(8,128)}, bf16[8,128,256]{2,1,0:T(8,128)(2,1)}) custom-call(s32[2]{0:T(128)} %pad_add_fusion.idx, bf16[3,18,160,128]{3,2,1,0:T(8,128)(2,1)} %hidden_grad.1.g3, bf16[256,3456]{1,0:T(8,128)(2,1)} %copy-done.11, bf16[8,128,256]{2,1,0:T(8,128)(2,1)} %bitcast.10), custom_call_target="tpu_custom_call" | custom-call | flops 3623878656 | bytes 6078472 | tf_op jit(solution)/shard_map/input_grads/pallas_call | solution.py:276
  94.9 1.4 collective-permute-start.11
  96.4 7.8 %second_grad.1 = (bf16[64,6912]{1,0:T(8,128)(2,1)}, bf16[64,6912]{1,0:T(8,128)(2,1)}) custom-call(bf16[128,2048]{1,0:T(8,128)(2,1)} %get-tuple-element.33.at, bf16[3,18,160,256]{3,2,1,0:T(8,128)(2,1)} %spread_cotangent.1.c3), custom_call_target="tpu_custom_call" | custom-call | flops 3623878656 | bytes 6717440 | tf_op jit(solution)/shard_map/second_grad/pallas_call | solution.py:276
  104.2 0.0 collective-permute-start.17
  104.2 0.9 add_convert_fusion.1
  105.1 0.4 copy-done.4
  105.6 0.2 add_convert_fusion.5
  105.8 1.6 %collective-permute-start.13 = (bf16[64,3456]{1,0:T(8,128)(2,1)S(1)}, bf16[64,3456]{1,0:T(8,128)(2,1)S(1)}, u32[]{:S(2)}, u32[]{:S(2)}) collective-permute-start(bf16[64,3456]{1,0:T(8,128)(2,1)S(1)} %get-tuple-element.41), channel_id=1, source_target_pairs={{0,4},{2,6},{4,0},{6,2},{8,12},{10,14},{12,8},{14,10},{16,20},{18,... | collective-permute-start | bytes 1327112 | tf_op jit(solution)/shard_map/ppermute | solution.py:290
  107.4 0.2 add_convert_fusion.3
  107.6 1.1 collective-permute-start.18
  108.6 10.2 %collective-permute-done.13 = bf16[64,3456]{1,0:T(8,128)(2,1)S(1)} collective-permute-done((bf16[64,3456]{1,0:T(8,128)(2,1)S(1)}, bf16[64,3456]{1,0:T(8,128)(2,1)S(1)}, u32[]{:S(2)}, u32[]{:S(2)}) %collective-permute-start.13) | collective-permute-done | bytes 442400 | tf_op jit(solution)/shard_map/ppermute | solution.py:290
  118.8 0.1 add_convert_fusion.9
  119.0 2.5 %collective-permute-start.14 = (bf16[32,3456]{1,0:T(8,128)(2,1)S(1)}, bf16[32,3456]{1,0:T(8,128)(2,1)S(1)}, u32[]{:S(2)}, u32[]{:S(2)}) collective-permute-start(bf16[32,3456]{1,0:T(8,128)(2,1)S(1)} %get-tuple-element.45), channel_id=1, source_target_pairs={{0,8},{2,10},{4,12},{6,14},{8,0},{10,2},{12,4},{14,6},{16,24},{18,... | collective-permute-start | bytes 663560 | tf_op jit(solution)/shard_map/ppermute | solution.py:290
  121.5 6.0 %collective-permute-done.18 = bf16[32,6912]{1,0:T(8,128)(2,1)S(1)} collective-permute-done((bf16[32,6912]{1,0:T(8,128)(2,1)S(1)}, bf16[32,6912]{1,0:T(8,128)(2,1)S(1)}, u32[]{:S(2)}, u32[]{:S(2)}) %collective-permute-start.18) | collective-permute-done | bytes 442400 | tf_op jit(solution)/shard_map/ppermute | solution.py:290
  127.5 0.1 add_convert_fusion.7
  127.6 2.5 %collective-permute-start.19 = (bf16[16,6912]{1,0:T(8,128)(2,1)S(1)}, bf16[16,6912]{1,0:T(8,128)(2,1)S(1)}, u32[]{:S(2)}, u32[]{:S(2)}) collective-permute-start(bf16[16,6912]{1,0:T(8,128)(2,1)S(1)} %get-tuple-element.43), channel_id=1, source_target_pairs={{0,8},{2,10},{4,12},{6,14},{8,0},{10,2},{12,4},{14,6},{16,24},{18,... | collective-permute-start | bytes 663560 | tf_op jit(solution)/shard_map/ppermute | solution.py:290
  130.2 3.7 %collective-permute-start.15 = (bf16[16,3456]{1,0:T(8,128)(2,1)S(1)}, bf16[16,3456]{1,0:T(8,128)(2,1)S(1)}, u32[]{:S(2)}, u32[]{:S(2)}) collective-permute-start(bf16[16,3456]{1,0:T(8,128)(2,1)S(1)} %add_convert_fusion.14), channel_id=1, source_target_pairs={{0,16},{2,18},{4,20},{6,22},{8,24},{10,26},{12,28},{14,30},{16,0},... | collective-permute-start | bytes 331784 | tf_op jit(solution)/shard_map/ppermute | solution.py:290
  133.9 3.5 %collective-permute-done.19 = bf16[16,6912]{1,0:T(8,128)(2,1)S(1)} collective-permute-done((bf16[16,6912]{1,0:T(8,128)(2,1)S(1)}, bf16[16,6912]{1,0:T(8,128)(2,1)S(1)}, u32[]{:S(2)}, u32[]{:S(2)}) %collective-permute-start.19) | collective-permute-done | bytes 221216 | tf_op jit(solution)/shard_map/ppermute | solution.py:290
  137.4 3.0 %collective-permute-start.20 = (bf16[8,6912]{1,0:T(8,128)(2,1)S(1)}, bf16[8,6912]{1,0:T(8,128)(2,1)S(1)}, u32[]{:S(2)}, u32[]{:S(2)}) collective-permute-start(bf16[8,6912]{1,0:T(8,128)(2,1)S(1)} %add_convert_fusion.11), channel_id=1, source_target_pairs={{0,16},{2,18},{4,20},{6,22},{8,24},{10,26},{12,28},{14,30},{16,0},... | collective-permute-start | bytes 331784 | tf_op jit(solution)/shard_map/ppermute | solution.py:290
  140.4 0.6 collective-permute-start.16
  141.0 2.9 %collective-permute-done.20 = bf16[8,6912]{1,0:T(8,128)(2,1)S(1)} collective-permute-done((bf16[8,6912]{1,0:T(8,128)(2,1)S(1)}, bf16[8,6912]{1,0:T(8,128)(2,1)S(1)}, u32[]{:S(2)}, u32[]{:S(2)}) %collective-permute-start.20) | collective-permute-done | bytes 110624 | tf_op jit(solution)/shard_map/ppermute | solution.py:290
  144.0 1.8 %collective-permute-start.21 = (bf16[8,6912]{1,0:T(8,128)(2,1)S(1)}, bf16[8,6912]{1,0:T(8,128)(2,1)S(1)}, u32[]{:S(2)}, u32[]{:S(2)}) collective-permute-start(bf16[8,6912]{1,0:T(8,128)(2,1)S(1)} %add_convert_fusion.10.own2), channel_id=1, source_target_pairs={{0,1},{1,0},{2,3},{3,2},{4,5},{5,4},{6,7},{7,6},{8,9},{9,8},{10,11... | collective-permute-start | bytes 331784 | tf_op jit(solution)/shard_map/ppermute | solution.py:290
  145.8 0.9 add_convert_fusion
  146.7 2.1 %collective-permute-done.21.other2 = bf16[8,6912]{1,0:T(8,128)(2,1)S(1)} collective-permute-done((bf16[8,6912]{1,0:T(8,128)(2,1)S(1)}, bf16[8,6912]{1,0:T(8,128)(2,1)S(1)}, u32[]{:S(2)}, u32[]{:S(2)}) %collective-permute-start.21) | collective-permute-done | bytes 110624 | tf_op jit(solution)/shard_map/ppermute | solution.py:290
  148.8 0.6 copy-done.10
  149.5 3.6 %update.1 = (f32[16,6912]{1,0:T(8,128)}, f32[16,6912]{1,0:T(8,128)}) custom-call(s32[2]{0:T(128)} %pad_add_fusion.idx, bf16[16,3456]{1,0:T(8,128)(2,1)} %copy-done.7, bf16[16,3456]{1,0:T(8,128)(2,1)} %copy-done.9, bf16[8,6912]{1,0:T(8,128)(2,1)} %copy-done.8, bf16[8,6912]{1,0:T(8,128)(2,1)} %copy-done.10, f32[16,6912]{1,0:T(8,128)} %first.3, ...), custom_call_target="tpu_custom_call" | custom-call | flops 56623104 | bytes 3096584 | tf_op jit(solution)/shard_map/update/pallas_call | solution.py:276
  (45 shorter events, 0.4 us)
Async XLA Ops:
  0.6 34.8 %collective-permute-start = (bf16[8,128,256]{2,1,0:T(8,128)(2,1)}, bf16[8,128,256]{2,1,0:T(8,128)(2,1)S(1)}, u32[]{:S(2)}, u32[]{:S(2)}) collective-permute-start(bf16[8,128,256]{2,1,0:T(8,128)(2,1)} %bitcast.11), channel_id=1, source_target_pairs={{0,1},{1,0},{2,3},{3,2},{4,5},{5,4},{6,7},{7,6},{8,9},{9,8},{10,11... | collective-permute-start | bytes 1572872 | tf_op jit(solution)/shard_map/ppermute | solution.py:290
  6.4 20.2 %copy-start.1 = (bf16[16,3456]{1,0:T(8,128)(2,1)S(1)}, bf16[16,3456]{1,0:T(8,128)(2,1)}, u32[]{:S(2)}) copy-start(bf16[16,3456]{1,0:T(8,128)(2,1)} %get-tuple-element.22) | copy-start | bytes 331780
  6.4 22.6 %copy-start = (bf16[8,6912]{1,0:T(8,128)(2,1)S(1)}, bf16[8,6912]{1,0:T(8,128)(2,1)}, u32[]{:S(2)}) copy-start(bf16[8,6912]{1,0:T(8,128)(2,1)} %get-tuple-element.24) | copy-start | bytes 331780
  6.4 11.5 %collective-permute-start.1 = (bf16[16,3456]{1,0:T(8,128)(2,1)}, bf16[16,3456]{1,0:T(8,128)(2,1)S(1)}, u32[]{:S(2)}, u32[]{:S(2)}) collective-permute-start(bf16[16,3456]{1,0:T(8,128)(2,1)} %get-tuple-element.22), channel_id=1, source_target_pairs={{0,16},{2,18},{4,20},{6,22},{8,24},{10,26},{12,28},{14,30},{16,0},... | collective-permute-start | bytes 331784 | tf_op jit(solution)/shard_map/ppermute | solution.py:290
  9.0 10.2 %collective-permute-start.5 = (bf16[8,6912]{1,0:T(8,128)(2,1)}, bf16[8,6912]{1,0:T(8,128)(2,1)S(1)}, u32[]{:S(2)}, u32[]{:S(2)}) collective-permute-start(bf16[8,6912]{1,0:T(8,128)(2,1)} %get-tuple-element.24), channel_id=1, source_target_pairs={{0,16},{2,18},{4,20},{6,22},{8,24},{10,26},{12,28},{14,30},{16,0},... | collective-permute-start | bytes 331784 | tf_op jit(solution)/shard_map/ppermute | solution.py:290
  9.3 21.3 %collective-permute-start.10 = (bf16[8,128,256]{2,1,0:T(8,128)(2,1)}, bf16[8,128,256]{2,1,0:T(8,128)(2,1)S(1)}, u32[]{:S(2)}, u32[]{:S(2)}) collective-permute-start(bf16[8,128,256]{2,1,0:T(8,128)(2,1)} %bitcast.8), channel_id=1, source_target_pairs={{0,1},{1,0},{2,3},{3,2},{4,5},{5,4},{6,7},{7,6},{8,9},{9,8},{10,11... | collective-permute-start | bytes 1572872 | tf_op jit(solution)/shard_map/ppermute | solution.py:290
  18.9 7.7 %collective-permute-start.2 = (bf16[32,3456]{1,0:T(8,128)(2,1)S(1)}, bf16[32,3456]{1,0:T(8,128)(2,1)S(1)}, u32[]{:S(2)}, u32[]{:S(2)}) collective-permute-start(bf16[32,3456]{1,0:T(8,128)(2,1)S(1)} %pad_maximum_fusion.4), channel_id=1, source_target_pairs={{0,8},{2,10},{4,12},{6,14},{8,0},{10,2},{12,4},{14,6},{16,24},{18,... | collective-permute-start | bytes 663560 | tf_op jit(solution)/shard_map/ppermute | solution.py:290
  20.1 8.9 %collective-permute-start.6 = (bf16[16,6912]{1,0:T(8,128)(2,1)S(1)}, bf16[16,6912]{1,0:T(8,128)(2,1)S(1)}, u32[]{:S(2)}, u32[]{:S(2)}) collective-permute-start(bf16[16,6912]{1,0:T(8,128)(2,1)S(1)} %pad_maximum_fusion.5), channel_id=1, source_target_pairs={{0,8},{2,10},{4,12},{6,14},{8,0},{10,2},{12,4},{14,6},{16,24},{18,... | collective-permute-start | bytes 663560 | tf_op jit(solution)/shard_map/ppermute | solution.py:290
  26.6 14.5 %collective-permute-start.3 = (bf16[64,3456]{1,0:T(8,128)(2,1)S(1)}, bf16[64,3456]{1,0:T(8,128)(2,1)S(1)}, u32[]{:S(2)}, u32[]{:S(2)}) collective-permute-start(bf16[64,3456]{1,0:T(8,128)(2,1)S(1)} %pad_maximum_fusion.2), channel_id=1, source_target_pairs={{0,4},{2,6},{4,0},{6,2},{8,12},{10,14},{12,8},{14,10},{16,20},{18,... | collective-permute-start | bytes 1327112 | tf_op jit(solution)/shard_map/ppermute | solution.py:290
  29.0 14.8 %collective-permute-start.7 = (bf16[32,6912]{1,0:T(8,128)(2,1)S(1)}, bf16[32,6912]{1,0:T(8,128)(2,1)S(1)}, u32[]{:S(2)}, u32[]{:S(2)}) collective-permute-start(bf16[32,6912]{1,0:T(8,128)(2,1)S(1)} %pad_maximum_fusion.3), channel_id=1, source_target_pairs={{0,4},{2,6},{4,0},{6,2},{8,12},{10,14},{12,8},{14,10},{16,20},{18,... | collective-permute-start | bytes 1327112 | tf_op jit(solution)/shard_map/ppermute | solution.py:290
  30.6 0.8 copy-start.6
  35.4 0.8 copy-start.13
  41.2 2.8 %collective-permute-start.4 = (bf16[128,3456]{1,0:T(8,128)(2,1)S(1)}, bf16[128,3456]{1,0:T(8,128)(2,1)S(1)}, u32[]{:S(2)}, u32[]{:S(2)}) collective-permute-start(bf16[128,3456]{1,0:T(8,128)(2,1)S(1)} %pad_maximum_fusion), channel_id=1, source_target_pairs={{0,2},{2,0},{4,6},{6,4},{8,10},{10,8},{12,14},{14,12},{16,18},{18,... | collective-permute-start | bytes 2654216 | tf_op jit(solution)/shard_map/ppermute | solution.py:290
  43.8 12.3 %collective-permute-start.8 = (bf16[64,6912]{1,0:T(8,128)(2,1)S(1)}, bf16[64,6912]{1,0:T(8,128)(2,1)S(1)}, u32[]{:S(2)}, u32[]{:S(2)}) collective-permute-start(bf16[64,6912]{1,0:T(8,128)(2,1)S(1)} %pad_maximum_fusion.1), channel_id=1, source_target_pairs={{0,2},{2,0},{4,6},{6,4},{8,10},{10,8},{12,14},{14,12},{16,18},{18,... | collective-permute-start | bytes 2654216 | tf_op jit(solution)/shard_map/ppermute | solution.py:290
  44.1 1.3 copy-start.11
  56.2 1.3 copy-start.12
  64.8 39.4 %collective-permute-start.9 = (bf16[8,128,256]{2,1,0:T(8,128)(2,1)}, bf16[8,128,256]{2,1,0:T(8,128)(2,1)S(1)}, u32[]{:S(2)}, u32[]{:S(2)}) collective-permute-start(bf16[8,128,256]{2,1,0:T(8,128)(2,1)} %get-tuple-element.26), channel_id=1, source_target_pairs={{0,1},{1,0},{2,3},{3,2},{4,5},{5,4},{6,7},{7,6},{8,9},{9,8},{10,11... | collective-permute-start | bytes 1572872 | tf_op jit(solution)/shard_map/ppermute | solution.py:290
  83.2 22.0 %collective-permute-start.12 = (bf16[128,3456]{1,0:T(8,128)(2,1)}, bf16[128,3456]{1,0:T(8,128)(2,1)S(1)}, u32[]{:S(2)}, u32[]{:S(2)}) collective-permute-start(bf16[128,3456]{1,0:T(8,128)(2,1)} %get-tuple-element.32), channel_id=1, source_target_pairs={{0,2},{2,0},{4,6},{6,4},{8,10},{10,8},{12,14},{14,12},{16,18},{18,... | collective-permute-start | bytes 2654216 | tf_op jit(solution)/shard_map/ppermute | solution.py:290
  94.9 50.9 %collective-permute-start.11 = (bf16[8,128,256]{2,1,0:T(8,128)(2,1)}, bf16[8,128,256]{2,1,0:T(8,128)(2,1)S(1)}, u32[]{:S(2)}, u32[]{:S(2)}) collective-permute-start(bf16[8,128,256]{2,1,0:T(8,128)(2,1)} %get-tuple-element.29), channel_id=1, source_target_pairs={{0,1},{1,0},{2,3},{3,2},{4,5},{5,4},{6,7},{7,6},{8,9},{9,8},{10,11... | collective-permute-start | bytes 1572872 | tf_op jit(solution)/shard_map/ppermute | solution.py:290
  96.4 7.9 %copy-start.3 = (f32[8,128,256]{2,1,0:T(8,128)S(1)}, f32[8,128,256]{2,1,0:T(8,128)}, u32[]{:S(2)}) copy-start(f32[8,128,256]{2,1,0:T(8,128)} %get-tuple-element.25) | copy-start | bytes 3145732
  104.2 1.4 copy-start.4
  104.2 3.1 %collective-permute-start.17 = (bf16[64,6912]{1,0:T(8,128)(2,1)}, bf16[64,6912]{1,0:T(8,128)(2,1)S(1)}, u32[]{:S(2)}, u32[]{:S(2)}) collective-permute-start(bf16[64,6912]{1,0:T(8,128)(2,1)} %get-tuple-element.35), channel_id=1, source_target_pairs={{0,2},{2,0},{4,6},{6,4},{8,10},{10,8},{12,14},{14,12},{16,18},{18,... | collective-permute-start | bytes 2654216 | tf_op jit(solution)/shard_map/ppermute | solution.py:290
  105.1 2.2 %copy-start.5 = (bf16[64,6912]{1,0:T(8,128)(2,1)S(1)}, bf16[64,6912]{1,0:T(8,128)(2,1)}, u32[]{:S(2)}) copy-start(bf16[64,6912]{1,0:T(8,128)(2,1)} %get-tuple-element.34) | copy-start | bytes 2654212
  105.8 13.1 %collective-permute-start.13 = (bf16[64,3456]{1,0:T(8,128)(2,1)S(1)}, bf16[64,3456]{1,0:T(8,128)(2,1)S(1)}, u32[]{:S(2)}, u32[]{:S(2)}) collective-permute-start(bf16[64,3456]{1,0:T(8,128)(2,1)S(1)} %get-tuple-element.41), channel_id=1, source_target_pairs={{0,4},{2,6},{4,0},{6,2},{8,12},{10,14},{12,8},{14,10},{16,20},{18,... | collective-permute-start | bytes 1327112 | tf_op jit(solution)/shard_map/ppermute | solution.py:290
  107.6 19.9 %collective-permute-start.18 = (bf16[32,6912]{1,0:T(8,128)(2,1)S(1)}, bf16[32,6912]{1,0:T(8,128)(2,1)S(1)}, u32[]{:S(2)}, u32[]{:S(2)}) collective-permute-start(bf16[32,6912]{1,0:T(8,128)(2,1)S(1)} %get-tuple-element.39), channel_id=1, source_target_pairs={{0,4},{2,6},{4,0},{6,2},{8,12},{10,14},{12,8},{14,10},{16,20},{18,... | collective-permute-start | bytes 1327112 | tf_op jit(solution)/shard_map/ppermute | solution.py:290
  119.0 26.9 %copy-start.2 = (f32[8,128,256]{2,1,0:T(8,128)S(1)}, f32[8,128,256]{2,1,0:T(8,128)}, u32[]{:S(2)}) copy-start(f32[8,128,256]{2,1,0:T(8,128)} %get-tuple-element.28) | copy-start | bytes 3145732
  119.0 11.2 %collective-permute-start.14 = (bf16[32,3456]{1,0:T(8,128)(2,1)S(1)}, bf16[32,3456]{1,0:T(8,128)(2,1)S(1)}, u32[]{:S(2)}, u32[]{:S(2)}) collective-permute-start(bf16[32,3456]{1,0:T(8,128)(2,1)S(1)} %get-tuple-element.45), channel_id=1, source_target_pairs={{0,8},{2,10},{4,12},{6,14},{8,0},{10,2},{12,4},{14,6},{16,24},{18,... | collective-permute-start | bytes 663560 | tf_op jit(solution)/shard_map/ppermute | solution.py:290
  127.6 9.8 %collective-permute-start.19 = (bf16[16,6912]{1,0:T(8,128)(2,1)S(1)}, bf16[16,6912]{1,0:T(8,128)(2,1)S(1)}, u32[]{:S(2)}, u32[]{:S(2)}) collective-permute-start(bf16[16,6912]{1,0:T(8,128)(2,1)S(1)} %get-tuple-element.43), channel_id=1, source_target_pairs={{0,8},{2,10},{4,12},{6,14},{8,0},{10,2},{12,4},{14,6},{16,24},{18,... | collective-permute-start | bytes 663560 | tf_op jit(solution)/shard_map/ppermute | solution.py:290
  130.2 10.2 %collective-permute-start.15 = (bf16[16,3456]{1,0:T(8,128)(2,1)S(1)}, bf16[16,3456]{1,0:T(8,128)(2,1)S(1)}, u32[]{:S(2)}, u32[]{:S(2)}) collective-permute-start(bf16[16,3456]{1,0:T(8,128)(2,1)S(1)} %add_convert_fusion.14), channel_id=1, source_target_pairs={{0,16},{2,18},{4,20},{6,22},{8,24},{10,26},{12,28},{14,30},{16,0},... | collective-permute-start | bytes 331784 | tf_op jit(solution)/shard_map/ppermute | solution.py:290
  137.4 6.5 %collective-permute-start.20 = (bf16[8,6912]{1,0:T(8,128)(2,1)S(1)}, bf16[8,6912]{1,0:T(8,128)(2,1)S(1)}, u32[]{:S(2)}, u32[]{:S(2)}) collective-permute-start(bf16[8,6912]{1,0:T(8,128)(2,1)S(1)} %add_convert_fusion.11), channel_id=1, source_target_pairs={{0,16},{2,18},{4,20},{6,22},{8,24},{10,26},{12,28},{14,30},{16,0},... | collective-permute-start | bytes 331784 | tf_op jit(solution)/shard_map/ppermute | solution.py:290
  140.4 8.4 %copy-start.7 = (bf16[16,3456]{1,0:T(8,128)(2,1)}, bf16[16,3456]{1,0:T(8,128)(2,1)S(1)}, u32[]{:S(2)}) copy-start(bf16[16,3456]{1,0:T(8,128)(2,1)S(1)} %add_convert_fusion.13.own1) | copy-start | bytes 331780
  140.4 6.3 %collective-permute-start.16 = (bf16[16,3456]{1,0:T(8,128)(2,1)S(1)}, bf16[16,3456]{1,0:T(8,128)(2,1)S(1)}, u32[]{:S(2)}, u32[]{:S(2)}) collective-permute-start(bf16[16,3456]{1,0:T(8,128)(2,1)S(1)} %add_convert_fusion.13.own1), channel_id=1, source_target_pairs={{0,1},{1,0},{2,3},{3,2},{4,5},{5,4},{6,7},{7,6},{8,9},{9,8},{10,11... | collective-permute-start | bytes 331784 | tf_op jit(solution)/shard_map/ppermute | solution.py:290
  144.0 4.8 %copy-start.8 = (bf16[8,6912]{1,0:T(8,128)(2,1)}, bf16[8,6912]{1,0:T(8,128)(2,1)S(1)}, u32[]{:S(2)}) copy-start(bf16[8,6912]{1,0:T(8,128)(2,1)S(1)} %add_convert_fusion.10.own2) | copy-start | bytes 331780
  144.0 4.8 %collective-permute-start.21 = (bf16[8,6912]{1,0:T(8,128)(2,1)S(1)}, bf16[8,6912]{1,0:T(8,128)(2,1)S(1)}, u32[]{:S(2)}, u32[]{:S(2)}) collective-permute-start(bf16[8,6912]{1,0:T(8,128)(2,1)S(1)} %add_convert_fusion.10.own2), channel_id=1, source_target_pairs={{0,1},{1,0},{2,3},{3,2},{4,5},{5,4},{6,7},{7,6},{8,9},{9,8},{10,11... | collective-permute-start | bytes 331784 | tf_op jit(solution)/shard_map/ppermute | solution.py:290
  146.7 2.1 %copy-start.9 = (bf16[16,3456]{1,0:T(8,128)(2,1)}, bf16[16,3456]{1,0:T(8,128)(2,1)S(1)}, u32[]{:S(2)}) copy-start(bf16[16,3456]{1,0:T(8,128)(2,1)S(1)} %collective-permute-done.16.other1) | copy-start | bytes 331780
  148.8 0.6 copy-start.10
where the time goes:
time: 153 us
  Pallas kernels  69.8 us (46%)
  waiting for transfers between devices  39.3 us (26%)
  starting transfers between devices  30.5 us (20%)
  local copies, waits for them, and re-layouts  7.37 us (5%)
  other arithmetic  5.25 us (3%)
    pallas_call x10, Pallas kernels, run(): pl.pallas_call(kernel, out_shape=tuple(outs), in_specs=[smem] * scalars +...  69.8 us
    ppermute x22, waiting for transfers between devices, trade(): return lax.ppermute(array, axis, [(i, i ^ bit) for i in range(size)])  39.3 us
    ppermute x22, starting transfers between devices, trade(): return lax.ppermute(array, axis, [(i, i ^ bit) for i in range(size)])  30.5 us
    unnamed x36, local copies, waits for them, and re-layouts  7.2 us
  transfers between devices with their start and end apart: 22, of which 10 were waited for; matrix products, arithmetic and copies ran while one was open for 5% of the time, Pallas kernels for 38%

commit v1 on v0

--- a/solution.py
+++ b/solution.py
@@ -11,7 +11,8 @@
 NOISE_COEF = 0.25
 BF = jnp.bfloat16
 F32 = jnp.float32
-VMEM_LIMIT = 56 * 2**20
+SPARE = 8 * 2**20
+NONE, SHORTER, ALL = 1, 10**10, 10**11
 
 
 def dot(a, b):
@@ -20,6 +21,14 @@
 
 def dot_nt(a, b):
     return lax.dot_general(a, b, (((1,), (1,)), ((), ())), preferred_element_type=F32)
+
+
+def over(value, size):
+    return value >> (size.bit_length() - 1)
+
+
+def within(value, size):
+    return value & (size - 1)
 
 
 def reverse_bits(value, bits):
@@ -32,14 +41,14 @@
 def relative_matrix(k, size, rows, bits):
     rel = lax.broadcasted_iota(jnp.int32, (size, size), 0)
     nat = lax.broadcasted_iota(jnp.int32, (size, size), 1)
-    want = (k ^ reverse_bits(rel // rows, bits)) * rows + rel % rows
+    want = (k ^ reverse_bits(over(rel, rows), bits)) * rows + within(rel, rows)
     return jnp.where(want == nat, 1.0, 0.0).astype(BF)
 
 
 def member_matrix(h, channels, half):
     chan = lax.broadcasted_iota(jnp.int32, (channels, channels // 2), 0)
     hid = lax.broadcasted_iota(jnp.int32, (channels, channels // 2), 1)
-    want = (hid // half) * (2 * half) + h * half + hid % half
+    want = over(hid, half) * (2 * half) + h * half + within(hid, half)
     return jnp.where(want == chan, 1.0, 0.0).astype(BF)
 
 
@@ -47,8 +56,9 @@
     out = lax.broadcasted_iota(jnp.int32, (2 * cells, cells), 0)
     src = lax.broadcasted_iota(jnp.int32, (2 * cells, cells), 1)
     step = jnp.where(out < cells, -1, 1)
-    cell = out % cells
-    inside = (cell % width + step >= 0) & (cell % width + step < width)
+    cell = within(out, cells)
+    place = within(cell, width) + step
+    inside = (place >= 0) & (place < width)
     return jnp.where(inside & (src == cell + step), 1.0, 0.0).astype(BF)
 
 
@@ -76,7 +86,15 @@
     return block.reshape(count * area, t3.shape[3])
 
 
-def weights_kernel(half, idx, first, second, w1, w2):
+def base_kernel(weight, noise, base):
+    base[...] = weight[...] + NOISE_COEF * noise[...]
+
+
+def second_rows_kernel(half, idx, second, w2):
+    w2[...] = jnp.where(idx[1] == 0, second[0:half, :], second[half : 2 * half, :]).astype(BF)
+
+
+def first_columns_kernel(half, idx, first, w1):
     h = idx[1]
     channels = 2 * w1.shape[1] // 27
     hid = channels // 2
@@ -87,7 +105,6 @@
             u = bc * 3 + a
             taps = first[:, t * channels : (t + 1) * channels].astype(BF)
             w1[:, u * hid : (u + 1) * hid] = dot(taps, select).astype(BF)
-    w2[...] = jnp.where(h == 0, second[0:half, :], second[half : 2 * half, :]).astype(BF)
 
 
 def spread_kernel(dims, relative, idx, own, other, t3, *rest):
@@ -106,7 +123,6 @@
         value = jnp.where(h == member, mine, theirs)
         if relative:
             rest[0][:, plane * area : (plane + 2) * area] = dot_nt(matrix, value).astype(BF)
-            value = dot_nt(value, matrix).astype(BF)
         store_shifted(t3, plane + 1, value, shifts, width, area)
 
 
@@ -201,53 +217,42 @@
         send[:, u * hid : (u + len(blocks)) * hid] = value[half:]
 
 
-def outputs_kernel(dims, idx, a3, w2, base, keep, send):
-    slab, width, area, rows, bits = dims
-    h = idx[1]
+def outputs_kernel(dims, mine, idx, a3, w2, *refs):
+    slab, width, area, rows, bits = dims
     channels = w2.shape[1] // 27
     taps = [(a, b, c) for a in range(3) for b in range(3) for c in range(3)]
-    for mine in (False, True):
-        start = (h if mine else 1 - h) * slab
-        total = None
-        for t in range(0, 27, 2):
-            left = [window(a3, c, start + a, slab, b, width, area) for a, b, c in taps[t : t + 2]]
-            right = [w2[:, v * channels : (v + 1) * channels] for v in range(t, t + len(left))]
-            part = dot(jnp.concatenate(left, axis=1), jnp.concatenate(right, axis=0))
-            total = part if total is None else total + part
-        total = total.reshape(slab, area, channels)
-        if mine:
-            keep[...] = base[...].astype(F32) + total
-        else:
-            send[...] = total.astype(BF)
-
-
-def input_grads_kernel(dims, idx, g3, w1, base, keep, send):
-    slab, width, area, rows, bits = dims
-    k, h = idx[0], idx[1]
+    start = (idx[1] if mine else 1 - idx[1]) * slab
+    total = None
+    for t in range(0, 27, 2):
+        left = [window(a3, c, start + a, slab, b, width, area) for a, b, c in taps[t : t + 2]]
+        right = [w2[:, v * channels : (v + 1) * channels] for v in range(t, t + len(left))]
+        part = dot(jnp.concatenate(left, axis=1), jnp.concatenate(right, axis=0))
+        total = part if total is None else total + part
+    total = total.reshape(slab, area, channels)
+    if mine:
+        total = refs[0][...].astype(F32) + total
+    refs[-1][...] = total.astype(refs[-1].dtype)
+
+
+def input_grads_kernel(dims, mine, idx, g3, w1, *refs):
+    slab, width, area, rows, bits = dims
     hid = w1.shape[1] // 27
-    channels = w1.shape[0]
-    matrix = relative_matrix(k, channels, rows, bits)
     taps = [(a, b, c) for b in range(3) for c in range(3) for a in range(3)]
-    for mine in (False, True):
-        start = (h if mine else 1 - h) * slab
-        total = None
-        for u in range(0, 27, 2):
-            left = [window(g3, 2 - c, start + 2 - a, slab, 2 - b, width, area) for a, b, c in taps[u : u + 2]]
-            part = dot_nt(jnp.concatenate(left, axis=1), w1[:, u * hid : (u + len(left)) * hid])
-            total = part if total is None else total + part
-        high = total.astype(BF)
-        natural = dot(high, matrix)
-        if mine:
-            low = (total - high.astype(F32)).astype(BF)
-            natural = natural + dot(low, matrix)
-            keep[...] = base[...].astype(F32) + natural.reshape(slab, area, channels)
-        else:
-            send[...] = natural.astype(BF).reshape(slab, area, channels)
-
-
-def update_kernel(half, rate, idx, own1, other1, own2, other2, first, second, noise1, noise2, new1, new2):
+    start = (idx[1] if mine else 1 - idx[1]) * slab
+    total = None
+    for u in range(0, 27, 2):
+        left = [window(g3, 2 - c, start + 2 - a, slab, 2 - b, width, area) for a, b, c in taps[u : u + 2]]
+        part = dot_nt(jnp.concatenate(left, axis=1), w1[:, u * hid : (u + len(left)) * hid])
+        total = part if total is None else total + part
+    total = total.reshape(slab, area, w1.shape[0])
+    if mine:
+        total = refs[0][...].astype(F32) + total
+    refs[-1][...] = total.astype(refs[-1].dtype)
+
+
+def update_first_kernel(half, rate, idx, own, other, base, new):
     h = idx[1]
-    hid = own1.shape[1] // 27
+    hid = own.shape[1] // 27
     channels = 2 * hid
     mine = member_matrix(h, channels, half)
     theirs = member_matrix(1 - h, channels, half)
@@ -257,32 +262,45 @@
             u = bc * 3 + a
             cols = slice(t * channels, (t + 1) * channels)
             part = slice(u * hid, (u + 1) * hid)
-            grad = dot_nt(own1[:, part], mine) + dot_nt(other1[:, part], theirs)
-            new1[:, cols] = first[:, cols] - rate * grad + NOISE_COEF * noise1[:, cols]
-    mine2 = own2[...].astype(F32)
-    theirs2 = other2[...].astype(F32)
-    low = jnp.where(h == 0, mine2, theirs2)
-    high = jnp.where(h == 0, theirs2, mine2)
-    new2[0:half, :] = second[0:half, :] - rate * low + NOISE_COEF * noise2[0:half, :]
-    new2[half : 2 * half, :] = (
-        second[half : 2 * half, :] - rate * high + NOISE_COEF * noise2[half : 2 * half, :]
-    )
-
-
-def run(kernel, args, outs, name, flops, scalars=1, scratch=()):
+            grad = dot_nt(own[:, part], mine) + dot_nt(other[:, part], theirs)
+            new[:, cols] = base[:, cols] - rate * grad
+
+
+def update_second_kernel(half, rate, idx, own, other, base, new):
+    h = idx[1]
+    mine = own[...].astype(F32)
+    theirs = other[...].astype(F32)
+    for member in range(2):
+        grad = jnp.where(h == member, mine, theirs)
+        rows = slice(member * half, (member + 1) * half)
+        new[rows, :] = base[rows, :] - rate * grad
+
+
+def finish_kernel(own, came, out):
+    out[...] = (own[...] + came[...].astype(F32)).astype(BF)
+
+
+def run(kernel, args, outs, name, cost, scalars=1, scratch=(), after=()):
     moved = sum(math.prod(a.shape) * a.dtype.itemsize for a in (*args, *outs))
+    room = moved + sum(math.prod(a.shape) * a.dtype.itemsize for a in scratch)
     smem = pl.BlockSpec(memory_space=pltpu.SMEM)
     vmem = pl.BlockSpec(memory_space=pltpu.VMEM)
+    anywhere = pl.BlockSpec(memory_space=pl.ANY)
+    count = len(args)
+
+    def entry(*refs):
+        kernel(*refs[:count], *refs[count + len(after) :])
+
     return pl.pallas_call(
-        kernel,
+        entry,
         out_shape=tuple(outs),
-        in_specs=[smem] * scalars + [vmem] * (len(args) - scalars),
+        in_specs=[smem] * scalars + [vmem] * (count - scalars) + [anywhere] * len(after),
         out_specs=tuple([vmem] * len(outs)),
         scratch_shapes=list(scratch),
-        compiler_params=pltpu.CompilerParams(vmem_limit_bytes=VMEM_LIMIT),
-        cost_estimate=pl.CostEstimate(flops=flops, bytes_accessed=moved, transcendentals=0),
+        compiler_params=pltpu.CompilerParams(vmem_limit_bytes=room + SPARE),
+        cost_estimate=pl.CostEstimate(flops=cost, bytes_accessed=1, transcendentals=0),
         name=name,
-    )(*args)
+    )(*args, *after)
 
 
 def trade(array, axis, bit):
@@ -290,30 +308,56 @@
     return lax.ppermute(array, axis, [(i, i ^ bit) for i in range(size)])
 
 
-def gather(array, bits):
-    for b in range(bits - 1, -1, -1):
-        array = jnp.concatenate([array, trade(array, "dp", 1 << b)], axis=0)
-    return array
+def join_kernel(*refs):
+    row = 0
+    for ref in refs[:-1]:
+        refs[-1][row : row + ref.shape[0], :] = ref[...]
+        row += ref.shape[0]
+
+
+def join(parts, name, after=(), cost=NONE):
+    total = jax.ShapeDtypeStruct((sum(p.shape[0] for p in parts), parts[0].shape[1]), BF)
+    return run(join_kernel, tuple(parts), (total,), name, cost, scalars=0, after=after)[0]
+
+
+def place_kernel(rows, bits, idx, *refs):
+    q = 0
+    for ref in refs[:-1]:
+        for row in range(0, ref.shape[0], rows):
+            owner = idx[0] ^ int(f"{q:0{bits}b}"[::-1], 2)
+            refs[-1][pl.ds(pl.multiple_of(owner * rows, rows), rows), :] = ref[row : row + rows, :]
+            q += 1
+
+
+def fold_kernel(count, *refs):
+    total = refs[0][...].astype(F32)
+    for ref in refs[1:count]:
+        total = total + ref[...].astype(F32)
+    total = total.astype(BF)
+    row = 0
+    for out in refs[count:]:
+        out[...] = total[row : row + out.shape[0]]
+        row += out.shape[0]
+
+
+def fold(parts, name, split=1, after=(), cost=NONE):
+    rows, columns = parts[0].shape
+    out = jax.ShapeDtypeStruct((rows // split, columns), BF)
+    kernel = functools.partial(fold_kernel, len(parts))
+    return run(kernel, tuple(parts), (out,) * split, name, cost, scalars=0, after=after)
 
 
 def add(a, b):
     return (a.astype(F32) + b.astype(F32)).astype(BF)
 
 
-def scatter(keep, send, bits):
-    for b in range(bits):
-        came = trade(send, "dp", 1 << b)
-        if b == bits - 1:
-            keep = add(keep, came)
-        else:
-            half = keep.shape[0] // 2
-            keep, send = add(keep[:half], came[:half]), add(keep[half:], came[half:])
+def over_pairs(share):
     pairs = lax.axis_size("space") // 2
     step = 1
     while step < pairs:
-        keep = add(keep, trade(keep, "space", 2 * step))
+        share = add(share, trade(share, "space", 2 * step))
         step *= 2
-    return keep
+    return share
 
 
 def with_halo(t3):
@@ -339,7 +383,6 @@
     halo = members > 2
     planes = 2 * slab
     cells = planes * area
-    heavy = 2 * cells * 27 * channels * hid
     idx = jnp.stack([lax.axis_index("dp"), lax.axis_index("space") % 2]).astype(jnp.int32)
     volume = volumes.reshape(slab, area, channels)
     upstream = cotangent.reshape(slab, area, channels)
@@ -348,92 +391,163 @@
     def padded(count):
         return shape((3, planes + 2, area + 2 * width, count), BF)
 
-    w1, w2 = run(
-        functools.partial(weights_kernel, half),
-        (idx, first_weight, second_weight),
-        (shape((rows, 27 * hid), BF), shape((half, 27 * channels), BF)),
-        "weights",
-        2 * rows * 27 * channels * hid,
-    )
-    w1 = gather(w1, bits)
+    core, near, line, far = 1, 2, 4, 8
+
     other_volume = trade(volume, "space", 1)
+    (w1,) = run(
+        functools.partial(first_columns_kernel, half),
+        (idx, first_weight),
+        (shape((rows, 27 * hid), BF),),
+        "first_columns",
+        NONE,
+    )
+    w1 = join((w1, trade(w1, "dp", far)), "join1")
+    (w2,) = run(
+        functools.partial(second_rows_kernel, half),
+        (idx, second_weight),
+        (shape((half, 27 * channels), BF),),
+        "second_rows",
+        SHORTER,
+        after=(w1,),
+    )
+    line1, near1 = trade(w1, "dp", line), trade(w1, "dp", near)
+    w1 = join((w1, line1, near1), "join1", after=(w2,))
+    both1 = trade(line1, "dp", near)
+    far2 = trade(w2, "dp", far)
     x3, xt = run(
         functools.partial(spread_kernel, dims, True),
         (idx, volume, other_volume),
         (padded(channels), shape((channels, cells), BF)),
         "spread_volumes",
-        8 * cells * channels * channels,
+        ALL,
+        after=(w1,),
     )
     x3 = with_halo(x3)
+    sum_of = shape(first_weight.shape, F32)
+    (base1,) = run(base_kernel, (first_weight, first_noise), (sum_of,), "base1", NONE, scalars=0, after=(xt,))
+    w1 = join((w1, both1), "join1", after=(base1,))
+    core1 = trade(w1, "dp", core)
+    w2 = join((w2, far2), "join2", after=(w1,), cost=ALL)
+    line2, near2 = trade(w2, "dp", line), trade(w2, "dp", near)
+    (w1,) = run(
+        functools.partial(place_kernel, rows, bits),
+        (idx, w1, core1),
+        (shape((channels, 27 * hid), BF),),
+        "place1",
+        NONE,
+        after=(w2,),
+    )
+    scratch = [pltpu.VMEM((planes + 2, area, 3 * hid), F32)]
+    a3, at, slope = run(
+        functools.partial(hidden_kernel, dims, halo),
+        (idx, x3, w1),
+        (padded(hid), shape((hid, cells), BF), shape((planes, area, hid), BF)),
+        "hidden",
+        SHORTER,
+        scratch=scratch,
+    )
+    a3 = with_halo(a3)
+
+    w2 = join((w2, line2, near2), "join2", after=(slope,))
+    line2 = join((line2,), "join2", after=(slope,))
+    both2 = trade(line2, "dp", near)
     other_upstream = trade(upstream, "space", 1)
     (c3,) = run(
         functools.partial(spread_kernel, dims, False),
         (idx, upstream, other_upstream),
         (padded(channels),),
         "spread_cotangent",
-        4 * cells * channels * channels,
+        ALL,
+        after=(w2,),
     )
     c3 = with_halo(c3)
-    w2 = gather(w2, bits)
-    scratch = [pltpu.VMEM((planes + 2, area, 3 * hid), F32)]
-    a3, at, slope = run(
-        functools.partial(hidden_kernel, dims, halo),
-        (idx, x3, w1),
-        (padded(hid), shape((hid, cells), BF), shape((planes, area, hid), BF)),
-        "hidden",
-        heavy,
-        scratch=scratch,
-    )
-    a3 = with_halo(a3)
     keep2, send2 = run(
         functools.partial(second_grad_kernel, dims),
         (at, c3),
         (shape((hid // 2, 27 * channels), BF),) * 2,
         "second_grad",
-        heavy,
+        NONE,
         scalars=0,
     )
-    share2 = scatter(keep2, send2, bits)
+    w2 = join((w2, both2), "join2", after=(keep2,), cost=ALL)
+    core2 = trade(w2, "dp", core)
+    q01, q23, q45, q67 = fold((keep2, trade(send2, "dp", core)), "fold2", split=4, after=(w2,), cost=ALL)
+    w2 = join((w2, core2), "join2", after=(q01,))
     (g3,) = run(
         functools.partial(hidden_grad_kernel, dims, halo),
         (idx, c3, w2, slope),
         (padded(hid),),
         "hidden_grad",
-        heavy,
+        ALL,
         scratch=scratch,
     )
     g3 = with_halo(g3)
+
+    (q23,) = fold((q23, trade(q67, "dp", near)), "fold2", after=(g3,))
+    line2, near2 = trade(q23, "dp", line), trade(join((q45,), "join2", after=(g3,)), "dp", near)
     keep1, send1 = run(
         functools.partial(first_grad_kernel, dims),
         (xt, g3),
         (shape((channels // 2, 27 * hid), BF),) * 2,
         "first_grad",
-        heavy,
+        ALL,
         scalars=0,
-    )
-    share1 = scatter(keep1, send1, bits)
-    parts = (shape((slab, area, channels), F32), shape((slab, area, channels), BF))
-    own_out, send_out = run(
-        functools.partial(outputs_kernel, dims), (idx, a3, w2, volume), parts, "outputs", heavy
+        after=(q23,),
+    )
+    q0, q1 = fold((q01, line2, near2), "fold2", split=2, after=(keep1,), cost=ALL)
+    p01, p23, p45, p67 = fold((keep1, trade(send1, "dp", core)), "fold1", split=4, after=(q0,))
+    near1 = trade(p67, "dp", near)
+    part, whole = shape((slab, area, channels), BF), shape((slab, area, channels), F32)
+    (send_out,) = run(
+        functools.partial(outputs_kernel, dims, False), (idx, a3, w2), (part,), "outputs_send", ALL, after=(p01,)
     )
     came_out = trade(send_out, "space", 1)
-    own_in, send_in = run(
-        functools.partial(input_grads_kernel, dims), (idx, g3, w1, upstream), parts, "input_grads", heavy
+    (p23,) = fold((p23, near1), "fold1", after=(send_out,))
+    line1, near1 = trade(p23, "dp", line), trade(join((p45,), "join1", after=(send_out,)), "dp", near)
+    far2 = trade(join((q1,), "join2", after=(p23,)), "dp", far)
+    (send_in,) = run(
+        functools.partial(input_grads_kernel, dims, False), (idx, g3, w1), (part,), "input_grads_send", ALL, after=(p23,)
     )
     came_in = trade(send_in, "space", 1)
-    outputs = (own_out + came_out.astype(F32)).astype(BF).reshape(volumes.shape)
-    input_grads = (own_in + came_in.astype(F32)).astype(BF).reshape(volumes.shape)
+    p0, p1 = fold((p01, line1, near1), "fold1", split=2, after=(send_in,))
+    (own_out,) = run(
+        functools.partial(outputs_kernel, dims, True), (idx, a3, w2, volume), (whole,), "outputs", SHORTER, after=(p0,)
+    )
+    (share2,) = fold((q0, far2), "fold2", after=(own_out,))
+    share2 = over_pairs(share2)
     other2 = trade(share2, "space", 1)
+    (own_in,) = run(
+        functools.partial(input_grads_kernel, dims, True),
+        (idx, g3, w1, upstream),
+        (whole,),
+        "input_grads",
+        NONE,
+        after=(share2,),
+    )
+    (share1,) = fold((p0, trade(p1, "dp", far)), "fold1", after=(own_in,))
+    share1 = over_pairs(share1)
     other1 = trade(share1, "space", 1)
+    (base2,) = run(base_kernel, (second_weight, second_noise), (sum_of,), "base2", NONE, scalars=0, after=(own_out,))
+    (outputs,) = run(finish_kernel, (own_out, came_out), (part,), "finish", NONE, scalars=0, after=(share1, base2))
     rate = 1.0 / math.sqrt(slab * area * devices * members)
-    new_first, new_second = run(
-        functools.partial(update_kernel, half, rate),
-        (idx, share1, other1, share2, other2, first_weight, second_weight, first_noise, second_noise),
-        (shape(first_weight.shape, F32),) * 2,
-        "update",
-        4 * rows * 27 * channels * hid,
-    )
-    return (outputs, input_grads, new_first, new_second)
+    (new_second,) = run(
+        functools.partial(update_second_kernel, half, rate),
+        (idx, share2, other2, base2),
+        (sum_of,),
+        "update_second",
+        NONE,
+        after=(outputs,),
+    )
+    (new_first,) = run(
+        functools.partial(update_first_kernel, half, rate),
+        (idx, share1, other1, base1),
+        (sum_of,),
+        "update_first",
+        NONE,
+        after=(new_second,),
+    )
+    (input_grads,) = run(finish_kernel, (own_in, came_in), (part,), "finish", NONE, scalars=0, after=(new_first,))
+    return (outputs.reshape(volumes.shape), input_grads.reshape(volumes.shape), new_first, new_second)
 
 
 def solution(mesh):

time: 153 us -> 106 us (0.69)
  Pallas kernels: 69.8 us -> 45.6 us
  waiting for transfers between devices: 39.3 us -> 15.7 us
  starting transfers between devices: 30.5 us -> 37.3 us
  other arithmetic: 5.25 us -> 0.08 us
    pallas_call x10 -> x38, Pallas kernels: 69.8 us -> 45.6 us  [run(): pl.pallas_call(entry, out_shape=tuple(outs), in_specs=[smem] * scalars +...]
    ppermute x22 -> x26, waiting for transfers between devices: 39.3 us -> 15.7 us  [trade(): return lax.ppermute(array, axis, [(i, i ^ bit) for i in range(size)])]
    ppermute x22 -> x26, starting transfers between devices: 30.5 us -> 37.3 us  [trade(): return lax.ppermute(array, axis, [(i, i ^ bit) for i in range(size)])]
    convert_element_type x10 -> x0, other arithmetic: 2.62 us -> none  [the longest x1 0.92 us: body(): outputs = (own_out + came_out.astype(F32)).astype(BF).reshape(volumes.shape)]
    concatenate x6 -> x0, other arithmetic: 2.04 us -> none  [gather(): array = jnp.concatenate([array, trade(array, 'dp', 1 << b)], axis=0)]
    unnamed x36 -> x50, local copies, waits for them, and re-layouts: 7.2 us -> 6.05 us
  transfers between devices with their start and end apart: 22 -> 26, of which waited for: 10 -> 11; matrix products, arithmetic and copies ran while one was open for 5% -> 0% of each run, Pallas kernels for 38% -> 41%
where the time goes in v1:
time: 106 us
  Pallas kernels  45.6 us (43%)
  starting transfers between devices  37.3 us (35%)
  waiting for transfers between devices  15.7 us (15%)
  local copies, waits for them, and re-layouts  6.05 us (6%)
  between operations  1.15 us (1%)
    pallas_call x38, Pallas kernels, run(): pl.pallas_call(entry, out_shape=tuple(outs), in_specs=[smem] * scalars +...  45.6 us
    ppermute x26, starting transfers between devices, trade(): return lax.ppermute(array, axis, [(i, i ^ bit) for i in range(size)])  37.3 us
    ppermute x26, waiting for transfers between devices, trade(): return lax.ppermute(array, axis, [(i, i ^ bit) for i in range(size)])  15.7 us
    unnamed x50, local copies, waits for them, and re-layouts  6.05 us
  transfers between devices with their start and end apart: 26, of which 11 were waited for; matrix products, arithmetic and copies ran while one was open for 0% of the time, Pallas kernels for 41%

profile of v1, /device:TPU:0, one launch (start us, length us, event | category | flops | bytes accessed | tf_op | source)
XLA Modules:
  0.0 105.8 jit_solution(17046287244424004895)
XLA Ops:
  0.6 0.1 pad_add_fusion.refs_0_
  0.7 1.0 copy-done.7
  1.7 0.9 first_columns.1.refs_0_
  2.6 4.1 %collective-permute-start.1 = (bf16[16,3456]{1,0:T(8,128)(2,1)S(1)}, bf16[16,3456]{1,0:T(8,128)(2,1)S(1)}, u32[]{:S(2)}, u32[]{:S(2)}) collective-permute-start(bf16[16,3456]{1,0:T(8,128)(2,1)S(1)} %first_columns.1.refs_0_), channel_id=1, source_target_pairs={{0,16},{2,18},{4,20},{6,22},{8,24},{10,26},{12,28},{14,30},{16,0},... | collective-permute-start | bytes 331784 | tf_op jit(solution)/shard_map/ppermute | solution.py:308
  6.7 1.5 %collective-permute-start = (bf16[8,128,256]{2,1,0:T(8,128)(2,1)}, bf16[8,128,256]{2,1,0:T(8,128)(2,1)S(1)}, u32[]{:S(2)}, u32[]{:S(2)}) collective-permute-start(bf16[8,128,256]{2,1,0:T(8,128)(2,1)} %bitcast.10), channel_id=1, source_target_pairs={{0,1},{1,0},{2,3},{3,2},{4,5},{5,4},{6,7},{7,6},{8,9},{9,8},{10,11... | collective-permute-start | bytes 1572872 | tf_op jit(solution)/shard_map/ppermute | solution.py:308
  8.2 0.5 collective-permute-start.10
  8.7 3.4 %collective-permute-done.1.refs_1_ = bf16[16,3456]{1,0:T(8,128)(2,1)S(1)} collective-permute-done((bf16[16,3456]{1,0:T(8,128)(2,1)S(1)}, bf16[16,3456]{1,0:T(8,128)(2,1)S(1)}, u32[]{:S(2)}, u32[]{:S(2)}) %collective-permute-start.1) | collective-permute-done | bytes 110624 | tf_op jit(solution)/shard_map/ppermute | solution.py:308
  12.2 1.6 %collective-permute-start.3 = (bf16[32,3456]{1,0:T(8,128)(2,1)S(1)}, bf16[32,3456]{1,0:T(8,128)(2,1)S(1)}, u32[]{:S(2)}, u32[]{:S(2)}) collective-permute-start(bf16[32,3456]{1,0:T(8,128)(2,1)S(1)} %join1.4.refs_2_.refs_0_), channel_id=1, source_target_pairs={{0,4},{2,6},{4,0},{6,2},{8,12},{10,14},{12,8},{14,10},{16,20},{18,... | collective-permute-start | bytes 663560 | tf_op jit(solution)/shard_map/ppermute | solution.py:308
  13.8 0.7 collective-permute-start.2
  14.5 1.0 copy-done.16
  15.5 0.6 second_rows.1.refs_3_.refs_0_
  16.1 3.4 %collective-permute-start.6 = (bf16[8,6912]{1,0:T(8,128)(2,1)S(1)}, bf16[8,6912]{1,0:T(8,128)(2,1)S(1)}, u32[]{:S(2)}, u32[]{:S(2)}) collective-permute-start(bf16[8,6912]{1,0:T(8,128)(2,1)S(1)} %second_rows.1.refs_3_.refs_0_), channel_id=1, source_target_pairs={{0,16},{2,18},{4,20},{6,22},{8,24},{10,26},{12,28},{14,30},{16,0},... | collective-permute-start | bytes 331784 | tf_op jit(solution)/shard_map/ppermute | solution.py:308
  19.5 0.3 collective-permute-done.2.refs_1_
  19.8 2.8 %collective-permute-start.4 = (bf16[32,3456]{1,0:T(8,128)(2,1)S(1)}, bf16[32,3456]{1,0:T(8,128)(2,1)S(1)}, u32[]{:S(2)}, u32[]{:S(2)}) collective-permute-start(bf16[32,3456]{1,0:T(8,128)(2,1)S(1)} %collective-permute-done.2.refs_1_), channel_id=1, source_target_pairs={{0,4},{2,6},{4,0},{6,2},{8,12},{10,14},{12,8},{14,10},{16,20},{18,... | collective-permute-start | bytes 663560 | tf_op jit(solution)/shard_map/ppermute | solution.py:308
  22.7 1.7 %spread_volumes.1 = (bf16[3,18,160,256]{3,2,1,0:T(8,128)(2,1)S(1)}, bf16[256,2048]{1,0:T(8,128)(2,1)S(1)}) custom-call(s32[2]{0:T(128)S(1)} %pad_add_fusion.refs_0_, bf16[8,128,256]{2,1,0:T(8,128)(2,1)S(1)} %bitcast.11, bf16[8,128,256]{2,1,0:T(8,128)(2,1)S(1)} %collective-permute-done.refs_2_, bf16[96,3456]{1,0:T(8,128)(2,1)S(1)} %join1.5.refs_3_.refs_0_), custom_call_target="tpu_custom_call" | custom-call | flops 99999997952 | bytes 1 | tf_op jit(solution)/shard_map/spread_volumes/pallas_call | solution.py:294
  24.5 2.0 %collective-permute-done.4.refs_1_ = bf16[32,3456]{1,0:T(8,128)(2,1)S(1)} collective-permute-done((bf16[32,3456]{1,0:T(8,128)(2,1)S(1)}, bf16[32,3456]{1,0:T(8,128)(2,1)S(1)}, u32[]{:S(2)}, u32[]{:S(2)}) %collective-permute-start.4) | collective-permute-done | bytes 221216 | tf_op jit(solution)/shard_map/ppermute | solution.py:308
  26.6 0.1 collective-permute-start.5
  26.7 2.1 %collective-permute-start.8 = (bf16[16,6912]{1,0:T(8,128)(2,1)S(1)}, bf16[16,6912]{1,0:T(8,128)(2,1)S(1)}, u32[]{:S(2)}, u32[]{:S(2)}) collective-permute-start(bf16[16,6912]{1,0:T(8,128)(2,1)S(1)} %join2.7.refs_3_.refs_0_), channel_id=1, source_target_pairs={{0,4},{2,6},{4,0},{6,2},{8,12},{10,14},{12,8},{14,10},{16,20},{18,... | collective-permute-start | bytes 663560 | tf_op jit(solution)/shard_map/ppermute | solution.py:308
  28.8 0.3 collective-permute-done.5.refs_2_
  29.1 0.7 place1.1.refs_2_
  29.8 7.1 %hidden.1 = (bf16[3,18,160,128]{3,2,1,0:T(8,128)(2,1)S(1)}, bf16[128,2048]{1,0:T(8,128)(2,1)S(1)}, bf16[16,128,128]{2,1,0:T(8,128)(2,1)S(1)}) custom-call(s32[2]{0:T(128)S(1)} %pad_add_fusion.refs_0_, bf16[3,18,160,256]{3,2,1,0:T(8,128)(2,1)S(1)} %get-tuple-element.25.refs_1_, bf16[256,3456]{1,0:T(8,128)(2,1)S(1)} %place1.1.refs_2_), custom_call_target="tpu_custom_call" | custom-call | flops 10000000000 | bytes 1 | tf_op jit(solution)/shard_map/hidden/pallas_call | solution.py:294
  36.9 2.1 %collective-permute-start.9 = (bf16[16,6912]{1,0:T(8,128)(2,1)S(1)}, bf16[16,6912]{1,0:T(8,128)(2,1)S(1)}, u32[]{:S(2)}, u32[]{:S(2)}) collective-permute-start(bf16[16,6912]{1,0:T(8,128)(2,1)S(1)} %join2.9), channel_id=1, source_target_pairs={{0,4},{2,6},{4,0},{6,2},{8,12},{10,14},{12,8},{14,10},{16,20},{18,... | collective-permute-start | bytes 663560 | tf_op jit(solution)/shard_map/ppermute | solution.py:308
  39.1 1.9 %spread_cotangent.1.refs_1_ = bf16[3,18,160,256]{3,2,1,0:T(8,128)(2,1)S(1)} custom-call(s32[2]{0:T(128)S(1)} %pad_add_fusion.refs_0_, bf16[8,128,256]{2,1,0:T(8,128)(2,1)S(1)} %bitcast.8, bf16[8,128,256]{2,1,0:T(8,128)(2,1)} %collective-permute-done.10.refs_2_, bf16[48,6912]{1,0:T(8,128)(2,1)S(1)} %join2.8.refs_3_.refs_0_), custom_call_target="tpu_custom_call" | custom-call | flops 99999997952 | bytes 1 | tf_op jit(solution)/shard_map/spread_cotangent/pallas_call | solution.py:294
  41.0 4.4 %second_grad.1 = (bf16[64,6912]{1,0:T(8,128)(2,1)S(1)}, bf16[64,6912]{1,0:T(8,128)(2,1)S(1)}) custom-call(bf16[128,2048]{1,0:T(8,128)(2,1)S(1)} %get-tuple-element.29.refs_0_, bf16[3,18,160,256]{3,2,1,0:T(8,128)(2,1)S(1)} %spread_cotangent.1.refs_1_), custom_call_target="tpu_custom_call" | custom-call | flops 1 | bytes 1 | tf_op jit(solution)/shard_map/second_grad/pallas_call | solution.py:294
  45.6 0.5 collective-permute-start.11
  46.1 1.8 %collective-permute-done.12.refs_1_ = bf16[64,6912]{1,0:T(8,128)(2,1)S(1)} collective-permute-done((bf16[64,6912]{1,0:T(8,128)(2,1)S(1)}, bf16[64,6912]{1,0:T(8,128)(2,1)S(1)}, u32[]{:S(2)}, u32[]{:S(2)}) %collective-permute-start.12) | collective-permute-done | bytes 884768 | tf_op jit(solution)/shard_map/ppermute | solution.py:308
  47.9 0.2 fold2.4
  48.1 0.9 collective-permute-start.13
  49.0 0.1 collective-permute-done.11.refs_1_
  49.2 0.1 join2.11.refs_2_
  49.3 0.7 copy-done.21
  50.0 0.2 copy-done.3
  50.2 6.9 %hidden_grad.1.refs_2_.refs_1_ = bf16[3,18,160,128]{3,2,1,0:T(8,128)(2,1)S(1)} custom-call(s32[2]{0:T(128)S(1)} %pad_add_fusion.refs_0_, bf16[3,18,160,256]{3,2,1,0:T(8,128)(2,1)S(1)} %copy-done.3, bf16[128,6912]{1,0:T(8,128)(2,1)S(1)} %join2.11.refs_2_, bf16[16,128,128]{2,1,0:T(8,128)(2,1)S(1)} %get-tuple-element.28.refs_3_.refs_1_), custom_call_target="tpu_custom_call" | custom-call | flops 99999997952 | bytes 1 | tf_op jit(solution)/shard_map/hidden_grad/pallas_call | solution.py:294
  57.1 0.9 collective-permute-start.16
  58.1 1.0 collective-permute-start.15
  59.1 4.0 %first_grad.1 = (bf16[128,3456]{1,0:T(8,128)(2,1)S(1)}, bf16[128,3456]{1,0:T(8,128)(2,1)S(1)}) custom-call(bf16[256,2048]{1,0:T(8,128)(2,1)S(1)} %copy-done.12, bf16[3,18,160,128]{3,2,1,0:T(8,128)(2,1)S(1)} %hidden_grad.1.refs_2_.refs_1_, bf16[16,6912]{1,0:T(8,128)(2,1)S(1)} %fold2.5.refs_2_), custom_call_target="tpu_custom_call" | custom-call | flops 99999997952 | bytes 1 | tf_op jit(solution)/shard_map/first_grad/pallas_call | solution.py:294
  63.2 1.5 %collective-permute-done.16.refs_2_ = bf16[16,6912]{1,0:T(8,128)(2,1)S(1)} collective-permute-done((bf16[16,6912]{1,0:T(8,128)(2,1)S(1)}, bf16[16,6912]{1,0:T(8,128)(2,1)S(1)}, u32[]{:S(2)}, u32[]{:S(2)}) %collective-permute-start.16) | collective-permute-done | bytes 221216 | tf_op jit(solution)/shard_map/ppermute | solution.py:308
  64.7 0.7 collective-permute-done.15.refs_1_
  65.4 0.1 fold2.6
  65.5 0.1 collective-permute-done.14.refs_1_
  65.6 0.2 fold1.4
  65.8 1.1 %collective-permute-start.17 = (bf16[32,3456]{1,0:T(8,128)(2,1)S(1)}, bf16[32,3456]{1,0:T(8,128)(2,1)S(1)}, u32[]{:S(2)}, u32[]{:S(2)}) collective-permute-start(bf16[32,3456]{1,0:T(8,128)(2,1)S(1)} %get-tuple-element.41), channel_id=1, source_target_pairs={{0,4},{2,6},{4,0},{6,2},{8,12},{10,14},{12,8},{14,10},{16,20},{18,... | collective-permute-start | bytes 663560 | tf_op jit(solution)/shard_map/ppermute | solution.py:308
  67.0 2.8 %outputs_send.1.refs_2_.refs_1_ = bf16[8,128,256]{2,1,0:T(8,128)(2,1)S(1)} custom-call(s32[2]{0:T(128)S(1)} %pad_add_fusion.refs_0_, bf16[3,18,160,128]{3,2,1,0:T(8,128)(2,1)S(1)} %get-tuple-element.27.refs_1_, bf16[128,6912]{1,0:T(8,128)(2,1)S(1)} %join2.11.refs_2_, bf16[32,3456]{1,0:T(8,128)(2,1)S(1)} %get-tuple-element.39.refs_3_.refs_0_), custom_call_target="tpu_custom_call" | custom-call | flops 99999997952 | bytes 1 | tf_op jit(solution)/shard_map/outputs_send/pallas_call | solution.py:294
  69.8 0.8 collective-permute-start.20
  70.6 1.2 %collective-permute-start.19 = (bf16[32,3456]{1,0:T(8,128)(2,1)S(1)}, bf16[32,3456]{1,0:T(8,128)(2,1)S(1)}, u32[]{:S(2)}, u32[]{:S(2)}) collective-permute-start(bf16[32,3456]{1,0:T(8,128)(2,1)S(1)} %join1.7), channel_id=1, source_target_pairs={{0,4},{2,6},{4,0},{6,2},{8,12},{10,14},{12,8},{14,10},{16,20},{18,... | collective-permute-start | bytes 663560 | tf_op jit(solution)/shard_map/ppermute | solution.py:308
  71.8 2.0 %collective-permute-done.17.refs_1_ = bf16[32,3456]{1,0:T(8,128)(2,1)S(1)} collective-permute-done((bf16[32,3456]{1,0:T(8,128)(2,1)S(1)}, bf16[32,3456]{1,0:T(8,128)(2,1)S(1)}, u32[]{:S(2)}, u32[]{:S(2)}) %collective-permute-start.17) | collective-permute-done | bytes 221216 | tf_op jit(solution)/shard_map/ppermute | solution.py:308
  73.9 1.5 %collective-permute-start.18 = (bf16[32,3456]{1,0:T(8,128)(2,1)S(1)}, bf16[32,3456]{1,0:T(8,128)(2,1)S(1)}, u32[]{:S(2)}, u32[]{:S(2)}) collective-permute-start(bf16[32,3456]{1,0:T(8,128)(2,1)S(1)} %fold1.5.refs_3_.refs_1_), channel_id=1, source_target_pairs={{0,8},{2,10},{4,12},{6,14},{8,0},{10,2},{12,4},{14,6},{16,24},{18,... | collective-permute-start | bytes 663560 | tf_op jit(solution)/shard_map/ppermute | solution.py:308
  75.3 2.6 %input_grads_send.1.refs_3_ = bf16[8,128,256]{2,1,0:T(8,128)(2,1)S(1)} custom-call(s32[2]{0:T(128)S(1)} %pad_add_fusion.refs_0_, bf16[3,18,160,128]{3,2,1,0:T(8,128)(2,1)S(1)} %hidden_grad.1.refs_2_.refs_1_, bf16[256,3456]{1,0:T(8,128)(2,1)S(1)} %copy-done.1, bf16[32,3456]{1,0:T(8,128)(2,1)S(1)} %fold1.5.refs_3_.refs_1_), custom_call_target="tpu_custom_call" | custom-call | flops 99999997952 | bytes 1 | tf_op jit(solution)/shard_map/input_grads_send/pallas_call | solution.py:294
  78.0 3.0 %collective-permute-start.22 = (bf16[8,6912]{1,0:T(8,128)(2,1)S(1)}, bf16[8,6912]{1,0:T(8,128)(2,1)S(1)}, u32[]{:S(2)}, u32[]{:S(2)}) collective-permute-start(bf16[8,6912]{1,0:T(8,128)(2,1)S(1)} %join2.13), channel_id=1, source_target_pairs={{0,16},{2,18},{4,20},{6,22},{8,24},{10,26},{12,28},{14,30},{16,0},... | collective-permute-start | bytes 331784 | tf_op jit(solution)/shard_map/ppermute | solution.py:308
  80.9 2.1 %collective-permute-start.23 = (bf16[8,128,256]{2,1,0:T(8,128)(2,1)S(1)}, bf16[8,128,256]{2,1,0:T(8,128)(2,1)S(1)}, u32[]{:S(2)}, u32[]{:S(2)}) collective-permute-start(bf16[8,128,256]{2,1,0:T(8,128)(2,1)S(1)} %input_grads_send.1.refs_3_), channel_id=1, source_target_pairs={{0,1},{1,0},{2,3},{3,2},{4,5},{5,4},{6,7},{7,6},{8,9},{9,8},{10,11... | collective-permute-start | bytes 1572872 | tf_op jit(solution)/shard_map/ppermute | solution.py:308
  83.0 0.1 fold1.6
  83.1 2.5 %collective-permute-start.21 = (bf16[16,3456]{1,0:T(8,128)(2,1)S(1)}, bf16[16,3456]{1,0:T(8,128)(2,1)S(1)}, u32[]{:S(2)}, u32[]{:S(2)}) collective-permute-start(bf16[16,3456]{1,0:T(8,128)(2,1)S(1)} %get-tuple-element.44), channel_id=1, source_target_pairs={{0,16},{2,18},{4,20},{6,22},{8,24},{10,26},{12,28},{14,30},{16,0},... | collective-permute-start | bytes 331784 | tf_op jit(solution)/shard_map/ppermute | solution.py:308
  85.6 2.6 %outputs.1.refs_2_.refs_0_ = f32[8,128,256]{2,1,0:T(8,128)S(1)} custom-call(s32[2]{0:T(128)S(1)} %pad_add_fusion.refs_0_, bf16[3,18,160,128]{3,2,1,0:T(8,128)(2,1)S(1)} %get-tuple-element.27.refs_1_, bf16[128,6912]{1,0:T(8,128)(2,1)S(1)} %join2.11.refs_2_, bf16[8,128,256]{2,1,0:T(8,128)(2,1)S(1)} %bitcast.12, ...), custom_call_target="tpu_custom_call" | custom-call | flops 10000000000 | bytes 1 | tf_op jit(solution)/shard_map/outputs/pallas_call | solution.py:294
  88.3 2.6 %input_grads.1.refs_2_.refs_0_ = f32[8,128,256]{2,1,0:T(8,128)S(1)} custom-call(s32[2]{0:T(128)S(1)} %pad_add_fusion.refs_0_, bf16[3,18,160,128]{3,2,1,0:T(8,128)(2,1)S(1)} %hidden_grad.1.refs_2_.refs_1_, bf16[256,3456]{1,0:T(8,128)(2,1)S(1)} %copy-done.1, bf16[8,128,256]{2,1,0:T(8,128)(2,1)S(1)} %bitcast.9, bf16[8,6912]{1,0:T(8,128)(2,1)S(1)} %fold2.7.refs_4_.refs_1_), custom_call_target="tpu_custom_call" | custom-call | flops 1 | bytes 1 | tf_op jit(solution)/shard_map/input_grads/pallas_call | solution.py:294
  91.0 2.6 %collective-permute-start.25 = (bf16[8,6912]{1,0:T(8,128)(2,1)S(1)}, bf16[8,6912]{1,0:T(8,128)(2,1)S(1)}, u32[]{:S(2)}, u32[]{:S(2)}) collective-permute-start(bf16[8,6912]{1,0:T(8,128)(2,1)S(1)} %fold2.7.refs_4_.refs_1_), channel_id=1, source_target_pairs={{0,1},{1,0},{2,3},{3,2},{4,5},{5,4},{6,7},{7,6},{8,9},{9,8},{10,11... | collective-permute-start | bytes 331784 | tf_op jit(solution)/shard_map/ppermute | solution.py:308
  93.6 0.1 collective-permute-start.24
  93.8 0.9 finish.2.refs_4_
  94.7 3.4 %collective-permute-done.25.refs_2_ = bf16[8,6912]{1,0:T(8,128)(2,1)S(1)} collective-permute-done((bf16[8,6912]{1,0:T(8,128)(2,1)S(1)}, bf16[8,6912]{1,0:T(8,128)(2,1)S(1)}, u32[]{:S(2)}, u32[]{:S(2)}) %collective-permute-start.25) | collective-permute-done | bytes 110624 | tf_op jit(solution)/shard_map/ppermute | solution.py:308
  98.1 1.0 copy-done.6
  99.2 1.4 %update_second.1.refs_4_ = f32[16,6912]{1,0:T(8,128)} custom-call(s32[2]{0:T(128)S(1)} %pad_add_fusion.refs_0_, bf16[8,6912]{1,0:T(8,128)(2,1)S(1)} %fold2.7.refs_4_.refs_1_, bf16[8,6912]{1,0:T(8,128)(2,1)S(1)} %collective-permute-done.25.refs_2_, f32[16,6912]{1,0:T(8,128)S(1)} %base2.1.refs_3_, bf16[8,128,256]{2,1,0:T(8,128)(2,1)S(1)} %copy-done.6), custom_call_target="tpu_custom_call" | custom-call | flops 1 | bytes 1 | tf_op jit(solution)/shard_map/update_second/pallas_call | solution.py:294
  100.5 1.0 copy-done.9
  101.6 2.3 %update_first.1.refs_2_ = f32[16,6912]{1,0:T(8,128)} custom-call(s32[2]{0:T(128)S(1)} %pad_add_fusion.refs_0_, bf16[16,3456]{1,0:T(8,128)(2,1)S(1)} %fold1.7.refs_2_.refs_1_, bf16[16,3456]{1,0:T(8,128)(2,1)S(1)} %collective-permute-done.24.refs_2_, f32[16,6912]{1,0:T(8,128)S(1)} %copy-done.5, f32[16,6912]{1,0:T(8,128)S(1)} %copy-done.9), custom_call_target="tpu_custom_call" | custom-call | flops 1 | bytes 1 | tf_op jit(solution)/shard_map/update_first/pallas_call | solution.py:294
  103.9 1.0 copy-done.10
  104.9 0.9 finish.3
  (77 shorter events, 0.9 us)
Async XLA Ops:
  0.7 1.0 copy-start.7
  2.6 9.5 %collective-permute-start.1 = (bf16[16,3456]{1,0:T(8,128)(2,1)S(1)}, bf16[16,3456]{1,0:T(8,128)(2,1)S(1)}, u32[]{:S(2)}, u32[]{:S(2)}) collective-permute-start(bf16[16,3456]{1,0:T(8,128)(2,1)S(1)} %first_columns.1.refs_0_), channel_id=1, source_target_pairs={{0,16},{2,18},{4,20},{6,22},{8,24},{10,26},{12,28},{14,30},{16,0},... | collective-permute-start | bytes 331784 | tf_op jit(solution)/shard_map/ppermute | solution.py:308
  6.7 16.0 %collective-permute-start = (bf16[8,128,256]{2,1,0:T(8,128)(2,1)}, bf16[8,128,256]{2,1,0:T(8,128)(2,1)S(1)}, u32[]{:S(2)}, u32[]{:S(2)}) collective-permute-start(bf16[8,128,256]{2,1,0:T(8,128)(2,1)} %bitcast.10), channel_id=1, source_target_pairs={{0,1},{1,0},{2,3},{3,2},{4,5},{5,4},{6,7},{7,6},{8,9},{9,8},{10,11... | collective-permute-start | bytes 1572872 | tf_op jit(solution)/shard_map/ppermute | solution.py:308
  8.2 30.9 %collective-permute-start.10 = (bf16[8,128,256]{2,1,0:T(8,128)(2,1)}, bf16[8,128,256]{2,1,0:T(8,128)(2,1)}, u32[]{:S(2)}, u32[]{:S(2)}) collective-permute-start(bf16[8,128,256]{2,1,0:T(8,128)(2,1)} %bitcast.7), channel_id=1, source_target_pairs={{0,1},{1,0},{2,3},{3,2},{4,5},{5,4},{6,7},{7,6},{8,9},{9,8},{10,11... | collective-permute-start | bytes 1572872 | tf_op jit(solution)/shard_map/ppermute | solution.py:308
  12.2 10.5 %collective-permute-start.3 = (bf16[32,3456]{1,0:T(8,128)(2,1)S(1)}, bf16[32,3456]{1,0:T(8,128)(2,1)S(1)}, u32[]{:S(2)}, u32[]{:S(2)}) collective-permute-start(bf16[32,3456]{1,0:T(8,128)(2,1)S(1)} %join1.4.refs_2_.refs_0_), channel_id=1, source_target_pairs={{0,4},{2,6},{4,0},{6,2},{8,12},{10,14},{12,8},{14,10},{16,20},{18,... | collective-permute-start | bytes 663560 | tf_op jit(solution)/shard_map/ppermute | solution.py:308
  13.8 6.0 %collective-permute-start.2 = (bf16[32,3456]{1,0:T(8,128)(2,1)S(1)}, bf16[32,3456]{1,0:T(8,128)(2,1)S(1)}, u32[]{:S(2)}, u32[]{:S(2)}) collective-permute-start(bf16[32,3456]{1,0:T(8,128)(2,1)S(1)} %join1.4.refs_2_.refs_0_), channel_id=1, source_target_pairs={{0,8},{2,10},{4,12},{6,14},{8,0},{10,2},{12,4},{14,6},{16,24},{18,... | collective-permute-start | bytes 663560 | tf_op jit(solution)/shard_map/ppermute | solution.py:308
  14.5 1.0 copy-start.16
  15.5 7.2 %copy-start.23 = (bf16[1,8,8,16,256]{4,3,2,1,0:T(8,128)(2,1)S(1)}, bf16[1,8,8,16,256]{4,3,2,1,0:T(8,128)(2,1)}, u32[]{:S(2)}) copy-start(bf16[1,8,8,16,256]{4,3,2,1,0:T(8,128)(2,1)} %param.6) | copy-start | bytes 1572868
  16.1 10.6 %collective-permute-start.6 = (bf16[8,6912]{1,0:T(8,128)(2,1)S(1)}, bf16[8,6912]{1,0:T(8,128)(2,1)S(1)}, u32[]{:S(2)}, u32[]{:S(2)}) collective-permute-start(bf16[8,6912]{1,0:T(8,128)(2,1)S(1)} %second_rows.1.refs_3_.refs_0_), channel_id=1, source_target_pairs={{0,16},{2,18},{4,20},{6,22},{8,24},{10,26},{12,28},{14,30},{16,0},... | collective-permute-start | bytes 331784 | tf_op jit(solution)/shard_map/ppermute | solution.py:308
  19.8 6.7 %collective-permute-start.4 = (bf16[32,3456]{1,0:T(8,128)(2,1)S(1)}, bf16[32,3456]{1,0:T(8,128)(2,1)S(1)}, u32[]{:S(2)}, u32[]{:S(2)}) collective-permute-start(bf16[32,3456]{1,0:T(8,128)(2,1)S(1)} %collective-permute-done.2.refs_1_), channel_id=1, source_target_pairs={{0,4},{2,6},{4,0},{6,2},{8,12},{10,14},{12,8},{14,10},{16,20},{18,... | collective-permute-start | bytes 663560 | tf_op jit(solution)/shard_map/ppermute | solution.py:308
  22.7 1.8 %copy-start.8 = (f32[16,6912]{1,0:T(8,128)S(1)}, f32[16,6912]{1,0:T(8,128)}, u32[]{:S(2)}) copy-start(f32[16,6912]{1,0:T(8,128)} %refs_0_.2) | copy-start | bytes 1327108
  22.7 1.8 %copy-start.15 = (f32[16,6912]{1,0:T(8,128)S(1)}, f32[16,6912]{1,0:T(8,128)}, u32[]{:S(2)}) copy-start(f32[16,6912]{1,0:T(8,128)} %refs_1_.6) | copy-start | bytes 1327108
  24.4 2.2 %copy-start.11 = (bf16[256,2048]{1,0:T(8,128)(2,1)}, bf16[256,2048]{1,0:T(8,128)(2,1)S(1)}, u32[]{:S(2)}) copy-start(bf16[256,2048]{1,0:T(8,128)(2,1)S(1)} %get-tuple-element.26.refs_2_.refs_0_) | copy-start | bytes 3145732
  24.5 2.2 %copy-start.4 = (f32[16,6912]{1,0:T(8,128)}, f32[16,6912]{1,0:T(8,128)S(1)}, u32[]{:S(2)}) copy-start(f32[16,6912]{1,0:T(8,128)S(1)} %base1.1.refs_2_.refs_3_) | copy-start | bytes 1327108
  26.6 2.5 %collective-permute-start.5 = (bf16[128,3456]{1,0:T(8,128)(2,1)S(1)}, bf16[128,3456]{1,0:T(8,128)(2,1)S(1)}, u32[]{:S(2)}, u32[]{:S(2)}) collective-permute-start(bf16[128,3456]{1,0:T(8,128)(2,1)S(1)} %join1.6.refs_2_.refs_1_), channel_id=1, source_target_pairs={{0,2},{2,0},{4,6},{6,4},{8,10},{10,8},{12,14},{14,12},{16,18},{18,... | collective-permute-start | bytes 2654216 | tf_op jit(solution)/shard_map/ppermute | solution.py:308
  26.7 12.3 %collective-permute-start.8 = (bf16[16,6912]{1,0:T(8,128)(2,1)S(1)}, bf16[16,6912]{1,0:T(8,128)(2,1)S(1)}, u32[]{:S(2)}, u32[]{:S(2)}) collective-permute-start(bf16[16,6912]{1,0:T(8,128)(2,1)S(1)} %join2.7.refs_3_.refs_0_), channel_id=1, source_target_pairs={{0,4},{2,6},{4,0},{6,2},{8,12},{10,14},{12,8},{14,10},{16,20},{18,... | collective-permute-start | bytes 663560 | tf_op jit(solution)/shard_map/ppermute | solution.py:308
  28.8 8.1 %collective-permute-start.7 = (bf16[16,6912]{1,0:T(8,128)(2,1)S(1)}, bf16[16,6912]{1,0:T(8,128)(2,1)S(1)}, u32[]{:S(2)}, u32[]{:S(2)}) collective-permute-start(bf16[16,6912]{1,0:T(8,128)(2,1)S(1)} %join2.7.refs_3_.refs_0_), channel_id=1, source_target_pairs={{0,8},{2,10},{4,12},{6,14},{8,0},{10,2},{12,4},{14,6},{16,24},{18,... | collective-permute-start | bytes 663560 | tf_op jit(solution)/shard_map/ppermute | solution.py:308
  29.8 7.1 %copy-start = (bf16[256,3456]{1,0:T(8,128)(2,1)}, bf16[256,3456]{1,0:T(8,128)(2,1)S(1)}, u32[]{:S(2)}) copy-start(bf16[256,3456]{1,0:T(8,128)(2,1)S(1)} %place1.1.refs_2_) | copy-start | bytes 5308420
  36.9 2.2 %copy-start.13 = (bf16[1,8,8,16,256]{4,3,2,1,0:T(8,128)(2,1)S(1)}, bf16[1,8,8,16,256]{4,3,2,1,0:T(8,128)(2,1)}, u32[]{:S(2)}) copy-start(bf16[1,8,8,16,256]{4,3,2,1,0:T(8,128)(2,1)} %param.7) | copy-start | bytes 1572868
  36.9 8.6 %collective-permute-start.9 = (bf16[16,6912]{1,0:T(8,128)(2,1)S(1)}, bf16[16,6912]{1,0:T(8,128)(2,1)S(1)}, u32[]{:S(2)}, u32[]{:S(2)}) collective-permute-start(bf16[16,6912]{1,0:T(8,128)(2,1)S(1)} %join2.9), channel_id=1, source_target_pairs={{0,4},{2,6},{4,0},{6,2},{8,12},{10,14},{12,8},{14,10},{16,20},{18,... | collective-permute-start | bytes 663560 | tf_op jit(solution)/shard_map/ppermute | solution.py:308
  41.0 4.4 %copy-start.2 = (bf16[3,18,160,256]{3,2,1,0:T(8,128)(2,1)}, bf16[3,18,160,256]{3,2,1,0:T(8,128)(2,1)S(1)}, u32[]{:S(2)}) copy-start(bf16[3,18,160,256]{3,2,1,0:T(8,128)(2,1)S(1)} %spread_cotangent.1.refs_1_) | copy-start | bytes 13271044
  45.4 2.5 %collective-permute-start.12 = (bf16[64,6912]{1,0:T(8,128)(2,1)S(1)}, bf16[64,6912]{1,0:T(8,128)(2,1)S(1)}, u32[]{:S(2)}, u32[]{:S(2)}) collective-permute-start(bf16[64,6912]{1,0:T(8,128)(2,1)S(1)} %get-tuple-element.31), channel_id=1, source_target_pairs={{0,2},{2,0},{4,6},{6,4},{8,10},{10,8},{12,14},{14,12},{16,18},{18,... | collective-permute-start | bytes 2654216 | tf_op jit(solution)/shard_map/ppermute | solution.py:308
  45.6 3.6 %collective-permute-start.11 = (bf16[64,6912]{1,0:T(8,128)(2,1)S(1)}, bf16[64,6912]{1,0:T(8,128)(2,1)S(1)}, u32[]{:S(2)}, u32[]{:S(2)}) collective-permute-start(bf16[64,6912]{1,0:T(8,128)(2,1)S(1)} %join2.10.refs_2_.refs_0_), channel_id=1, source_target_pairs={{0,2},{2,0},{4,6},{6,4},{8,10},{10,8},{12,14},{14,12},{16,18},{18,... | collective-permute-start | bytes 2654216 | tf_op jit(solution)/shard_map/ppermute | solution.py:308
  47.9 2.3 %copy-start.3 = (bf16[3,18,160,256]{3,2,1,0:T(8,128)(2,1)S(1)}, bf16[3,18,160,256]{3,2,1,0:T(8,128)(2,1)}, u32[]{:S(2)}) copy-start(bf16[3,18,160,256]{3,2,1,0:T(8,128)(2,1)} %copy-done.2) | copy-start | bytes 13271044
  48.1 10.0 %collective-permute-start.13 = (bf16[16,6912]{1,0:T(8,128)(2,1)S(1)}, bf16[16,6912]{1,0:T(8,128)(2,1)S(1)}, u32[]{:S(2)}, u32[]{:S(2)}) collective-permute-start(bf16[16,6912]{1,0:T(8,128)(2,1)S(1)} %get-tuple-element.34), channel_id=1, source_target_pairs={{0,4},{2,6},{4,0},{6,2},{8,12},{10,14},{12,8},{14,10},{16,20},{18,... | collective-permute-start | bytes 663560 | tf_op jit(solution)/shard_map/ppermute | solution.py:308
  49.3 0.7 copy-start.21
  57.1 2.0 %copy-start.12 = (bf16[256,2048]{1,0:T(8,128)(2,1)S(1)}, bf16[256,2048]{1,0:T(8,128)(2,1)}, u32[]{:S(2)}) copy-start(bf16[256,2048]{1,0:T(8,128)(2,1)} %copy-done.11) | copy-start | bytes 3145732
  57.1 7.5 %collective-permute-start.16 = (bf16[16,6912]{1,0:T(8,128)(2,1)S(1)}, bf16[16,6912]{1,0:T(8,128)(2,1)S(1)}, u32[]{:S(2)}, u32[]{:S(2)}) collective-permute-start(bf16[16,6912]{1,0:T(8,128)(2,1)S(1)} %join2.12), channel_id=1, source_target_pairs={{0,4},{2,6},{4,0},{6,2},{8,12},{10,14},{12,8},{14,10},{16,20},{18,... | collective-permute-start | bytes 663560 | tf_op jit(solution)/shard_map/ppermute | solution.py:308
  58.1 7.3 %copy-start.22 = (bf16[16,6912]{1,0:T(8,128)(2,1)S(1)}, bf16[16,6912]{1,0:T(8,128)(2,1)}, u32[]{:S(2)}) copy-start(bf16[16,6912]{1,0:T(8,128)(2,1)} %copy-done.21) | copy-start | bytes 663556
  58.1 7.3 %collective-permute-start.15 = (bf16[16,6912]{1,0:T(8,128)(2,1)S(1)}, bf16[16,6912]{1,0:T(8,128)(2,1)S(1)}, u32[]{:S(2)}, u32[]{:S(2)}) collective-permute-start(bf16[16,6912]{1,0:T(8,128)(2,1)S(1)} %fold2.5.refs_2_), channel_id=1, source_target_pairs={{0,8},{2,10},{4,12},{6,14},{8,0},{10,2},{12,4},{14,6},{16,24},{18,... | collective-permute-start | bytes 663560 | tf_op jit(solution)/shard_map/ppermute | solution.py:308
  63.1 2.5 %collective-permute-start.14 = (bf16[128,3456]{1,0:T(8,128)(2,1)S(1)}, bf16[128,3456]{1,0:T(8,128)(2,1)S(1)}, u32[]{:S(2)}, u32[]{:S(2)}) collective-permute-start(bf16[128,3456]{1,0:T(8,128)(2,1)S(1)} %get-tuple-element.36), channel_id=1, source_target_pairs={{0,2},{2,0},{4,6},{6,4},{8,10},{10,8},{12,14},{14,12},{16,18},{18,... | collective-permute-start | bytes 2654216 | tf_op jit(solution)/shard_map/ppermute | solution.py:308
  65.5 1.5 %copy-start.19 = (bf16[8,6912]{1,0:T(8,128)(2,1)}, bf16[8,6912]{1,0:T(8,128)(2,1)S(1)}, u32[]{:S(2)}) copy-start(bf16[8,6912]{1,0:T(8,128)(2,1)S(1)} %get-tuple-element.38.refs_2_.refs_0_) | copy-start | bytes 331780
  65.8 8.0 %collective-permute-start.17 = (bf16[32,3456]{1,0:T(8,128)(2,1)S(1)}, bf16[32,3456]{1,0:T(8,128)(2,1)S(1)}, u32[]{:S(2)}, u32[]{:S(2)}) collective-permute-start(bf16[32,3456]{1,0:T(8,128)(2,1)S(1)} %get-tuple-element.41), channel_id=1, source_target_pairs={{0,4},{2,6},{4,0},{6,2},{8,12},{10,14},{12,8},{14,10},{16,20},{18,... | collective-permute-start | bytes 663560 | tf_op jit(solution)/shard_map/ppermute | solution.py:308
  67.0 8.4 %copy-start.1 = (bf16[256,3456]{1,0:T(8,128)(2,1)S(1)}, bf16[256,3456]{1,0:T(8,128)(2,1)}, u32[]{:S(2)}) copy-start(bf16[256,3456]{1,0:T(8,128)(2,1)} %copy-done) | copy-start | bytes 5308420
  69.8 24.0 %collective-permute-start.20 = (bf16[8,128,256]{2,1,0:T(8,128)(2,1)S(1)}, bf16[8,128,256]{2,1,0:T(8,128)(2,1)S(1)}, u32[]{:S(2)}, u32[]{:S(2)}) collective-permute-start(bf16[8,128,256]{2,1,0:T(8,128)(2,1)S(1)} %outputs_send.1.refs_2_.refs_1_), channel_id=1, source_target_pairs={{0,1},{1,0},{2,3},{3,2},{4,5},{5,4},{6,7},{7,6},{8,9},{9,8},{10,11... | collective-permute-start | bytes 1572872 | tf_op jit(solution)/shard_map/ppermute | solution.py:308
  70.6 12.4 %collective-permute-start.19 = (bf16[32,3456]{1,0:T(8,128)(2,1)S(1)}, bf16[32,3456]{1,0:T(8,128)(2,1)S(1)}, u32[]{:S(2)}, u32[]{:S(2)}) collective-permute-start(bf16[32,3456]{1,0:T(8,128)(2,1)S(1)} %join1.7), channel_id=1, source_target_pairs={{0,4},{2,6},{4,0},{6,2},{8,12},{10,14},{12,8},{14,10},{16,20},{18,... | collective-permute-start | bytes 663560 | tf_op jit(solution)/shard_map/ppermute | solution.py:308
  73.9 11.8 %copy-start.24 = (bf16[1,8,8,16,256]{4,3,2,1,0:T(8,128)(2,1)S(1)}, bf16[1,8,8,16,256]{4,3,2,1,0:T(8,128)(2,1)}, u32[]{:S(2)}) copy-start(bf16[1,8,8,16,256]{4,3,2,1,0:T(8,128)(2,1)} %param.6) | copy-start | bytes 1572868
  73.9 9.1 %collective-permute-start.18 = (bf16[32,3456]{1,0:T(8,128)(2,1)S(1)}, bf16[32,3456]{1,0:T(8,128)(2,1)S(1)}, u32[]{:S(2)}, u32[]{:S(2)}) collective-permute-start(bf16[32,3456]{1,0:T(8,128)(2,1)S(1)} %fold1.5.refs_3_.refs_1_), channel_id=1, source_target_pairs={{0,8},{2,10},{4,12},{6,14},{8,0},{10,2},{12,4},{14,6},{16,24},{18,... | collective-permute-start | bytes 663560 | tf_op jit(solution)/shard_map/ppermute | solution.py:308
  78.0 10.3 %collective-permute-start.22 = (bf16[8,6912]{1,0:T(8,128)(2,1)S(1)}, bf16[8,6912]{1,0:T(8,128)(2,1)S(1)}, u32[]{:S(2)}, u32[]{:S(2)}) collective-permute-start(bf16[8,6912]{1,0:T(8,128)(2,1)S(1)} %join2.13), channel_id=1, source_target_pairs={{0,16},{2,18},{4,20},{6,22},{8,24},{10,26},{12,28},{14,30},{16,0},... | collective-permute-start | bytes 331784 | tf_op jit(solution)/shard_map/ppermute | solution.py:308
  80.9 23.0 %collective-permute-start.23 = (bf16[8,128,256]{2,1,0:T(8,128)(2,1)S(1)}, bf16[8,128,256]{2,1,0:T(8,128)(2,1)S(1)}, u32[]{:S(2)}, u32[]{:S(2)}) collective-permute-start(bf16[8,128,256]{2,1,0:T(8,128)(2,1)S(1)} %input_grads_send.1.refs_3_), channel_id=1, source_target_pairs={{0,1},{1,0},{2,3},{3,2},{4,5},{5,4},{6,7},{7,6},{8,9},{9,8},{10,11... | collective-permute-start | bytes 1572872 | tf_op jit(solution)/shard_map/ppermute | solution.py:308
  83.1 10.5 %collective-permute-start.21 = (bf16[16,3456]{1,0:T(8,128)(2,1)S(1)}, bf16[16,3456]{1,0:T(8,128)(2,1)S(1)}, u32[]{:S(2)}, u32[]{:S(2)}) collective-permute-start(bf16[16,3456]{1,0:T(8,128)(2,1)S(1)} %get-tuple-element.44), channel_id=1, source_target_pairs={{0,16},{2,18},{4,20},{6,22},{8,24},{10,26},{12,28},{14,30},{16,0},... | collective-permute-start | bytes 331784 | tf_op jit(solution)/shard_map/ppermute | solution.py:308
  85.6 2.6 %copy-start.20 = (bf16[8,6912]{1,0:T(8,128)(2,1)S(1)}, bf16[8,6912]{1,0:T(8,128)(2,1)}, u32[]{:S(2)}) copy-start(bf16[8,6912]{1,0:T(8,128)(2,1)} %copy-done.19) | copy-start | bytes 331780
  85.6 2.7 %copy-start.14 = (bf16[1,8,8,16,256]{4,3,2,1,0:T(8,128)(2,1)S(1)}, bf16[1,8,8,16,256]{4,3,2,1,0:T(8,128)(2,1)}, u32[]{:S(2)}) copy-start(bf16[1,8,8,16,256]{4,3,2,1,0:T(8,128)(2,1)} %param.7) | copy-start | bytes 1572868
  88.3 5.4 %copy-start.17 = (f32[16,6912]{1,0:T(8,128)S(1)}, f32[16,6912]{1,0:T(8,128)}, u32[]{:S(2)}) copy-start(f32[16,6912]{1,0:T(8,128)} %refs_0_.3) | copy-start | bytes 1327108
  88.3 5.4 %copy-start.18 = (f32[16,6912]{1,0:T(8,128)S(1)}, f32[16,6912]{1,0:T(8,128)}, u32[]{:S(2)}) copy-start(f32[16,6912]{1,0:T(8,128)} %refs_1_.7) | copy-start | bytes 1327108
  91.0 7.2 %collective-permute-start.25 = (bf16[8,6912]{1,0:T(8,128)(2,1)S(1)}, bf16[8,6912]{1,0:T(8,128)(2,1)S(1)}, u32[]{:S(2)}, u32[]{:S(2)}) collective-permute-start(bf16[8,6912]{1,0:T(8,128)(2,1)S(1)} %fold2.7.refs_4_.refs_1_), channel_id=1, source_target_pairs={{0,1},{1,0},{2,3},{3,2},{4,5},{5,4},{6,7},{7,6},{8,9},{9,8},{10,11... | collective-permute-start | bytes 331784 | tf_op jit(solution)/shard_map/ppermute | solution.py:308
  93.6 6.9 %collective-permute-start.24 = (bf16[16,3456]{1,0:T(8,128)(2,1)S(1)}, bf16[16,3456]{1,0:T(8,128)(2,1)S(1)}, u32[]{:S(2)}, u32[]{:S(2)}) collective-permute-start(bf16[16,3456]{1,0:T(8,128)(2,1)S(1)} %fold1.7.refs_2_.refs_1_), channel_id=1, source_target_pairs={{0,1},{1,0},{2,3},{3,2},{4,5},{5,4},{6,7},{7,6},{8,9},{9,8},{10,11... | collective-permute-start | bytes 331784 | tf_op jit(solution)/shard_map/ppermute | solution.py:308
  93.8 6.7 %copy-start.5 = (f32[16,6912]{1,0:T(8,128)S(1)}, f32[16,6912]{1,0:T(8,128)}, u32[]{:S(2)}) copy-start(f32[16,6912]{1,0:T(8,128)} %copy-done.4) | copy-start | bytes 1327108
  98.1 1.0 copy-start.6
  100.5 1.0 copy-start.9
  103.9 1.0 copy-start.10

commit v2 on v1

--- a/solution.py
+++ b/solution.py
@@ -11,7 +11,7 @@
 NOISE_COEF = 0.25
 BF = jnp.bfloat16
 F32 = jnp.float32
-SPARE = 8 * 2**20
+SPARE, SPARE_HEAVY = 2**20, 5 * 2**20
 NONE, SHORTER, ALL = 1, 10**10, 10**11
 
 
@@ -254,16 +254,15 @@
     h = idx[1]
     hid = own.shape[1] // 27
     channels = 2 * hid
-    mine = member_matrix(h, channels, half)
-    theirs = member_matrix(1 - h, channels, half)
+    rows = own.shape[0]
+    spread = jnp.concatenate([member_matrix(h, channels, half), member_matrix(1 - h, channels, half)], axis=1)
+    both = [jnp.concatenate([r[:, u * hid : (u + 1) * hid] for u in range(27)], axis=0) for r in (own, other)]
+    grad = dot_nt(jnp.concatenate(both, axis=1), spread)
     for a in range(3):
         for bc in range(9):
-            t = a * 9 + bc
-            u = bc * 3 + a
+            t, u = a * 9 + bc, bc * 3 + a
             cols = slice(t * channels, (t + 1) * channels)
-            part = slice(u * hid, (u + 1) * hid)
-            grad = dot_nt(own[:, part], mine) + dot_nt(other[:, part], theirs)
-            new[:, cols] = base[:, cols] - rate * grad
+            new[:, cols] = base[:, cols] - rate * grad[u * rows : (u + 1) * rows]
 
 
 def update_second_kernel(half, rate, idx, own, other, base, new):
@@ -297,7 +296,7 @@
         in_specs=[smem] * scalars + [vmem] * (count - scalars) + [anywhere] * len(after),
         out_specs=tuple([vmem] * len(outs)),
         scratch_shapes=list(scratch),
-        compiler_params=pltpu.CompilerParams(vmem_limit_bytes=room + SPARE),
+        compiler_params=pltpu.CompilerParams(vmem_limit_bytes=room + (SPARE if room < 5 * 2**20 else SPARE_HEAVY)),
         cost_estimate=pl.CostEstimate(flops=cost, bytes_accessed=1, transcendentals=0),
         name=name,
     )(*args, *after)
@@ -485,50 +484,51 @@
 
     (q23,) = fold((q23, trade(q67, "dp", near)), "fold2", after=(g3,))
     line2, near2 = trade(q23, "dp", line), trade(join((q45,), "join2", after=(g3,)), "dp", near)
+    part, whole = shape((slab, area, channels), BF), shape((slab, area, channels), F32)
+    (send_out,) = run(
+        functools.partial(outputs_kernel, dims, False), (idx, a3, w2), (part,), "outputs_send", ALL, after=(q23,)
+    )
+    came_out = trade(send_out, "space", 1)
     keep1, send1 = run(
         functools.partial(first_grad_kernel, dims),
         (xt, g3),
         (shape((channels // 2, 27 * hid), BF),) * 2,
         "first_grad",
-        ALL,
+        NONE,
         scalars=0,
-        after=(q23,),
+        after=(send_out,),
     )
     q0, q1 = fold((q01, line2, near2), "fold2", split=2, after=(keep1,), cost=ALL)
     p01, p23, p45, p67 = fold((keep1, trade(send1, "dp", core)), "fold1", split=4, after=(q0,))
     near1 = trade(p67, "dp", near)
-    part, whole = shape((slab, area, channels), BF), shape((slab, area, channels), F32)
-    (send_out,) = run(
-        functools.partial(outputs_kernel, dims, False), (idx, a3, w2), (part,), "outputs_send", ALL, after=(p01,)
-    )
-    came_out = trade(send_out, "space", 1)
-    (p23,) = fold((p23, near1), "fold1", after=(send_out,))
-    line1, near1 = trade(p23, "dp", line), trade(join((p45,), "join1", after=(send_out,)), "dp", near)
-    far2 = trade(join((q1,), "join2", after=(p23,)), "dp", far)
     (send_in,) = run(
-        functools.partial(input_grads_kernel, dims, False), (idx, g3, w1), (part,), "input_grads_send", ALL, after=(p23,)
+        functools.partial(input_grads_kernel, dims, False), (idx, g3, w1), (part,), "input_grads_send", ALL, after=(p01,)
     )
     came_in = trade(send_in, "space", 1)
-    p0, p1 = fold((p01, line1, near1), "fold1", split=2, after=(send_in,))
+    (p23,) = fold((p23, near1), "fold1", after=(send_in,))
+    line1, near1 = trade(p23, "dp", line), trade(join((p45,), "join1", after=(p23,)), "dp", near)
+    far2 = trade(q1, "dp", far)
     (own_out,) = run(
-        functools.partial(outputs_kernel, dims, True), (idx, a3, w2, volume), (whole,), "outputs", SHORTER, after=(p0,)
-    )
-    (share2,) = fold((q0, far2), "fold2", after=(own_out,))
-    share2 = over_pairs(share2)
-    other2 = trade(share2, "space", 1)
+        functools.partial(outputs_kernel, dims, True), (idx, a3, w2, volume), (whole,), "outputs", ALL, after=(p23,)
+    )
+    p0, p1 = fold((p01, line1, near1), "fold1", split=2, after=(own_out,))
     (own_in,) = run(
         functools.partial(input_grads_kernel, dims, True),
         (idx, g3, w1, upstream),
         (whole,),
         "input_grads",
-        NONE,
-        after=(share2,),
-    )
-    (share1,) = fold((p0, trade(p1, "dp", far)), "fold1", after=(own_in,))
+        SHORTER,
+        after=(p0,),
+    )
+    (share2,) = fold((q0, far2), "fold2", after=(own_in,))
+    share2 = over_pairs(share2)
+    other2 = trade(share2, "space", 1)
+    (base2,) = run(base_kernel, (second_weight, second_noise), (sum_of,), "base2", NONE, scalars=0, after=(share2,))
+    (outputs,) = run(finish_kernel, (own_out, came_out), (part,), "finish", NONE, scalars=0, after=(base2,))
+    (input_grads,) = run(finish_kernel, (own_in, came_in), (part,), "finish", NONE, scalars=0, after=(outputs,))
+    (share1,) = fold((p0, trade(p1, "dp", far)), "fold1", after=(input_grads,))
     share1 = over_pairs(share1)
     other1 = trade(share1, "space", 1)
-    (base2,) = run(base_kernel, (second_weight, second_noise), (sum_of,), "base2", NONE, scalars=0, after=(own_out,))
-    (outputs,) = run(finish_kernel, (own_out, came_out), (part,), "finish", NONE, scalars=0, after=(share1, base2))
     rate = 1.0 / math.sqrt(slab * area * devices * members)
     (new_second,) = run(
         functools.partial(update_second_kernel, half, rate),
@@ -536,7 +536,7 @@
         (sum_of,),
         "update_second",
         NONE,
-        after=(outputs,),
+        after=(share1,),
     )
     (new_first,) = run(
         functools.partial(update_first_kernel, half, rate),
@@ -546,7 +546,6 @@
         NONE,
         after=(new_second,),
     )
-    (input_grads,) = run(finish_kernel, (own_in, came_in), (part,), "finish", NONE, scalars=0, after=(new_first,))
     return (outputs.reshape(volumes.shape), input_grads.reshape(volumes.shape), new_first, new_second)
 
 

time: 106 us -> 107 us (level)
  Pallas kernels: 45.6 us -> 48.2 us
  starting transfers between devices: 37.3 us -> 35.1 us
    pallas_call x38 -> x37, Pallas kernels: 45.6 us -> 48.2 us  [run(): pl.pallas_call(entry, out_shape=tuple(outs), in_specs=[smem] * scalars +...]
    ppermute x26, starting transfers between devices: 37.3 us -> 35.1 us  [trade(): return lax.ppermute(array, axis, [(i, i ^ bit) for i in range(size)])]
  transfers between devices with their start and end apart: 26 -> 26, of which waited for: 11 -> 9; matrix products, arithmetic and copies ran while one was open for 0% -> 0% of each run, Pallas kernels for 41% -> 43%
where the time goes in v2:
time: 107 us; the launch traced here: 106 us
  Pallas kernels  48.2 us (45%)
  starting transfers between devices  35.1 us (33%)
  waiting for transfers between devices  15.9 us (15%)
  local copies, waits for them, and re-layouts  6.12 us (6%)
  between operations  1.1 us (1%)
    pallas_call x37, Pallas kernels, run(): pl.pallas_call(entry, out_shape=tuple(outs), in_specs=[smem] * scalars +...  48.2 us
    ppermute x26, starting transfers between devices, trade(): return lax.ppermute(array, axis, [(i, i ^ bit) for i in range(size)])  35.1 us
    ppermute x26, waiting for transfers between devices, trade(): return lax.ppermute(array, axis, [(i, i ^ bit) for i in range(size)])  15.9 us
    unnamed x50, local copies, waits for them, and re-layouts  6.12 us
  transfers between devices with their start and end apart: 26, of which 9 were waited for; matrix products, arithmetic and copies ran while one was open for 0% of the time, Pallas kernels for 43%

profile of v2, /device:TPU:0, one launch (start us, length us, event | category | flops | bytes accessed | tf_op | source)
XLA Modules:
  0.0 106.5 jit_solution(8316382411098514653)
XLA Ops:
  0.6 0.1 pad_add_fusion.refs_0_
  0.7 1.0 copy-done.8
  1.7 0.9 first_columns.1.refs_0_
  2.6 4.1 %collective-permute-start.1 = (bf16[16,3456]{1,0:T(8,128)(2,1)S(1)}, bf16[16,3456]{1,0:T(8,128)(2,1)S(1)}, u32[]{:S(2)}, u32[]{:S(2)}) collective-permute-start(bf16[16,3456]{1,0:T(8,128)(2,1)S(1)} %first_columns.1.refs_0_), channel_id=1, source_target_pairs={{0,16},{2,18},{4,20},{6,22},{8,24},{10,26},{12,28},{14,30},{16,0},... | collective-permute-start | bytes 331784 | tf_op jit(solution)/shard_map/ppermute | solution.py:307
  6.7 1.5 %collective-permute-start = (bf16[8,128,256]{2,1,0:T(8,128)(2,1)}, bf16[8,128,256]{2,1,0:T(8,128)(2,1)S(1)}, u32[]{:S(2)}, u32[]{:S(2)}) collective-permute-start(bf16[8,128,256]{2,1,0:T(8,128)(2,1)} %bitcast.8), channel_id=1, source_target_pairs={{0,1},{1,0},{2,3},{3,2},{4,5},{5,4},{6,7},{7,6},{8,9},{9,8},{10,11... | collective-permute-start | bytes 1572872 | tf_op jit(solution)/shard_map/ppermute | solution.py:307
  8.2 0.5 collective-permute-start.10
  8.7 3.4 %collective-permute-done.1.refs_1_ = bf16[16,3456]{1,0:T(8,128)(2,1)S(1)} collective-permute-done((bf16[16,3456]{1,0:T(8,128)(2,1)S(1)}, bf16[16,3456]{1,0:T(8,128)(2,1)S(1)}, u32[]{:S(2)}, u32[]{:S(2)}) %collective-permute-start.1) | collective-permute-done | bytes 110624 | tf_op jit(solution)/shard_map/ppermute | solution.py:307
  12.2 1.6 %collective-permute-start.3 = (bf16[32,3456]{1,0:T(8,128)(2,1)S(1)}, bf16[32,3456]{1,0:T(8,128)(2,1)S(1)}, u32[]{:S(2)}, u32[]{:S(2)}) collective-permute-start(bf16[32,3456]{1,0:T(8,128)(2,1)S(1)} %join1.4.refs_2_.refs_0_), channel_id=1, source_target_pairs={{0,4},{2,6},{4,0},{6,2},{8,12},{10,14},{12,8},{14,10},{16,20},{18,... | collective-permute-start | bytes 663560 | tf_op jit(solution)/shard_map/ppermute | solution.py:307
  13.8 0.7 collective-permute-start.2
  14.5 1.0 copy-done.14
  15.5 0.6 second_rows.1.refs_3_.refs_0_
  16.1 3.4 %collective-permute-start.6 = (bf16[8,6912]{1,0:T(8,128)(2,1)S(1)}, bf16[8,6912]{1,0:T(8,128)(2,1)S(1)}, u32[]{:S(2)}, u32[]{:S(2)}) collective-permute-start(bf16[8,6912]{1,0:T(8,128)(2,1)S(1)} %second_rows.1.refs_3_.refs_0_), channel_id=1, source_target_pairs={{0,16},{2,18},{4,20},{6,22},{8,24},{10,26},{12,28},{14,30},{16,0},... | collective-permute-start | bytes 331784 | tf_op jit(solution)/shard_map/ppermute | solution.py:307
  19.5 0.3 collective-permute-done.2.refs_1_
  19.8 2.8 %collective-permute-start.4 = (bf16[32,3456]{1,0:T(8,128)(2,1)S(1)}, bf16[32,3456]{1,0:T(8,128)(2,1)S(1)}, u32[]{:S(2)}, u32[]{:S(2)}) collective-permute-start(bf16[32,3456]{1,0:T(8,128)(2,1)S(1)} %collective-permute-done.2.refs_1_), channel_id=1, source_target_pairs={{0,4},{2,6},{4,0},{6,2},{8,12},{10,14},{12,8},{14,10},{16,20},{18,... | collective-permute-start | bytes 663560 | tf_op jit(solution)/shard_map/ppermute | solution.py:307
  22.7 1.7 %spread_volumes.1 = (bf16[3,18,160,256]{3,2,1,0:T(8,128)(2,1)S(1)}, bf16[256,2048]{1,0:T(8,128)(2,1)S(1)}) custom-call(s32[2]{0:T(128)S(1)} %pad_add_fusion.refs_0_, bf16[8,128,256]{2,1,0:T(8,128)(2,1)S(1)} %bitcast.9, bf16[8,128,256]{2,1,0:T(8,128)(2,1)S(1)} %collective-permute-done.refs_2_, bf16[96,3456]{1,0:T(8,128)(2,1)S(1)} %join1.5.refs_3_.refs_0_), custom_call_target="tpu_custom_call" | custom-call | flops 99999997952 | bytes 1 | tf_op jit(solution)/shard_map/spread_volumes/pallas_call | solution.py:293
  24.5 2.0 %collective-permute-done.4.refs_1_ = bf16[32,3456]{1,0:T(8,128)(2,1)S(1)} collective-permute-done((bf16[32,3456]{1,0:T(8,128)(2,1)S(1)}, bf16[32,3456]{1,0:T(8,128)(2,1)S(1)}, u32[]{:S(2)}, u32[]{:S(2)}) %collective-permute-start.4) | collective-permute-done | bytes 221216 | tf_op jit(solution)/shard_map/ppermute | solution.py:307
  26.6 0.1 collective-permute-start.5
  26.7 2.1 %collective-permute-start.8 = (bf16[16,6912]{1,0:T(8,128)(2,1)S(1)}, bf16[16,6912]{1,0:T(8,128)(2,1)S(1)}, u32[]{:S(2)}, u32[]{:S(2)}) collective-permute-start(bf16[16,6912]{1,0:T(8,128)(2,1)S(1)} %join2.6.refs_3_.refs_0_), channel_id=1, source_target_pairs={{0,4},{2,6},{4,0},{6,2},{8,12},{10,14},{12,8},{14,10},{16,20},{18,... | collective-permute-start | bytes 663560 | tf_op jit(solution)/shard_map/ppermute | solution.py:307
  28.8 0.3 collective-permute-done.5.refs_2_
  29.1 0.7 place1.1.refs_2_
  29.8 7.1 %hidden.1 = (bf16[3,18,160,128]{3,2,1,0:T(8,128)(2,1)S(1)}, bf16[128,2048]{1,0:T(8,128)(2,1)S(1)}, bf16[16,128,128]{2,1,0:T(8,128)(2,1)S(1)}) custom-call(s32[2]{0:T(128)S(1)} %pad_add_fusion.refs_0_, bf16[3,18,160,256]{3,2,1,0:T(8,128)(2,1)S(1)} %get-tuple-element.25.refs_1_, bf16[256,3456]{1,0:T(8,128)(2,1)S(1)} %place1.1.refs_2_), custom_call_target="tpu_custom_call" | custom-call | flops 10000000000 | bytes 1 | tf_op jit(solution)/shard_map/hidden/pallas_call | solution.py:293
  36.9 2.1 %collective-permute-start.9 = (bf16[16,6912]{1,0:T(8,128)(2,1)S(1)}, bf16[16,6912]{1,0:T(8,128)(2,1)S(1)}, u32[]{:S(2)}, u32[]{:S(2)}) collective-permute-start(bf16[16,6912]{1,0:T(8,128)(2,1)S(1)} %join2.8), channel_id=1, source_target_pairs={{0,4},{2,6},{4,0},{6,2},{8,12},{10,14},{12,8},{14,10},{16,20},{18,... | collective-permute-start | bytes 663560 | tf_op jit(solution)/shard_map/ppermute | solution.py:307
  39.1 1.9 %spread_cotangent.1.refs_1_ = bf16[3,18,160,256]{3,2,1,0:T(8,128)(2,1)S(1)} custom-call(s32[2]{0:T(128)S(1)} %pad_add_fusion.refs_0_, bf16[8,128,256]{2,1,0:T(8,128)(2,1)S(1)} %bitcast.12, bf16[8,128,256]{2,1,0:T(8,128)(2,1)} %collective-permute-done.10.refs_2_, bf16[48,6912]{1,0:T(8,128)(2,1)S(1)} %join2.7.refs_3_.refs_0_), custom_call_target="tpu_custom_call" | custom-call | flops 99999997952 | bytes 1 | tf_op jit(solution)/shard_map/spread_cotangent/pallas_call | solution.py:293
  41.0 4.4 %second_grad.1 = (bf16[64,6912]{1,0:T(8,128)(2,1)S(1)}, bf16[64,6912]{1,0:T(8,128)(2,1)S(1)}) custom-call(bf16[128,2048]{1,0:T(8,128)(2,1)S(1)} %get-tuple-element.29.refs_0_, bf16[3,18,160,256]{3,2,1,0:T(8,128)(2,1)S(1)} %spread_cotangent.1.refs_1_), custom_call_target="tpu_custom_call" | custom-call | flops 1 | bytes 1 | tf_op jit(solution)/shard_map/second_grad/pallas_call | solution.py:293
  45.4 0.1 collective-permute-start.12
  45.6 0.5 collective-permute-start.11
  46.1 1.8 %collective-permute-done.12.refs_1_ = bf16[64,6912]{1,0:T(8,128)(2,1)S(1)} collective-permute-done((bf16[64,6912]{1,0:T(8,128)(2,1)S(1)}, bf16[64,6912]{1,0:T(8,128)(2,1)S(1)}, u32[]{:S(2)}, u32[]{:S(2)}) %collective-permute-start.12) | collective-permute-done | bytes 884768 | tf_op jit(solution)/shard_map/ppermute | solution.py:307
  47.9 0.2 fold2.4
  48.1 0.9 collective-permute-start.13
  49.0 0.1 collective-permute-done.11.refs_1_
  49.2 0.1 join2.10.refs_2_
  49.3 0.7 copy-done.19
  50.0 0.2 copy-done.1
  50.2 6.9 %hidden_grad.1.refs_2_.refs_1_ = bf16[3,18,160,128]{3,2,1,0:T(8,128)(2,1)S(1)} custom-call(s32[2]{0:T(128)S(1)} %pad_add_fusion.refs_0_, bf16[3,18,160,256]{3,2,1,0:T(8,128)(2,1)S(1)} %copy-done.1, bf16[128,6912]{1,0:T(8,128)(2,1)S(1)} %join2.10.refs_2_, bf16[16,128,128]{2,1,0:T(8,128)(2,1)S(1)} %get-tuple-element.28.refs_3_.refs_1_), custom_call_target="tpu_custom_call" | custom-call | flops 99999997952 | bytes 1 | tf_op jit(solution)/shard_map/hidden_grad/pallas_call | solution.py:293
  57.1 0.9 collective-permute-start.16
  58.1 1.0 collective-permute-start.15
  59.1 3.4 %outputs_send.1.refs_2_ = bf16[8,128,256]{2,1,0:T(8,128)(2,1)} custom-call(s32[2]{0:T(128)S(1)} %pad_add_fusion.refs_0_, bf16[3,18,160,128]{3,2,1,0:T(8,128)(2,1)S(1)} %get-tuple-element.27.refs_1_, bf16[128,6912]{1,0:T(8,128)(2,1)S(1)} %join2.10.refs_2_, bf16[16,6912]{1,0:T(8,128)(2,1)S(1)} %fold2.5.refs_3_), custom_call_target="tpu_custom_call" | custom-call | flops 99999997952 | bytes 1 | tf_op jit(solution)/shard_map/outputs_send/pallas_call | solution.py:293
  62.5 0.9 collective-permute-start.18
  63.4 4.0 %first_grad.1 = (bf16[128,3456]{1,0:T(8,128)(2,1)S(1)}, bf16[128,3456]{1,0:T(8,128)(2,1)S(1)}) custom-call(bf16[256,2048]{1,0:T(8,128)(2,1)S(1)} %copy-done.3, bf16[3,18,160,128]{3,2,1,0:T(8,128)(2,1)S(1)} %hidden_grad.1.refs_2_.refs_1_, bf16[8,128,256]{2,1,0:T(8,128)(2,1)} %outputs_send.1.refs_2_), custom_call_target="tpu_custom_call" | custom-call | flops 1 | bytes 1 | tf_op jit(solution)/shard_map/first_grad/pallas_call | solution.py:293
  67.5 0.9 fold2.6
  68.4 4.7 %collective-permute-start.19 = (bf16[8,6912]{1,0:T(8,128)(2,1)}, bf16[8,6912]{1,0:T(8,128)(2,1)}, u32[]{:S(2)}, u32[]{:S(2)}) collective-permute-start(bf16[8,6912]{1,0:T(8,128)(2,1)} %get-tuple-element.42), channel_id=1, source_target_pairs={{0,16},{2,18},{4,20},{6,22},{8,24},{10,26},{12,28},{14,30},{16,0},... | collective-permute-start | bytes 331784 | tf_op jit(solution)/shard_map/ppermute | solution.py:307
  73.2 0.2 fold1.4
  73.4 0.9 collective-permute-start.17
  74.3 2.6 %input_grads_send.1.refs_2_ = bf16[8,128,256]{2,1,0:T(8,128)(2,1)S(1)} custom-call(s32[2]{0:T(128)S(1)} %pad_add_fusion.refs_0_, bf16[3,18,160,128]{3,2,1,0:T(8,128)(2,1)S(1)} %hidden_grad.1.refs_2_.refs_1_, bf16[256,3456]{1,0:T(8,128)(2,1)S(1)} %copy-done.12, bf16[32,3456]{1,0:T(8,128)(2,1)S(1)} %get-tuple-element.41.refs_3_.refs_0_), custom_call_target="tpu_custom_call" | custom-call | flops 99999997952 | bytes 1 | tf_op jit(solution)/shard_map/input_grads_send/pallas_call | solution.py:293
  77.0 0.6 collective-permute-start.22
  77.5 3.4 %collective-permute-done.17.refs_1_ = bf16[32,3456]{1,0:T(8,128)(2,1)S(1)} collective-permute-done((bf16[32,3456]{1,0:T(8,128)(2,1)S(1)}, bf16[32,3456]{1,0:T(8,128)(2,1)S(1)}, u32[]{:S(2)}, u32[]{:S(2)}) %collective-permute-start.17) | collective-permute-done | bytes 221216 | tf_op jit(solution)/shard_map/ppermute | solution.py:307
  81.0 0.6 collective-permute-start.20
  81.7 1.2 %collective-permute-start.21 = (bf16[32,3456]{1,0:T(8,128)(2,1)S(1)}, bf16[32,3456]{1,0:T(8,128)(2,1)S(1)}, u32[]{:S(2)}, u32[]{:S(2)}) collective-permute-start(bf16[32,3456]{1,0:T(8,128)(2,1)S(1)} %join1.7), channel_id=1, source_target_pairs={{0,4},{2,6},{4,0},{6,2},{8,12},{10,14},{12,8},{14,10},{16,20},{18,... | collective-permute-start | bytes 663560 | tf_op jit(solution)/shard_map/ppermute | solution.py:307
  83.0 2.6 %outputs.1.refs_3_.refs_0_ = f32[8,128,256]{2,1,0:T(8,128)S(1)} custom-call(s32[2]{0:T(128)S(1)} %pad_add_fusion.refs_0_, bf16[3,18,160,128]{3,2,1,0:T(8,128)(2,1)S(1)} %get-tuple-element.27.refs_1_, bf16[128,6912]{1,0:T(8,128)(2,1)S(1)} %join2.10.refs_2_, bf16[8,128,256]{2,1,0:T(8,128)(2,1)S(1)} %bitcast.10, bf16[32,3456]{1,0:T(8,128)(2,1)S(1)} %fold1.5.refs_4_.refs_1_), custom_call_target="tpu_custom_call" | custom-call | flops 99999997952 | bytes 1 | tf_op jit(solution)/shard_map/outputs/pallas_call | solution.py:293
  85.6 2.7 %collective-permute-done.21.refs_2_ = bf16[32,3456]{1,0:T(8,128)(2,1)S(1)} collective-permute-done((bf16[32,3456]{1,0:T(8,128)(2,1)S(1)}, bf16[32,3456]{1,0:T(8,128)(2,1)S(1)}, u32[]{:S(2)}, u32[]{:S(2)}) %collective-permute-start.21) | collective-permute-done | bytes 221216 | tf_op jit(solution)/shard_map/ppermute | solution.py:307
  88.2 0.1 fold1.6
  88.3 1.5 %collective-permute-start.23 = (bf16[16,3456]{1,0:T(8,128)(2,1)S(1)}, bf16[16,3456]{1,0:T(8,128)(2,1)S(1)}, u32[]{:S(2)}, u32[]{:S(2)}) collective-permute-start(bf16[16,3456]{1,0:T(8,128)(2,1)S(1)} %get-tuple-element.45), channel_id=1, source_target_pairs={{0,16},{2,18},{4,20},{6,22},{8,24},{10,26},{12,28},{14,30},{16,0},... | collective-permute-start | bytes 331784 | tf_op jit(solution)/shard_map/ppermute | solution.py:307
  89.8 2.6 %input_grads.1.refs_2_.refs_0_ = f32[8,128,256]{2,1,0:T(8,128)S(1)} custom-call(s32[2]{0:T(128)S(1)} %pad_add_fusion.refs_0_, bf16[3,18,160,128]{3,2,1,0:T(8,128)(2,1)S(1)} %hidden_grad.1.refs_2_.refs_1_, bf16[256,3456]{1,0:T(8,128)(2,1)S(1)} %copy-done.12, bf16[8,128,256]{2,1,0:T(8,128)(2,1)S(1)} %bitcast.13, ...), custom_call_target="tpu_custom_call" | custom-call | flops 10000000000 | bytes 1 | tf_op jit(solution)/shard_map/input_grads/pallas_call | solution.py:293
  92.5 0.9 fold2.7.refs_2_.refs_1_
  93.4 0.6 collective-permute-start.25
  94.1 2.0 %finish.2.refs_2_ = bf16[8,128,256]{2,1,0:T(8,128)(2,1)} custom-call(f32[8,128,256]{2,1,0:T(8,128)S(1)} %outputs.1.refs_3_.refs_0_, bf16[8,128,256]{2,1,0:T(8,128)(2,1)} %collective-permute-done.18.refs_1_, f32[16,6912]{1,0:T(8,128)S(1)} %base2.1.refs_2_.refs_3_), custom_call_target="tpu_custom_call" | custom-call | flops 1 | bytes 1 | tf_op jit(solution)/shard_map/finish/pallas_call | solution.py:293
  96.0 1.1 %copy-done.6 = bf16[8,128,256]{2,1,0:T(8,128)(2,1)S(1)} copy-done((bf16[8,128,256]{2,1,0:T(8,128)(2,1)S(1)}, bf16[8,128,256]{2,1,0:T(8,128)(2,1)}, u32[]{:S(2)}) %copy-start.6) | copy-done | bytes 524312
  97.1 0.9 finish.3.refs_2_
  98.0 1.0 copy-done.7
  99.1 1.6 %collective-permute-start.24 = (bf16[16,3456]{1,0:T(8,128)(2,1)S(1)}, bf16[16,3456]{1,0:T(8,128)(2,1)S(1)}, u32[]{:S(2)}, u32[]{:S(2)}) collective-permute-start(bf16[16,3456]{1,0:T(8,128)(2,1)S(1)} %fold1.7.refs_4_.refs_1_), channel_id=1, source_target_pairs={{0,1},{1,0},{2,3},{3,2},{4,5},{5,4},{6,7},{7,6},{8,9},{9,8},{10,11... | collective-permute-start | bytes 331784 | tf_op jit(solution)/shard_map/ppermute | solution.py:307
  100.7 1.4 %update_second.1.refs_4_ = f32[16,6912]{1,0:T(8,128)} custom-call(s32[2]{0:T(128)S(1)} %pad_add_fusion.refs_0_, bf16[8,6912]{1,0:T(8,128)(2,1)S(1)} %fold2.7.refs_2_.refs_1_, bf16[8,6912]{1,0:T(8,128)(2,1)S(1)} %collective-permute-done.25.refs_2_, f32[16,6912]{1,0:T(8,128)S(1)} %base2.1.refs_2_.refs_3_, bf16[16,3456]{1,0:T(8,128)(2,1)S(1)} %fold1.7.refs_4_.refs_1_), custom_call_target="tpu_custom_call" | custom-call | flops 1 | bytes 1 | tf_op jit(solution)/shard_map/update_second/pallas_call | solution.py:293
  102.0 1.9 %collective-permute-done.24.refs_2_ = bf16[16,3456]{1,0:T(8,128)(2,1)S(1)} collective-permute-done((bf16[16,3456]{1,0:T(8,128)(2,1)S(1)}, bf16[16,3456]{1,0:T(8,128)(2,1)S(1)}, u32[]{:S(2)}, u32[]{:S(2)}) %collective-permute-start.24) | collective-permute-done | bytes 110624 | tf_op jit(solution)/shard_map/ppermute | solution.py:307
  103.9 1.0 copy-done.10
  104.9 1.6 %update_first.1 = f32[16,6912]{1,0:T(8,128)} custom-call(s32[2]{0:T(128)S(1)} %pad_add_fusion.refs_0_, bf16[16,3456]{1,0:T(8,128)(2,1)S(1)} %fold1.7.refs_4_.refs_1_, bf16[16,3456]{1,0:T(8,128)(2,1)S(1)} %collective-permute-done.24.refs_2_, f32[16,6912]{1,0:T(8,128)S(1)} %copy-done.5, f32[16,6912]{1,0:T(8,128)S(1)} %copy-done.10), custom_call_target="tpu_custom_call" | custom-call | flops 1 | bytes 1 | tf_op jit(solution)/shard_map/update_first/pallas_call | solution.py:293
  (76 shorter events, 0.7 us)
Async XLA Ops:
  0.7 1.0 copy-start.8
  2.6 9.5 %collective-permute-start.1 = (bf16[16,3456]{1,0:T(8,128)(2,1)S(1)}, bf16[16,3456]{1,0:T(8,128)(2,1)S(1)}, u32[]{:S(2)}, u32[]{:S(2)}) collective-permute-start(bf16[16,3456]{1,0:T(8,128)(2,1)S(1)} %first_columns.1.refs_0_), channel_id=1, source_target_pairs={{0,16},{2,18},{4,20},{6,22},{8,24},{10,26},{12,28},{14,30},{16,0},... | collective-permute-start | bytes 331784 | tf_op jit(solution)/shard_map/ppermute | solution.py:307
  6.7 16.0 %collective-permute-start = (bf16[8,128,256]{2,1,0:T(8,128)(2,1)}, bf16[8,128,256]{2,1,0:T(8,128)(2,1)S(1)}, u32[]{:S(2)}, u32[]{:S(2)}) collective-permute-start(bf16[8,128,256]{2,1,0:T(8,128)(2,1)} %bitcast.8), channel_id=1, source_target_pairs={{0,1},{1,0},{2,3},{3,2},{4,5},{5,4},{6,7},{7,6},{8,9},{9,8},{10,11... | collective-permute-start | bytes 1572872 | tf_op jit(solution)/shard_map/ppermute | solution.py:307
  8.2 30.9 %collective-permute-start.10 = (bf16[8,128,256]{2,1,0:T(8,128)(2,1)}, bf16[8,128,256]{2,1,0:T(8,128)(2,1)}, u32[]{:S(2)}, u32[]{:S(2)}) collective-permute-start(bf16[8,128,256]{2,1,0:T(8,128)(2,1)} %bitcast.11), channel_id=1, source_target_pairs={{0,1},{1,0},{2,3},{3,2},{4,5},{5,4},{6,7},{7,6},{8,9},{9,8},{10,11... | collective-permute-start | bytes 1572872 | tf_op jit(solution)/shard_map/ppermute | solution.py:307
  12.2 10.5 %collective-permute-start.3 = (bf16[32,3456]{1,0:T(8,128)(2,1)S(1)}, bf16[32,3456]{1,0:T(8,128)(2,1)S(1)}, u32[]{:S(2)}, u32[]{:S(2)}) collective-permute-start(bf16[32,3456]{1,0:T(8,128)(2,1)S(1)} %join1.4.refs_2_.refs_0_), channel_id=1, source_target_pairs={{0,4},{2,6},{4,0},{6,2},{8,12},{10,14},{12,8},{14,10},{16,20},{18,... | collective-permute-start | bytes 663560 | tf_op jit(solution)/shard_map/ppermute | solution.py:307
  13.8 6.0 %collective-permute-start.2 = (bf16[32,3456]{1,0:T(8,128)(2,1)S(1)}, bf16[32,3456]{1,0:T(8,128)(2,1)S(1)}, u32[]{:S(2)}, u32[]{:S(2)}) collective-permute-start(bf16[32,3456]{1,0:T(8,128)(2,1)S(1)} %join1.4.refs_2_.refs_0_), channel_id=1, source_target_pairs={{0,8},{2,10},{4,12},{6,14},{8,0},{10,2},{12,4},{14,6},{16,24},{18,... | collective-permute-start | bytes 663560 | tf_op jit(solution)/shard_map/ppermute | solution.py:307
  14.5 1.0 copy-start.14
  15.5 7.2 %copy-start.21 = (bf16[1,8,8,16,256]{4,3,2,1,0:T(8,128)(2,1)S(1)}, bf16[1,8,8,16,256]{4,3,2,1,0:T(8,128)(2,1)}, u32[]{:S(2)}) copy-start(bf16[1,8,8,16,256]{4,3,2,1,0:T(8,128)(2,1)} %param.6) | copy-start | bytes 1572868
  16.1 10.6 %collective-permute-start.6 = (bf16[8,6912]{1,0:T(8,128)(2,1)S(1)}, bf16[8,6912]{1,0:T(8,128)(2,1)S(1)}, u32[]{:S(2)}, u32[]{:S(2)}) collective-permute-start(bf16[8,6912]{1,0:T(8,128)(2,1)S(1)} %second_rows.1.refs_3_.refs_0_), channel_id=1, source_target_pairs={{0,16},{2,18},{4,20},{6,22},{8,24},{10,26},{12,28},{14,30},{16,0},... | collective-permute-start | bytes 331784 | tf_op jit(solution)/shard_map/ppermute | solution.py:307
  19.8 6.7 %collective-permute-start.4 = (bf16[32,3456]{1,0:T(8,128)(2,1)S(1)}, bf16[32,3456]{1,0:T(8,128)(2,1)S(1)}, u32[]{:S(2)}, u32[]{:S(2)}) collective-permute-start(bf16[32,3456]{1,0:T(8,128)(2,1)S(1)} %collective-permute-done.2.refs_1_), channel_id=1, source_target_pairs={{0,4},{2,6},{4,0},{6,2},{8,12},{10,14},{12,8},{14,10},{16,20},{18,... | collective-permute-start | bytes 663560 | tf_op jit(solution)/shard_map/ppermute | solution.py:307
  22.7 1.8 %copy-start.9 = (f32[16,6912]{1,0:T(8,128)S(1)}, f32[16,6912]{1,0:T(8,128)}, u32[]{:S(2)}) copy-start(f32[16,6912]{1,0:T(8,128)} %refs_0_.2) | copy-start | bytes 1327108
  22.7 1.8 %copy-start.13 = (f32[16,6912]{1,0:T(8,128)S(1)}, f32[16,6912]{1,0:T(8,128)}, u32[]{:S(2)}) copy-start(f32[16,6912]{1,0:T(8,128)} %refs_1_.6) | copy-start | bytes 1327108
  24.4 2.2 %copy-start.2 = (bf16[256,2048]{1,0:T(8,128)(2,1)}, bf16[256,2048]{1,0:T(8,128)(2,1)S(1)}, u32[]{:S(2)}) copy-start(bf16[256,2048]{1,0:T(8,128)(2,1)S(1)} %get-tuple-element.26.refs_2_.refs_0_) | copy-start | bytes 3145732
  24.5 2.2 %copy-start.4 = (f32[16,6912]{1,0:T(8,128)}, f32[16,6912]{1,0:T(8,128)S(1)}, u32[]{:S(2)}) copy-start(f32[16,6912]{1,0:T(8,128)S(1)} %base1.1.refs_2_.refs_3_) | copy-start | bytes 1327108
  26.6 2.5 %collective-permute-start.5 = (bf16[128,3456]{1,0:T(8,128)(2,1)S(1)}, bf16[128,3456]{1,0:T(8,128)(2,1)S(1)}, u32[]{:S(2)}, u32[]{:S(2)}) collective-permute-start(bf16[128,3456]{1,0:T(8,128)(2,1)S(1)} %join1.6.refs_2_.refs_1_), channel_id=1, source_target_pairs={{0,2},{2,0},{4,6},{6,4},{8,10},{10,8},{12,14},{14,12},{16,18},{18,... | collective-permute-start | bytes 2654216 | tf_op jit(solution)/shard_map/ppermute | solution.py:307
  26.7 12.3 %collective-permute-start.8 = (bf16[16,6912]{1,0:T(8,128)(2,1)S(1)}, bf16[16,6912]{1,0:T(8,128)(2,1)S(1)}, u32[]{:S(2)}, u32[]{:S(2)}) collective-permute-start(bf16[16,6912]{1,0:T(8,128)(2,1)S(1)} %join2.6.refs_3_.refs_0_), channel_id=1, source_target_pairs={{0,4},{2,6},{4,0},{6,2},{8,12},{10,14},{12,8},{14,10},{16,20},{18,... | collective-permute-start | bytes 663560 | tf_op jit(solution)/shard_map/ppermute | solution.py:307
  28.8 8.1 %collective-permute-start.7 = (bf16[16,6912]{1,0:T(8,128)(2,1)S(1)}, bf16[16,6912]{1,0:T(8,128)(2,1)S(1)}, u32[]{:S(2)}, u32[]{:S(2)}) collective-permute-start(bf16[16,6912]{1,0:T(8,128)(2,1)S(1)} %join2.6.refs_3_.refs_0_), channel_id=1, source_target_pairs={{0,8},{2,10},{4,12},{6,14},{8,0},{10,2},{12,4},{14,6},{16,24},{18,... | collective-permute-start | bytes 663560 | tf_op jit(solution)/shard_map/ppermute | solution.py:307
  29.8 7.1 %copy-start.11 = (bf16[256,3456]{1,0:T(8,128)(2,1)}, bf16[256,3456]{1,0:T(8,128)(2,1)S(1)}, u32[]{:S(2)}) copy-start(bf16[256,3456]{1,0:T(8,128)(2,1)S(1)} %place1.1.refs_2_) | copy-start | bytes 5308420
  36.9 2.2 %copy-start.23 = (bf16[1,8,8,16,256]{4,3,2,1,0:T(8,128)(2,1)S(1)}, bf16[1,8,8,16,256]{4,3,2,1,0:T(8,128)(2,1)}, u32[]{:S(2)}) copy-start(bf16[1,8,8,16,256]{4,3,2,1,0:T(8,128)(2,1)} %param.7) | copy-start | bytes 1572868
  36.9 8.6 %collective-permute-start.9 = (bf16[16,6912]{1,0:T(8,128)(2,1)S(1)}, bf16[16,6912]{1,0:T(8,128)(2,1)S(1)}, u32[]{:S(2)}, u32[]{:S(2)}) collective-permute-start(bf16[16,6912]{1,0:T(8,128)(2,1)S(1)} %join2.8), channel_id=1, source_target_pairs={{0,4},{2,6},{4,0},{6,2},{8,12},{10,14},{12,8},{14,10},{16,20},{18,... | collective-permute-start | bytes 663560 | tf_op jit(solution)/shard_map/ppermute | solution.py:307
  41.0 4.4 %copy-start = (bf16[3,18,160,256]{3,2,1,0:T(8,128)(2,1)}, bf16[3,18,160,256]{3,2,1,0:T(8,128)(2,1)S(1)}, u32[]{:S(2)}) copy-start(bf16[3,18,160,256]{3,2,1,0:T(8,128)(2,1)S(1)} %spread_cotangent.1.refs_1_) | copy-start | bytes 13271044
  45.4 2.5 %collective-permute-start.12 = (bf16[64,6912]{1,0:T(8,128)(2,1)S(1)}, bf16[64,6912]{1,0:T(8,128)(2,1)S(1)}, u32[]{:S(2)}, u32[]{:S(2)}) collective-permute-start(bf16[64,6912]{1,0:T(8,128)(2,1)S(1)} %get-tuple-element.31), channel_id=1, source_target_pairs={{0,2},{2,0},{4,6},{6,4},{8,10},{10,8},{12,14},{14,12},{16,18},{18,... | collective-permute-start | bytes 2654216 | tf_op jit(solution)/shard_map/ppermute | solution.py:307
  45.6 3.6 %collective-permute-start.11 = (bf16[64,6912]{1,0:T(8,128)(2,1)S(1)}, bf16[64,6912]{1,0:T(8,128)(2,1)S(1)}, u32[]{:S(2)}, u32[]{:S(2)}) collective-permute-start(bf16[64,6912]{1,0:T(8,128)(2,1)S(1)} %join2.9.refs_2_.refs_0_), channel_id=1, source_target_pairs={{0,2},{2,0},{4,6},{6,4},{8,10},{10,8},{12,14},{14,12},{16,18},{18,... | collective-permute-start | bytes 2654216 | tf_op jit(solution)/shard_map/ppermute | solution.py:307
  47.9 2.3 %copy-start.1 = (bf16[3,18,160,256]{3,2,1,0:T(8,128)(2,1)S(1)}, bf16[3,18,160,256]{3,2,1,0:T(8,128)(2,1)}, u32[]{:S(2)}) copy-start(bf16[3,18,160,256]{3,2,1,0:T(8,128)(2,1)} %copy-done) | copy-start | bytes 13271044
  48.1 9.9 %collective-permute-start.13 = (bf16[16,6912]{1,0:T(8,128)(2,1)S(1)}, bf16[16,6912]{1,0:T(8,128)(2,1)S(1)}, u32[]{:S(2)}, u32[]{:S(2)}) collective-permute-start(bf16[16,6912]{1,0:T(8,128)(2,1)S(1)} %get-tuple-element.34), channel_id=1, source_target_pairs={{0,4},{2,6},{4,0},{6,2},{8,12},{10,14},{12,8},{14,10},{16,20},{18,... | collective-permute-start | bytes 663560 | tf_op jit(solution)/shard_map/ppermute | solution.py:307
  49.3 0.7 copy-start.19
  57.1 10.4 %collective-permute-start.16 = (bf16[16,6912]{1,0:T(8,128)(2,1)S(1)}, bf16[16,6912]{1,0:T(8,128)(2,1)S(1)}, u32[]{:S(2)}, u32[]{:S(2)}) collective-permute-start(bf16[16,6912]{1,0:T(8,128)(2,1)S(1)} %join2.11), channel_id=1, source_target_pairs={{0,4},{2,6},{4,0},{6,2},{8,12},{10,14},{12,8},{14,10},{16,20},{18,... | collective-permute-start | bytes 663560 | tf_op jit(solution)/shard_map/ppermute | solution.py:307
  58.1 9.4 %collective-permute-start.15 = (bf16[16,6912]{1,0:T(8,128)(2,1)S(1)}, bf16[16,6912]{1,0:T(8,128)(2,1)S(1)}, u32[]{:S(2)}, u32[]{:S(2)}) collective-permute-start(bf16[16,6912]{1,0:T(8,128)(2,1)S(1)} %fold2.5.refs_3_), channel_id=1, source_target_pairs={{0,8},{2,10},{4,12},{6,14},{8,0},{10,2},{12,4},{14,6},{16,24},{18,... | collective-permute-start | bytes 663560 | tf_op jit(solution)/shard_map/ppermute | solution.py:307
  59.1 4.3 %copy-start.3 = (bf16[256,2048]{1,0:T(8,128)(2,1)S(1)}, bf16[256,2048]{1,0:T(8,128)(2,1)}, u32[]{:S(2)}) copy-start(bf16[256,2048]{1,0:T(8,128)(2,1)} %copy-done.2) | copy-start | bytes 3145732
  62.5 5.0 %copy-start.20 = (bf16[16,6912]{1,0:T(8,128)(2,1)S(1)}, bf16[16,6912]{1,0:T(8,128)(2,1)}, u32[]{:S(2)}) copy-start(bf16[16,6912]{1,0:T(8,128)(2,1)} %copy-done.19) | copy-start | bytes 663556
  62.5 31.6 %collective-permute-start.18 = (bf16[8,128,256]{2,1,0:T(8,128)(2,1)}, bf16[8,128,256]{2,1,0:T(8,128)(2,1)}, u32[]{:S(2)}, u32[]{:S(2)}) collective-permute-start(bf16[8,128,256]{2,1,0:T(8,128)(2,1)} %outputs_send.1.refs_2_), channel_id=1, source_target_pairs={{0,1},{1,0},{2,3},{3,2},{4,5},{5,4},{6,7},{7,6},{8,9},{9,8},{10,11... | collective-permute-start | bytes 1572872 | tf_op jit(solution)/shard_map/ppermute | solution.py:307
  67.4 5.8 %collective-permute-start.14 = (bf16[128,3456]{1,0:T(8,128)(2,1)S(1)}, bf16[128,3456]{1,0:T(8,128)(2,1)S(1)}, u32[]{:S(2)}, u32[]{:S(2)}) collective-permute-start(bf16[128,3456]{1,0:T(8,128)(2,1)S(1)} %get-tuple-element.36), channel_id=1, source_target_pairs={{0,2},{2,0},{4,6},{6,4},{8,10},{10,8},{12,14},{14,12},{16,18},{18,... | collective-permute-start | bytes 2654216 | tf_op jit(solution)/shard_map/ppermute | solution.py:307
  67.5 6.8 %copy-start.12 = (bf16[256,3456]{1,0:T(8,128)(2,1)S(1)}, bf16[256,3456]{1,0:T(8,128)(2,1)}, u32[]{:S(2)}) copy-start(bf16[256,3456]{1,0:T(8,128)(2,1)} %copy-done.11) | copy-start | bytes 5308420
  68.4 5.9 %copy-start.17 = (bf16[8,6912]{1,0:T(8,128)(2,1)}, bf16[8,6912]{1,0:T(8,128)(2,1)S(1)}, u32[]{:S(2)}) copy-start(bf16[8,6912]{1,0:T(8,128)(2,1)S(1)} %get-tuple-element.38.refs_2_.refs_0_) | copy-start | bytes 331780
  68.4 24.0 %collective-permute-start.19 = (bf16[8,6912]{1,0:T(8,128)(2,1)}, bf16[8,6912]{1,0:T(8,128)(2,1)}, u32[]{:S(2)}, u32[]{:S(2)}) collective-permute-start(bf16[8,6912]{1,0:T(8,128)(2,1)} %get-tuple-element.42), channel_id=1, source_target_pairs={{0,16},{2,18},{4,20},{6,22},{8,24},{10,26},{12,28},{14,30},{16,0},... | collective-permute-start | bytes 331784 | tf_op jit(solution)/shard_map/ppermute | solution.py:307
  73.4 7.6 %collective-permute-start.17 = (bf16[32,3456]{1,0:T(8,128)(2,1)S(1)}, bf16[32,3456]{1,0:T(8,128)(2,1)S(1)}, u32[]{:S(2)}, u32[]{:S(2)}) collective-permute-start(bf16[32,3456]{1,0:T(8,128)(2,1)S(1)} %get-tuple-element.40), channel_id=1, source_target_pairs={{0,4},{2,6},{4,0},{6,2},{8,12},{10,14},{12,8},{14,10},{16,20},{18,... | collective-permute-start | bytes 663560 | tf_op jit(solution)/shard_map/ppermute | solution.py:307
  74.3 8.6 %copy-start.22 = (bf16[1,8,8,16,256]{4,3,2,1,0:T(8,128)(2,1)S(1)}, bf16[1,8,8,16,256]{4,3,2,1,0:T(8,128)(2,1)}, u32[]{:S(2)}) copy-start(bf16[1,8,8,16,256]{4,3,2,1,0:T(8,128)(2,1)} %param.6) | copy-start | bytes 1572868
  77.0 19.1 %collective-permute-start.22 = (bf16[8,128,256]{2,1,0:T(8,128)(2,1)S(1)}, bf16[8,128,256]{2,1,0:T(8,128)(2,1)S(1)}, u32[]{:S(2)}, u32[]{:S(2)}) collective-permute-start(bf16[8,128,256]{2,1,0:T(8,128)(2,1)S(1)} %input_grads_send.1.refs_2_), channel_id=1, source_target_pairs={{0,1},{1,0},{2,3},{3,2},{4,5},{5,4},{6,7},{7,6},{8,9},{9,8},{10,11... | collective-permute-start | bytes 1572872 | tf_op jit(solution)/shard_map/ppermute | solution.py:307
  81.0 7.2 %collective-permute-start.20 = (bf16[32,3456]{1,0:T(8,128)(2,1)S(1)}, bf16[32,3456]{1,0:T(8,128)(2,1)S(1)}, u32[]{:S(2)}, u32[]{:S(2)}) collective-permute-start(bf16[32,3456]{1,0:T(8,128)(2,1)S(1)} %fold1.5.refs_4_.refs_1_), channel_id=1, source_target_pairs={{0,8},{2,10},{4,12},{6,14},{8,0},{10,2},{12,4},{14,6},{16,24},{18,... | collective-permute-start | bytes 663560 | tf_op jit(solution)/shard_map/ppermute | solution.py:307
  81.7 8.1 %copy-start.24 = (bf16[1,8,8,16,256]{4,3,2,1,0:T(8,128)(2,1)S(1)}, bf16[1,8,8,16,256]{4,3,2,1,0:T(8,128)(2,1)}, u32[]{:S(2)}) copy-start(bf16[1,8,8,16,256]{4,3,2,1,0:T(8,128)(2,1)} %param.7) | copy-start | bytes 1572868
  81.7 6.5 %collective-permute-start.21 = (bf16[32,3456]{1,0:T(8,128)(2,1)S(1)}, bf16[32,3456]{1,0:T(8,128)(2,1)S(1)}, u32[]{:S(2)}, u32[]{:S(2)}) collective-permute-start(bf16[32,3456]{1,0:T(8,128)(2,1)S(1)} %join1.7), channel_id=1, source_target_pairs={{0,4},{2,6},{4,0},{6,2},{8,12},{10,14},{12,8},{14,10},{16,20},{18,... | collective-permute-start | bytes 663560 | tf_op jit(solution)/shard_map/ppermute | solution.py:307
  88.3 9.7 %collective-permute-start.23 = (bf16[16,3456]{1,0:T(8,128)(2,1)S(1)}, bf16[16,3456]{1,0:T(8,128)(2,1)S(1)}, u32[]{:S(2)}, u32[]{:S(2)}) collective-permute-start(bf16[16,3456]{1,0:T(8,128)(2,1)S(1)} %get-tuple-element.45), channel_id=1, source_target_pairs={{0,16},{2,18},{4,20},{6,22},{8,24},{10,26},{12,28},{14,30},{16,0},... | collective-permute-start | bytes 331784 | tf_op jit(solution)/shard_map/ppermute | solution.py:307
  89.8 2.7 %copy-start.18 = (bf16[8,6912]{1,0:T(8,128)(2,1)S(1)}, bf16[8,6912]{1,0:T(8,128)(2,1)}, u32[]{:S(2)}) copy-start(bf16[8,6912]{1,0:T(8,128)(2,1)} %copy-done.17) | copy-start | bytes 331780
  89.8 4.2 %copy-start.15 = (f32[16,6912]{1,0:T(8,128)S(1)}, f32[16,6912]{1,0:T(8,128)}, u32[]{:S(2)}) copy-start(f32[16,6912]{1,0:T(8,128)} %refs_0_.3) | copy-start | bytes 1327108
  89.8 4.2 %copy-start.16 = (f32[16,6912]{1,0:T(8,128)S(1)}, f32[16,6912]{1,0:T(8,128)}, u32[]{:S(2)}) copy-start(f32[16,6912]{1,0:T(8,128)} %refs_1_.7) | copy-start | bytes 1327108
  93.4 7.3 %collective-permute-start.25 = (bf16[8,6912]{1,0:T(8,128)(2,1)S(1)}, bf16[8,6912]{1,0:T(8,128)(2,1)S(1)}, u32[]{:S(2)}, u32[]{:S(2)}) collective-permute-start(bf16[8,6912]{1,0:T(8,128)(2,1)S(1)} %fold2.7.refs_2_.refs_1_), channel_id=1, source_target_pairs={{0,1},{1,0},{2,3},{3,2},{4,5},{5,4},{6,7},{7,6},{8,9},{9,8},{10,11... | collective-permute-start | bytes 331784 | tf_op jit(solution)/shard_map/ppermute | solution.py:307
  96.0 7.9 %copy-start.5 = (f32[16,6912]{1,0:T(8,128)S(1)}, f32[16,6912]{1,0:T(8,128)}, u32[]{:S(2)}) copy-start(f32[16,6912]{1,0:T(8,128)} %copy-done.4) | copy-start | bytes 1327108
  96.0 1.1 %copy-start.6 = (bf16[8,128,256]{2,1,0:T(8,128)(2,1)S(1)}, bf16[8,128,256]{2,1,0:T(8,128)(2,1)}, u32[]{:S(2)}) copy-start(bf16[8,128,256]{2,1,0:T(8,128)(2,1)} %finish.2.refs_2_) | copy-start | bytes 1572868
  98.0 1.0 copy-start.7
  99.1 4.8 %collective-permute-start.24 = (bf16[16,3456]{1,0:T(8,128)(2,1)S(1)}, bf16[16,3456]{1,0:T(8,128)(2,1)S(1)}, u32[]{:S(2)}, u32[]{:S(2)}) collective-permute-start(bf16[16,3456]{1,0:T(8,128)(2,1)S(1)} %fold1.7.refs_4_.refs_1_), channel_id=1, source_target_pairs={{0,1},{1,0},{2,3},{3,2},{4,5},{5,4},{6,7},{7,6},{8,9},{9,8},{10,11... | collective-permute-start | bytes 331784 | tf_op jit(solution)/shard_map/ppermute | solution.py:307
  103.9 1.0 copy-start.10

commit v3 on v2

--- a/solution.py
+++ b/solution.py
@@ -485,20 +485,20 @@
     (q23,) = fold((q23, trade(q67, "dp", near)), "fold2", after=(g3,))
     line2, near2 = trade(q23, "dp", line), trade(join((q45,), "join2", after=(g3,)), "dp", near)
     part, whole = shape((slab, area, channels), BF), shape((slab, area, channels), F32)
-    (send_out,) = run(
-        functools.partial(outputs_kernel, dims, False), (idx, a3, w2), (part,), "outputs_send", ALL, after=(q23,)
-    )
-    came_out = trade(send_out, "space", 1)
     keep1, send1 = run(
         functools.partial(first_grad_kernel, dims),
         (xt, g3),
         (shape((channels // 2, 27 * hid), BF),) * 2,
         "first_grad",
-        NONE,
+        ALL,
         scalars=0,
-        after=(send_out,),
-    )
-    q0, q1 = fold((q01, line2, near2), "fold2", split=2, after=(keep1,), cost=ALL)
+        after=(q23,),
+    )
+    (send_out,) = run(
+        functools.partial(outputs_kernel, dims, False), (idx, a3, w2), (part,), "outputs_send", ALL, after=(keep1,)
+    )
+    came_out = trade(send_out, "space", 1)
+    q0, q1 = fold((q01, line2, near2), "fold2", split=2, after=(send_out,))
     p01, p23, p45, p67 = fold((keep1, trade(send1, "dp", core)), "fold1", split=4, after=(q0,))
     near1 = trade(p67, "dp", near)
     (send_in,) = run(
@@ -507,7 +507,7 @@
     came_in = trade(send_in, "space", 1)
     (p23,) = fold((p23, near1), "fold1", after=(send_in,))
     line1, near1 = trade(p23, "dp", line), trade(join((p45,), "join1", after=(p23,)), "dp", near)
-    far2 = trade(q1, "dp", far)
+    far2 = trade(join((q1,), "join2", after=(p01,)), "dp", far)
     (own_out,) = run(
         functools.partial(outputs_kernel, dims, True), (idx, a3, w2, volume), (whole,), "outputs", ALL, after=(p23,)
     )

time: 107 us -> 107 us (level)
  waiting for transfers between devices: 15.9 us -> 14.4 us
    ppermute x26, waiting for transfers between devices: 15.9 us -> 14.4 us  [trade(): return lax.ppermute(array, axis, [(i, i ^ bit) for i in range(size)])]
    pallas_call x37 -> x38, Pallas kernels: 48.2 us -> 49.1 us  [run(): pl.pallas_call(entry, out_shape=tuple(outs), in_specs=[smem] * scalars +...]
  transfers between devices with their start and end apart: 26 -> 26, of which waited for: 9 -> 9; matrix products, arithmetic and copies ran while one was open for 0% -> 0% of each run, Pallas kernels for 43% -> 44%
where the time goes in v3:
time: 107 us; the launch traced here: 106 us
  Pallas kernels  49.1 us (46%)
  starting transfers between devices  35.4 us (33%)
  waiting for transfers between devices  14.4 us (13%)
  local copies, waits for them, and re-layouts  6.13 us (6%)
  between operations  1.13 us (1%)
    pallas_call x38, Pallas kernels, run(): pl.pallas_call(entry, out_shape=tuple(outs), in_specs=[smem] * scalars +...  49.1 us
    ppermute x26, starting transfers between devices, trade(): return lax.ppermute(array, axis, [(i, i ^ bit) for i in range(size)])  35.4 us
    ppermute x26, waiting for transfers between devices, trade(): return lax.ppermute(array, axis, [(i, i ^ bit) for i in range(size)])  14.4 us
    unnamed x50, local copies, waits for them, and re-layouts  6.13 us
  transfers between devices with their start and end apart: 26, of which 9 were waited for; matrix products, arithmetic and copies ran while one was open for 0% of the time, Pallas kernels for 44%

profile of v3, /device:TPU:0, one launch (start us, length us, event | category | flops | bytes accessed | tf_op | source)
XLA Modules:
  0.0 106.2 jit_solution(16688610429876086571)
XLA Ops:
  0.6 0.1 pad_add_fusion.refs_0_
  0.7 1.0 copy-done.6
  1.7 0.9 first_columns.1.refs_0_
  2.6 4.1 %collective-permute-start.1 = (bf16[16,3456]{1,0:T(8,128)(2,1)S(1)}, bf16[16,3456]{1,0:T(8,128)(2,1)S(1)}, u32[]{:S(2)}, u32[]{:S(2)}) collective-permute-start(bf16[16,3456]{1,0:T(8,128)(2,1)S(1)} %first_columns.1.refs_0_), channel_id=1, source_target_pairs={{0,16},{2,18},{4,20},{6,22},{8,24},{10,26},{12,28},{14,30},{16,0},... | collective-permute-start | bytes 331784 | tf_op jit(solution)/shard_map/ppermute | solution.py:307
  6.7 1.5 %collective-permute-start = (bf16[8,128,256]{2,1,0:T(8,128)(2,1)}, bf16[8,128,256]{2,1,0:T(8,128)(2,1)S(1)}, u32[]{:S(2)}, u32[]{:S(2)}) collective-permute-start(bf16[8,128,256]{2,1,0:T(8,128)(2,1)} %bitcast.8), channel_id=1, source_target_pairs={{0,1},{1,0},{2,3},{3,2},{4,5},{5,4},{6,7},{7,6},{8,9},{9,8},{10,11... | collective-permute-start | bytes 1572872 | tf_op jit(solution)/shard_map/ppermute | solution.py:307
  8.2 0.5 collective-permute-start.10
  8.7 3.4 %collective-permute-done.1.refs_1_ = bf16[16,3456]{1,0:T(8,128)(2,1)S(1)} collective-permute-done((bf16[16,3456]{1,0:T(8,128)(2,1)S(1)}, bf16[16,3456]{1,0:T(8,128)(2,1)S(1)}, u32[]{:S(2)}, u32[]{:S(2)}) %collective-permute-start.1) | collective-permute-done | bytes 110624 | tf_op jit(solution)/shard_map/ppermute | solution.py:307
  12.2 1.6 %collective-permute-start.3 = (bf16[32,3456]{1,0:T(8,128)(2,1)S(1)}, bf16[32,3456]{1,0:T(8,128)(2,1)S(1)}, u32[]{:S(2)}, u32[]{:S(2)}) collective-permute-start(bf16[32,3456]{1,0:T(8,128)(2,1)S(1)} %join1.4.refs_2_.refs_0_), channel_id=1, source_target_pairs={{0,4},{2,6},{4,0},{6,2},{8,12},{10,14},{12,8},{14,10},{16,20},{18,... | collective-permute-start | bytes 663560 | tf_op jit(solution)/shard_map/ppermute | solution.py:307
  13.8 0.7 collective-permute-start.2
  14.5 1.0 copy-done.16
  15.5 0.6 second_rows.1.refs_3_.refs_0_
  16.1 3.4 %collective-permute-start.6 = (bf16[8,6912]{1,0:T(8,128)(2,1)S(1)}, bf16[8,6912]{1,0:T(8,128)(2,1)S(1)}, u32[]{:S(2)}, u32[]{:S(2)}) collective-permute-start(bf16[8,6912]{1,0:T(8,128)(2,1)S(1)} %second_rows.1.refs_3_.refs_0_), channel_id=1, source_target_pairs={{0,16},{2,18},{4,20},{6,22},{8,24},{10,26},{12,28},{14,30},{16,0},... | collective-permute-start | bytes 331784 | tf_op jit(solution)/shard_map/ppermute | solution.py:307
  19.5 0.3 collective-permute-done.2.refs_1_
  19.8 2.8 %collective-permute-start.4 = (bf16[32,3456]{1,0:T(8,128)(2,1)S(1)}, bf16[32,3456]{1,0:T(8,128)(2,1)S(1)}, u32[]{:S(2)}, u32[]{:S(2)}) collective-permute-start(bf16[32,3456]{1,0:T(8,128)(2,1)S(1)} %collective-permute-done.2.refs_1_), channel_id=1, source_target_pairs={{0,4},{2,6},{4,0},{6,2},{8,12},{10,14},{12,8},{14,10},{16,20},{18,... | collective-permute-start | bytes 663560 | tf_op jit(solution)/shard_map/ppermute | solution.py:307
  22.7 1.7 %spread_volumes.1 = (bf16[3,18,160,256]{3,2,1,0:T(8,128)(2,1)S(1)}, bf16[256,2048]{1,0:T(8,128)(2,1)S(1)}) custom-call(s32[2]{0:T(128)S(1)} %pad_add_fusion.refs_0_, bf16[8,128,256]{2,1,0:T(8,128)(2,1)S(1)} %bitcast.9, bf16[8,128,256]{2,1,0:T(8,128)(2,1)S(1)} %collective-permute-done.refs_2_, bf16[96,3456]{1,0:T(8,128)(2,1)S(1)} %join1.5.refs_3_.refs_0_), custom_call_target="tpu_custom_call" | custom-call | flops 99999997952 | bytes 1 | tf_op jit(solution)/shard_map/spread_volumes/pallas_call | solution.py:293
  24.5 2.0 %collective-permute-done.4.refs_1_ = bf16[32,3456]{1,0:T(8,128)(2,1)S(1)} collective-permute-done((bf16[32,3456]{1,0:T(8,128)(2,1)S(1)}, bf16[32,3456]{1,0:T(8,128)(2,1)S(1)}, u32[]{:S(2)}, u32[]{:S(2)}) %collective-permute-start.4) | collective-permute-done | bytes 221216 | tf_op jit(solution)/shard_map/ppermute | solution.py:307
  26.6 0.1 collective-permute-start.5
  26.7 2.1 %collective-permute-start.8 = (bf16[16,6912]{1,0:T(8,128)(2,1)S(1)}, bf16[16,6912]{1,0:T(8,128)(2,1)S(1)}, u32[]{:S(2)}, u32[]{:S(2)}) collective-permute-start(bf16[16,6912]{1,0:T(8,128)(2,1)S(1)} %join2.7.refs_3_.refs_0_), channel_id=1, source_target_pairs={{0,4},{2,6},{4,0},{6,2},{8,12},{10,14},{12,8},{14,10},{16,20},{18,... | collective-permute-start | bytes 663560 | tf_op jit(solution)/shard_map/ppermute | solution.py:307
  28.8 0.3 collective-permute-done.5.refs_2_
  29.1 0.7 place1.1.refs_2_
  29.8 7.1 %hidden.1 = (bf16[3,18,160,128]{3,2,1,0:T(8,128)(2,1)S(1)}, bf16[128,2048]{1,0:T(8,128)(2,1)S(1)}, bf16[16,128,128]{2,1,0:T(8,128)(2,1)S(1)}) custom-call(s32[2]{0:T(128)S(1)} %pad_add_fusion.refs_0_, bf16[3,18,160,256]{3,2,1,0:T(8,128)(2,1)S(1)} %get-tuple-element.25.refs_1_, bf16[256,3456]{1,0:T(8,128)(2,1)S(1)} %place1.1.refs_2_), custom_call_target="tpu_custom_call" | custom-call | flops 10000000000 | bytes 1 | tf_op jit(solution)/shard_map/hidden/pallas_call | solution.py:293
  36.9 2.1 %collective-permute-start.9 = (bf16[16,6912]{1,0:T(8,128)(2,1)S(1)}, bf16[16,6912]{1,0:T(8,128)(2,1)S(1)}, u32[]{:S(2)}, u32[]{:S(2)}) collective-permute-start(bf16[16,6912]{1,0:T(8,128)(2,1)S(1)} %join2.9), channel_id=1, source_target_pairs={{0,4},{2,6},{4,0},{6,2},{8,12},{10,14},{12,8},{14,10},{16,20},{18,... | collective-permute-start | bytes 663560 | tf_op jit(solution)/shard_map/ppermute | solution.py:307
  39.1 1.9 %spread_cotangent.1.refs_1_ = bf16[3,18,160,256]{3,2,1,0:T(8,128)(2,1)S(1)} custom-call(s32[2]{0:T(128)S(1)} %pad_add_fusion.refs_0_, bf16[8,128,256]{2,1,0:T(8,128)(2,1)S(1)} %bitcast.12, bf16[8,128,256]{2,1,0:T(8,128)(2,1)} %collective-permute-done.10.refs_2_, bf16[48,6912]{1,0:T(8,128)(2,1)S(1)} %join2.8.refs_3_.refs_0_), custom_call_target="tpu_custom_call" | custom-call | flops 99999997952 | bytes 1 | tf_op jit(solution)/shard_map/spread_cotangent/pallas_call | solution.py:293
  41.0 4.4 %second_grad.1 = (bf16[64,6912]{1,0:T(8,128)(2,1)S(1)}, bf16[64,6912]{1,0:T(8,128)(2,1)S(1)}) custom-call(bf16[128,2048]{1,0:T(8,128)(2,1)S(1)} %get-tuple-element.29.refs_0_, bf16[3,18,160,256]{3,2,1,0:T(8,128)(2,1)S(1)} %spread_cotangent.1.refs_1_), custom_call_target="tpu_custom_call" | custom-call | flops 1 | bytes 1 | tf_op jit(solution)/shard_map/second_grad/pallas_call | solution.py:293
  45.6 0.5 collective-permute-start.11
  46.1 1.8 %collective-permute-done.12.refs_1_ = bf16[64,6912]{1,0:T(8,128)(2,1)S(1)} collective-permute-done((bf16[64,6912]{1,0:T(8,128)(2,1)S(1)}, bf16[64,6912]{1,0:T(8,128)(2,1)S(1)}, u32[]{:S(2)}, u32[]{:S(2)}) %collective-permute-start.12) | collective-permute-done | bytes 884768 | tf_op jit(solution)/shard_map/ppermute | solution.py:307
  47.9 0.2 fold2.4
  48.1 0.9 collective-permute-start.13
  49.0 0.1 collective-permute-done.11.refs_1_
  49.2 0.1 join2.11.refs_2_
  49.3 0.7 copy-done.13
  50.0 0.2 copy-done.1
  50.2 6.9 %hidden_grad.1.refs_2_.refs_1_ = bf16[3,18,160,128]{3,2,1,0:T(8,128)(2,1)S(1)} custom-call(s32[2]{0:T(128)S(1)} %pad_add_fusion.refs_0_, bf16[3,18,160,256]{3,2,1,0:T(8,128)(2,1)S(1)} %copy-done.1, bf16[128,6912]{1,0:T(8,128)(2,1)S(1)} %join2.11.refs_2_, bf16[16,128,128]{2,1,0:T(8,128)(2,1)S(1)} %get-tuple-element.28.refs_3_.refs_1_), custom_call_target="tpu_custom_call" | custom-call | flops 99999997952 | bytes 1 | tf_op jit(solution)/shard_map/hidden_grad/pallas_call | solution.py:293
  57.1 0.7 join2.12
  57.8 0.9 collective-permute-start.16
  58.7 0.7 fold2.5.refs_2_
  59.4 0.9 collective-permute-start.15
  60.3 4.0 %first_grad.1 = (bf16[128,3456]{1,0:T(8,128)(2,1)S(1)}, bf16[128,3456]{1,0:T(8,128)(2,1)S(1)}) custom-call(bf16[256,2048]{1,0:T(8,128)(2,1)S(1)} %copy-done.12, bf16[3,18,160,128]{3,2,1,0:T(8,128)(2,1)S(1)} %hidden_grad.1.refs_2_.refs_1_, bf16[16,6912]{1,0:T(8,128)(2,1)} %fold2.5.refs_2_), custom_call_target="tpu_custom_call" | custom-call | flops 99999997952 | bytes 1 | tf_op jit(solution)/shard_map/first_grad/pallas_call | solution.py:293
  64.4 3.4 %outputs_send.1.refs_3_ = bf16[8,128,256]{2,1,0:T(8,128)(2,1)} custom-call(s32[2]{0:T(128)S(1)} %pad_add_fusion.refs_0_, bf16[3,18,160,128]{3,2,1,0:T(8,128)(2,1)S(1)} %get-tuple-element.27.refs_1_, bf16[128,6912]{1,0:T(8,128)(2,1)S(1)} %join2.11.refs_2_, bf16[128,3456]{1,0:T(8,128)(2,1)S(1)} %get-tuple-element.35.refs_3_.refs_0_), custom_call_target="tpu_custom_call" | custom-call | flops 99999997952 | bytes 1 | tf_op jit(solution)/shard_map/outputs_send/pallas_call | solution.py:293
  67.8 0.9 collective-permute-start.18
  68.8 1.3 %fold2.6 = (bf16[8,6912]{1,0:T(8,128)(2,1)S(1)}, bf16[8,6912]{1,0:T(8,128)(2,1)S(1)}) custom-call(bf16[16,6912]{1,0:T(8,128)(2,1)S(1)} %copy-done.14, bf16[16,6912]{1,0:T(8,128)(2,1)} %collective-permute-done.15.refs_1_, bf16[16,6912]{1,0:T(8,128)(2,1)} %collective-permute-done.16.refs_2_, bf16[8,128,256]{2,1,0:T(8,128)(2,1)} %outputs_send.1.refs_3_), custom_call_target="tpu_custom_call" | custom-call | flops 1 | bytes 1 | tf_op jit(solution)/shard_map/fold2/pallas_call | solution.py:293
  70.1 0.2 fold1.4
  70.4 0.9 collective-permute-start.17
  71.3 2.6 %input_grads_send.1.refs_2_ = bf16[8,128,256]{2,1,0:T(8,128)(2,1)S(1)} custom-call(s32[2]{0:T(128)S(1)} %pad_add_fusion.refs_0_, bf16[3,18,160,128]{3,2,1,0:T(8,128)(2,1)S(1)} %hidden_grad.1.refs_2_.refs_1_, bf16[256,3456]{1,0:T(8,128)(2,1)S(1)} %copy-done.10, bf16[32,3456]{1,0:T(8,128)(2,1)S(1)} %get-tuple-element.41.refs_3_.refs_1_.refs_0_), custom_call_target="tpu_custom_call" | custom-call | flops 99999997952 | bytes 1 | tf_op jit(solution)/shard_map/input_grads_send/pallas_call | solution.py:293
  73.9 4.8 %collective-permute-start.19 = (bf16[8,6912]{1,0:T(8,128)(2,1)S(1)}, bf16[8,6912]{1,0:T(8,128)(2,1)S(1)}, u32[]{:S(2)}, u32[]{:S(2)}) collective-permute-start(bf16[8,6912]{1,0:T(8,128)(2,1)S(1)} %join2.13), channel_id=1, source_target_pairs={{0,16},{2,18},{4,20},{6,22},{8,24},{10,26},{12,28},{14,30},{16,0},... | collective-permute-start | bytes 331784 | tf_op jit(solution)/shard_map/ppermute | solution.py:307
  78.7 0.5 collective-permute-start.22
  79.3 1.0 collective-permute-start.20
  80.3 0.9 collective-permute-start.21
  81.2 2.6 %outputs.1.refs_3_.refs_0_ = f32[8,128,256]{2,1,0:T(8,128)S(1)} custom-call(s32[2]{0:T(128)S(1)} %pad_add_fusion.refs_0_, bf16[3,18,160,128]{3,2,1,0:T(8,128)(2,1)S(1)} %get-tuple-element.27.refs_1_, bf16[128,6912]{1,0:T(8,128)(2,1)S(1)} %join2.11.refs_2_, bf16[8,128,256]{2,1,0:T(8,128)(2,1)S(1)} %bitcast.10, bf16[32,3456]{1,0:T(8,128)(2,1)S(1)} %fold1.5.refs_4_.refs_1_), custom_call_target="tpu_custom_call" | custom-call | flops 99999997952 | bytes 1 | tf_op jit(solution)/shard_map/outputs/pallas_call | solution.py:293
  83.8 3.1 %collective-permute-done.21.refs_2_ = bf16[32,3456]{1,0:T(8,128)(2,1)S(1)} collective-permute-done((bf16[32,3456]{1,0:T(8,128)(2,1)S(1)}, bf16[32,3456]{1,0:T(8,128)(2,1)S(1)}, u32[]{:S(2)}, u32[]{:S(2)}) %collective-permute-start.21) | collective-permute-done | bytes 221216 | tf_op jit(solution)/shard_map/ppermute | solution.py:307
  86.9 1.2 %collective-permute-done.20.refs_1_ = bf16[32,3456]{1,0:T(8,128)(2,1)S(1)} collective-permute-done((bf16[32,3456]{1,0:T(8,128)(2,1)S(1)}, bf16[32,3456]{1,0:T(8,128)(2,1)S(1)}, u32[]{:S(2)}, u32[]{:S(2)}) %collective-permute-start.20) | collective-permute-done | bytes 221216 | tf_op jit(solution)/shard_map/ppermute | solution.py:307
  88.2 0.1 fold1.6
  88.2 1.9 %collective-permute-start.23 = (bf16[16,3456]{1,0:T(8,128)(2,1)S(1)}, bf16[16,3456]{1,0:T(8,128)(2,1)S(1)}, u32[]{:S(2)}, u32[]{:S(2)}) collective-permute-start(bf16[16,3456]{1,0:T(8,128)(2,1)S(1)} %get-tuple-element.45), channel_id=1, source_target_pairs={{0,16},{2,18},{4,20},{6,22},{8,24},{10,26},{12,28},{14,30},{16,0},... | collective-permute-start | bytes 331784 | tf_op jit(solution)/shard_map/ppermute | solution.py:307
  90.2 2.6 %input_grads.1.refs_2_.refs_0_ = f32[8,128,256]{2,1,0:T(8,128)S(1)} custom-call(s32[2]{0:T(128)S(1)} %pad_add_fusion.refs_0_, bf16[3,18,160,128]{3,2,1,0:T(8,128)(2,1)S(1)} %hidden_grad.1.refs_2_.refs_1_, bf16[256,3456]{1,0:T(8,128)(2,1)S(1)} %copy-done.10, bf16[8,128,256]{2,1,0:T(8,128)(2,1)S(1)} %bitcast.13, ...), custom_call_target="tpu_custom_call" | custom-call | flops 10000000000 | bytes 1 | tf_op jit(solution)/shard_map/input_grads/pallas_call | solution.py:293
  92.9 0.9 collective-permute-start.25
  93.8 2.0 %finish.2.refs_2_ = bf16[8,128,256]{2,1,0:T(8,128)(2,1)} custom-call(f32[8,128,256]{2,1,0:T(8,128)S(1)} %outputs.1.refs_3_.refs_0_, bf16[8,128,256]{2,1,0:T(8,128)(2,1)} %collective-permute-done.18.refs_1_, f32[16,6912]{1,0:T(8,128)S(1)} %base2.1.refs_2_.refs_3_), custom_call_target="tpu_custom_call" | custom-call | flops 1 | bytes 1 | tf_op jit(solution)/shard_map/finish/pallas_call | solution.py:293
  95.8 1.1 %copy-done.4 = bf16[8,128,256]{2,1,0:T(8,128)(2,1)S(1)} copy-done((bf16[8,128,256]{2,1,0:T(8,128)(2,1)S(1)}, bf16[8,128,256]{2,1,0:T(8,128)(2,1)}, u32[]{:S(2)}) %copy-start.4) | copy-done | bytes 524312
  96.9 0.9 finish.3.refs_2_
  97.8 1.0 copy-done.5
  98.8 1.3 %collective-permute-start.24 = (bf16[16,3456]{1,0:T(8,128)(2,1)S(1)}, bf16[16,3456]{1,0:T(8,128)(2,1)S(1)}, u32[]{:S(2)}, u32[]{:S(2)}) collective-permute-start(bf16[16,3456]{1,0:T(8,128)(2,1)S(1)} %fold1.7.refs_4_.refs_1_), channel_id=1, source_target_pairs={{0,1},{1,0},{2,3},{3,2},{4,5},{5,4},{6,7},{7,6},{8,9},{9,8},{10,11... | collective-permute-start | bytes 331784 | tf_op jit(solution)/shard_map/ppermute | solution.py:307
  100.1 1.4 %update_second.1.refs_4_ = f32[16,6912]{1,0:T(8,128)} custom-call(s32[2]{0:T(128)S(1)} %pad_add_fusion.refs_0_, bf16[8,6912]{1,0:T(8,128)(2,1)S(1)} %fold2.7.refs_2_.refs_1_, bf16[8,6912]{1,0:T(8,128)(2,1)S(1)} %collective-permute-done.25.refs_2_, f32[16,6912]{1,0:T(8,128)S(1)} %base2.1.refs_2_.refs_3_, bf16[16,3456]{1,0:T(8,128)(2,1)S(1)} %fold1.7.refs_4_.refs_1_), custom_call_target="tpu_custom_call" | custom-call | flops 1 | bytes 1 | tf_op jit(solution)/shard_map/update_second/pallas_call | solution.py:293
  101.5 2.1 %collective-permute-done.24.refs_2_ = bf16[16,3456]{1,0:T(8,128)(2,1)S(1)} collective-permute-done((bf16[16,3456]{1,0:T(8,128)(2,1)S(1)}, bf16[16,3456]{1,0:T(8,128)(2,1)S(1)}, u32[]{:S(2)}, u32[]{:S(2)}) %collective-permute-start.24) | collective-permute-done | bytes 110624 | tf_op jit(solution)/shard_map/ppermute | solution.py:307
  103.7 1.0 copy-done.8
  104.7 1.6 %update_first.1 = f32[16,6912]{1,0:T(8,128)} custom-call(s32[2]{0:T(128)S(1)} %pad_add_fusion.refs_0_, bf16[16,3456]{1,0:T(8,128)(2,1)S(1)} %fold1.7.refs_4_.refs_1_, bf16[16,3456]{1,0:T(8,128)(2,1)S(1)} %collective-permute-done.24.refs_2_, f32[16,6912]{1,0:T(8,128)S(1)} %copy-done.3, f32[16,6912]{1,0:T(8,128)S(1)} %copy-done.8), custom_call_target="tpu_custom_call" | custom-call | flops 1 | bytes 1 | tf_op jit(solution)/shard_map/update_first/pallas_call | solution.py:293
  (77 shorter events, 0.8 us)
Async XLA Ops:
  0.7 1.0 copy-start.6
  2.6 9.5 %collective-permute-start.1 = (bf16[16,3456]{1,0:T(8,128)(2,1)S(1)}, bf16[16,3456]{1,0:T(8,128)(2,1)S(1)}, u32[]{:S(2)}, u32[]{:S(2)}) collective-permute-start(bf16[16,3456]{1,0:T(8,128)(2,1)S(1)} %first_columns.1.refs_0_), channel_id=1, source_target_pairs={{0,16},{2,18},{4,20},{6,22},{8,24},{10,26},{12,28},{14,30},{16,0},... | collective-permute-start | bytes 331784 | tf_op jit(solution)/shard_map/ppermute | solution.py:307
  6.7 16.0 %collective-permute-start = (bf16[8,128,256]{2,1,0:T(8,128)(2,1)}, bf16[8,128,256]{2,1,0:T(8,128)(2,1)S(1)}, u32[]{:S(2)}, u32[]{:S(2)}) collective-permute-start(bf16[8,128,256]{2,1,0:T(8,128)(2,1)} %bitcast.8), channel_id=1, source_target_pairs={{0,1},{1,0},{2,3},{3,2},{4,5},{5,4},{6,7},{7,6},{8,9},{9,8},{10,11... | collective-permute-start | bytes 1572872 | tf_op jit(solution)/shard_map/ppermute | solution.py:307
  8.2 30.9 %collective-permute-start.10 = (bf16[8,128,256]{2,1,0:T(8,128)(2,1)}, bf16[8,128,256]{2,1,0:T(8,128)(2,1)}, u32[]{:S(2)}, u32[]{:S(2)}) collective-permute-start(bf16[8,128,256]{2,1,0:T(8,128)(2,1)} %bitcast.11), channel_id=1, source_target_pairs={{0,1},{1,0},{2,3},{3,2},{4,5},{5,4},{6,7},{7,6},{8,9},{9,8},{10,11... | collective-permute-start | bytes 1572872 | tf_op jit(solution)/shard_map/ppermute | solution.py:307
  12.2 10.5 %collective-permute-start.3 = (bf16[32,3456]{1,0:T(8,128)(2,1)S(1)}, bf16[32,3456]{1,0:T(8,128)(2,1)S(1)}, u32[]{:S(2)}, u32[]{:S(2)}) collective-permute-start(bf16[32,3456]{1,0:T(8,128)(2,1)S(1)} %join1.4.refs_2_.refs_0_), channel_id=1, source_target_pairs={{0,4},{2,6},{4,0},{6,2},{8,12},{10,14},{12,8},{14,10},{16,20},{18,... | collective-permute-start | bytes 663560 | tf_op jit(solution)/shard_map/ppermute | solution.py:307
  13.8 6.0 %collective-permute-start.2 = (bf16[32,3456]{1,0:T(8,128)(2,1)S(1)}, bf16[32,3456]{1,0:T(8,128)(2,1)S(1)}, u32[]{:S(2)}, u32[]{:S(2)}) collective-permute-start(bf16[32,3456]{1,0:T(8,128)(2,1)S(1)} %join1.4.refs_2_.refs_0_), channel_id=1, source_target_pairs={{0,8},{2,10},{4,12},{6,14},{8,0},{10,2},{12,4},{14,6},{16,24},{18,... | collective-permute-start | bytes 663560 | tf_op jit(solution)/shard_map/ppermute | solution.py:307
  14.5 1.0 copy-start.16
  15.5 7.2 %copy-start.21 = (bf16[1,8,8,16,256]{4,3,2,1,0:T(8,128)(2,1)S(1)}, bf16[1,8,8,16,256]{4,3,2,1,0:T(8,128)(2,1)}, u32[]{:S(2)}) copy-start(bf16[1,8,8,16,256]{4,3,2,1,0:T(8,128)(2,1)} %param.6) | copy-start | bytes 1572868
  16.1 10.6 %collective-permute-start.6 = (bf16[8,6912]{1,0:T(8,128)(2,1)S(1)}, bf16[8,6912]{1,0:T(8,128)(2,1)S(1)}, u32[]{:S(2)}, u32[]{:S(2)}) collective-permute-start(bf16[8,6912]{1,0:T(8,128)(2,1)S(1)} %second_rows.1.refs_3_.refs_0_), channel_id=1, source_target_pairs={{0,16},{2,18},{4,20},{6,22},{8,24},{10,26},{12,28},{14,30},{16,0},... | collective-permute-start | bytes 331784 | tf_op jit(solution)/shard_map/ppermute | solution.py:307
  19.8 6.7 %collective-permute-start.4 = (bf16[32,3456]{1,0:T(8,128)(2,1)S(1)}, bf16[32,3456]{1,0:T(8,128)(2,1)S(1)}, u32[]{:S(2)}, u32[]{:S(2)}) collective-permute-start(bf16[32,3456]{1,0:T(8,128)(2,1)S(1)} %collective-permute-done.2.refs_1_), channel_id=1, source_target_pairs={{0,4},{2,6},{4,0},{6,2},{8,12},{10,14},{12,8},{14,10},{16,20},{18,... | collective-permute-start | bytes 663560 | tf_op jit(solution)/shard_map/ppermute | solution.py:307
  22.7 1.8 %copy-start.7 = (f32[16,6912]{1,0:T(8,128)S(1)}, f32[16,6912]{1,0:T(8,128)}, u32[]{:S(2)}) copy-start(f32[16,6912]{1,0:T(8,128)} %refs_0_.2) | copy-start | bytes 1327108
  22.7 1.8 %copy-start.15 = (f32[16,6912]{1,0:T(8,128)S(1)}, f32[16,6912]{1,0:T(8,128)}, u32[]{:S(2)}) copy-start(f32[16,6912]{1,0:T(8,128)} %refs_1_.6) | copy-start | bytes 1327108
  24.4 2.2 %copy-start.11 = (bf16[256,2048]{1,0:T(8,128)(2,1)}, bf16[256,2048]{1,0:T(8,128)(2,1)S(1)}, u32[]{:S(2)}) copy-start(bf16[256,2048]{1,0:T(8,128)(2,1)S(1)} %get-tuple-element.26.refs_2_.refs_0_) | copy-start | bytes 3145732
  24.5 2.2 %copy-start.2 = (f32[16,6912]{1,0:T(8,128)}, f32[16,6912]{1,0:T(8,128)S(1)}, u32[]{:S(2)}) copy-start(f32[16,6912]{1,0:T(8,128)S(1)} %base1.1.refs_2_.refs_3_) | copy-start | bytes 1327108
  26.6 2.5 %collective-permute-start.5 = (bf16[128,3456]{1,0:T(8,128)(2,1)S(1)}, bf16[128,3456]{1,0:T(8,128)(2,1)S(1)}, u32[]{:S(2)}, u32[]{:S(2)}) collective-permute-start(bf16[128,3456]{1,0:T(8,128)(2,1)S(1)} %join1.6.refs_2_.refs_1_), channel_id=1, source_target_pairs={{0,2},{2,0},{4,6},{6,4},{8,10},{10,8},{12,14},{14,12},{16,18},{18,... | collective-permute-start | bytes 2654216 | tf_op jit(solution)/shard_map/ppermute | solution.py:307
  26.7 12.3 %collective-permute-start.8 = (bf16[16,6912]{1,0:T(8,128)(2,1)S(1)}, bf16[16,6912]{1,0:T(8,128)(2,1)S(1)}, u32[]{:S(2)}, u32[]{:S(2)}) collective-permute-start(bf16[16,6912]{1,0:T(8,128)(2,1)S(1)} %join2.7.refs_3_.refs_0_), channel_id=1, source_target_pairs={{0,4},{2,6},{4,0},{6,2},{8,12},{10,14},{12,8},{14,10},{16,20},{18,... | collective-permute-start | bytes 663560 | tf_op jit(solution)/shard_map/ppermute | solution.py:307
  28.8 8.1 %collective-permute-start.7 = (bf16[16,6912]{1,0:T(8,128)(2,1)S(1)}, bf16[16,6912]{1,0:T(8,128)(2,1)S(1)}, u32[]{:S(2)}, u32[]{:S(2)}) collective-permute-start(bf16[16,6912]{1,0:T(8,128)(2,1)S(1)} %join2.7.refs_3_.refs_0_), channel_id=1, source_target_pairs={{0,8},{2,10},{4,12},{6,14},{8,0},{10,2},{12,4},{14,6},{16,24},{18,... | collective-permute-start | bytes 663560 | tf_op jit(solution)/shard_map/ppermute | solution.py:307
  29.8 7.1 %copy-start.9 = (bf16[256,3456]{1,0:T(8,128)(2,1)}, bf16[256,3456]{1,0:T(8,128)(2,1)S(1)}, u32[]{:S(2)}) copy-start(bf16[256,3456]{1,0:T(8,128)(2,1)S(1)} %place1.1.refs_2_) | copy-start | bytes 5308420
  36.9 2.2 %copy-start.23 = (bf16[1,8,8,16,256]{4,3,2,1,0:T(8,128)(2,1)S(1)}, bf16[1,8,8,16,256]{4,3,2,1,0:T(8,128)(2,1)}, u32[]{:S(2)}) copy-start(bf16[1,8,8,16,256]{4,3,2,1,0:T(8,128)(2,1)} %param.7) | copy-start | bytes 1572868
  36.9 8.6 %collective-permute-start.9 = (bf16[16,6912]{1,0:T(8,128)(2,1)S(1)}, bf16[16,6912]{1,0:T(8,128)(2,1)S(1)}, u32[]{:S(2)}, u32[]{:S(2)}) collective-permute-start(bf16[16,6912]{1,0:T(8,128)(2,1)S(1)} %join2.9), channel_id=1, source_target_pairs={{0,4},{2,6},{4,0},{6,2},{8,12},{10,14},{12,8},{14,10},{16,20},{18,... | collective-permute-start | bytes 663560 | tf_op jit(solution)/shard_map/ppermute | solution.py:307
  41.0 4.4 %copy-start = (bf16[3,18,160,256]{3,2,1,0:T(8,128)(2,1)}, bf16[3,18,160,256]{3,2,1,0:T(8,128)(2,1)S(1)}, u32[]{:S(2)}) copy-start(bf16[3,18,160,256]{3,2,1,0:T(8,128)(2,1)S(1)} %spread_cotangent.1.refs_1_) | copy-start | bytes 13271044
  45.4 2.5 %collective-permute-start.12 = (bf16[64,6912]{1,0:T(8,128)(2,1)S(1)}, bf16[64,6912]{1,0:T(8,128)(2,1)S(1)}, u32[]{:S(2)}, u32[]{:S(2)}) collective-permute-start(bf16[64,6912]{1,0:T(8,128)(2,1)S(1)} %get-tuple-element.31), channel_id=1, source_target_pairs={{0,2},{2,0},{4,6},{6,4},{8,10},{10,8},{12,14},{14,12},{16,18},{18,... | collective-permute-start | bytes 2654216 | tf_op jit(solution)/shard_map/ppermute | solution.py:307
  45.6 3.6 %collective-permute-start.11 = (bf16[64,6912]{1,0:T(8,128)(2,1)S(1)}, bf16[64,6912]{1,0:T(8,128)(2,1)S(1)}, u32[]{:S(2)}, u32[]{:S(2)}) collective-permute-start(bf16[64,6912]{1,0:T(8,128)(2,1)S(1)} %join2.10.refs_2_.refs_0_), channel_id=1, source_target_pairs={{0,2},{2,0},{4,6},{6,4},{8,10},{10,8},{12,14},{14,12},{16,18},{18,... | collective-permute-start | bytes 2654216 | tf_op jit(solution)/shard_map/ppermute | solution.py:307
  47.9 2.3 %copy-start.1 = (bf16[3,18,160,256]{3,2,1,0:T(8,128)(2,1)S(1)}, bf16[3,18,160,256]{3,2,1,0:T(8,128)(2,1)}, u32[]{:S(2)}) copy-start(bf16[3,18,160,256]{3,2,1,0:T(8,128)(2,1)} %copy-done) | copy-start | bytes 13271044
  48.1 10.6 %collective-permute-start.13 = (bf16[16,6912]{1,0:T(8,128)(2,1)S(1)}, bf16[16,6912]{1,0:T(8,128)(2,1)S(1)}, u32[]{:S(2)}, u32[]{:S(2)}) collective-permute-start(bf16[16,6912]{1,0:T(8,128)(2,1)S(1)} %get-tuple-element.34), channel_id=1, source_target_pairs={{0,4},{2,6},{4,0},{6,2},{8,12},{10,14},{12,8},{14,10},{16,20},{18,... | collective-permute-start | bytes 663560 | tf_op jit(solution)/shard_map/ppermute | solution.py:307
  49.3 0.7 copy-start.13
  57.1 3.2 %copy-start.12 = (bf16[256,2048]{1,0:T(8,128)(2,1)S(1)}, bf16[256,2048]{1,0:T(8,128)(2,1)}, u32[]{:S(2)}) copy-start(bf16[256,2048]{1,0:T(8,128)(2,1)} %copy-done.11) | copy-start | bytes 3145732
  57.8 10.9 %collective-permute-start.16 = (bf16[16,6912]{1,0:T(8,128)(2,1)}, bf16[16,6912]{1,0:T(8,128)(2,1)}, u32[]{:S(2)}, u32[]{:S(2)}) collective-permute-start(bf16[16,6912]{1,0:T(8,128)(2,1)} %join2.12), channel_id=1, source_target_pairs={{0,4},{2,6},{4,0},{6,2},{8,12},{10,14},{12,8},{14,10},{16,20},{18,... | collective-permute-start | bytes 663560 | tf_op jit(solution)/shard_map/ppermute | solution.py:307
  59.4 9.3 %collective-permute-start.15 = (bf16[16,6912]{1,0:T(8,128)(2,1)}, bf16[16,6912]{1,0:T(8,128)(2,1)}, u32[]{:S(2)}, u32[]{:S(2)}) collective-permute-start(bf16[16,6912]{1,0:T(8,128)(2,1)} %fold2.5.refs_2_), channel_id=1, source_target_pairs={{0,8},{2,10},{4,12},{6,14},{8,0},{10,2},{12,4},{14,6},{16,24},{18,... | collective-permute-start | bytes 663560 | tf_op jit(solution)/shard_map/ppermute | solution.py:307
  64.3 5.8 %collective-permute-start.14 = (bf16[128,3456]{1,0:T(8,128)(2,1)S(1)}, bf16[128,3456]{1,0:T(8,128)(2,1)S(1)}, u32[]{:S(2)}, u32[]{:S(2)}) collective-permute-start(bf16[128,3456]{1,0:T(8,128)(2,1)S(1)} %get-tuple-element.36), channel_id=1, source_target_pairs={{0,2},{2,0},{4,6},{6,4},{8,10},{10,8},{12,14},{14,12},{16,18},{18,... | collective-permute-start | bytes 2654216 | tf_op jit(solution)/shard_map/ppermute | solution.py:307
  64.4 4.3 %copy-start.14 = (bf16[16,6912]{1,0:T(8,128)(2,1)S(1)}, bf16[16,6912]{1,0:T(8,128)(2,1)}, u32[]{:S(2)}) copy-start(bf16[16,6912]{1,0:T(8,128)(2,1)} %copy-done.13) | copy-start | bytes 663556
  67.8 3.5 %copy-start.10 = (bf16[256,3456]{1,0:T(8,128)(2,1)S(1)}, bf16[256,3456]{1,0:T(8,128)(2,1)}, u32[]{:S(2)}) copy-start(bf16[256,3456]{1,0:T(8,128)(2,1)} %copy-done.9) | copy-start | bytes 5308420
  67.8 26.0 %collective-permute-start.18 = (bf16[8,128,256]{2,1,0:T(8,128)(2,1)}, bf16[8,128,256]{2,1,0:T(8,128)(2,1)}, u32[]{:S(2)}, u32[]{:S(2)}) collective-permute-start(bf16[8,128,256]{2,1,0:T(8,128)(2,1)} %outputs_send.1.refs_3_), channel_id=1, source_target_pairs={{0,1},{1,0},{2,3},{3,2},{4,5},{5,4},{6,7},{7,6},{8,9},{9,8},{10,11... | collective-permute-start | bytes 1572872 | tf_op jit(solution)/shard_map/ppermute | solution.py:307
  70.1 3.8 %copy-start.19 = (bf16[8,6912]{1,0:T(8,128)(2,1)}, bf16[8,6912]{1,0:T(8,128)(2,1)S(1)}, u32[]{:S(2)}) copy-start(bf16[8,6912]{1,0:T(8,128)(2,1)S(1)} %get-tuple-element.38.refs_2_.refs_0_) | copy-start | bytes 331780
  70.4 8.9 %collective-permute-start.17 = (bf16[32,3456]{1,0:T(8,128)(2,1)S(1)}, bf16[32,3456]{1,0:T(8,128)(2,1)S(1)}, u32[]{:S(2)}, u32[]{:S(2)}) collective-permute-start(bf16[32,3456]{1,0:T(8,128)(2,1)S(1)} %get-tuple-element.40), channel_id=1, source_target_pairs={{0,4},{2,6},{4,0},{6,2},{8,12},{10,14},{12,8},{14,10},{16,20},{18,... | collective-permute-start | bytes 663560 | tf_op jit(solution)/shard_map/ppermute | solution.py:307
  73.9 7.3 %copy-start.22 = (bf16[1,8,8,16,256]{4,3,2,1,0:T(8,128)(2,1)S(1)}, bf16[1,8,8,16,256]{4,3,2,1,0:T(8,128)(2,1)}, u32[]{:S(2)}) copy-start(bf16[1,8,8,16,256]{4,3,2,1,0:T(8,128)(2,1)} %param.6) | copy-start | bytes 1572868
  73.9 18.9 %collective-permute-start.19 = (bf16[8,6912]{1,0:T(8,128)(2,1)S(1)}, bf16[8,6912]{1,0:T(8,128)(2,1)S(1)}, u32[]{:S(2)}, u32[]{:S(2)}) collective-permute-start(bf16[8,6912]{1,0:T(8,128)(2,1)S(1)} %join2.13), channel_id=1, source_target_pairs={{0,16},{2,18},{4,20},{6,22},{8,24},{10,26},{12,28},{14,30},{16,0},... | collective-permute-start | bytes 331784 | tf_op jit(solution)/shard_map/ppermute | solution.py:307
  78.7 17.1 %collective-permute-start.22 = (bf16[8,128,256]{2,1,0:T(8,128)(2,1)S(1)}, bf16[8,128,256]{2,1,0:T(8,128)(2,1)S(1)}, u32[]{:S(2)}, u32[]{:S(2)}) collective-permute-start(bf16[8,128,256]{2,1,0:T(8,128)(2,1)S(1)} %input_grads_send.1.refs_2_), channel_id=1, source_target_pairs={{0,1},{1,0},{2,3},{3,2},{4,5},{5,4},{6,7},{7,6},{8,9},{9,8},{10,11... | collective-permute-start | bytes 1572872 | tf_op jit(solution)/shard_map/ppermute | solution.py:307
  79.3 8.8 %collective-permute-start.20 = (bf16[32,3456]{1,0:T(8,128)(2,1)S(1)}, bf16[32,3456]{1,0:T(8,128)(2,1)S(1)}, u32[]{:S(2)}, u32[]{:S(2)}) collective-permute-start(bf16[32,3456]{1,0:T(8,128)(2,1)S(1)} %fold1.5.refs_4_.refs_1_), channel_id=1, source_target_pairs={{0,8},{2,10},{4,12},{6,14},{8,0},{10,2},{12,4},{14,6},{16,24},{18,... | collective-permute-start | bytes 663560 | tf_op jit(solution)/shard_map/ppermute | solution.py:307
  80.3 9.9 %copy-start.24 = (bf16[1,8,8,16,256]{4,3,2,1,0:T(8,128)(2,1)S(1)}, bf16[1,8,8,16,256]{4,3,2,1,0:T(8,128)(2,1)}, u32[]{:S(2)}) copy-start(bf16[1,8,8,16,256]{4,3,2,1,0:T(8,128)(2,1)} %param.7) | copy-start | bytes 1572868
  80.3 6.6 %collective-permute-start.21 = (bf16[32,3456]{1,0:T(8,128)(2,1)S(1)}, bf16[32,3456]{1,0:T(8,128)(2,1)S(1)}, u32[]{:S(2)}, u32[]{:S(2)}) collective-permute-start(bf16[32,3456]{1,0:T(8,128)(2,1)S(1)} %join1.7), channel_id=1, source_target_pairs={{0,4},{2,6},{4,0},{6,2},{8,12},{10,14},{12,8},{14,10},{16,20},{18,... | collective-permute-start | bytes 663560 | tf_op jit(solution)/shard_map/ppermute | solution.py:307
  88.2 9.5 %collective-permute-start.23 = (bf16[16,3456]{1,0:T(8,128)(2,1)S(1)}, bf16[16,3456]{1,0:T(8,128)(2,1)S(1)}, u32[]{:S(2)}, u32[]{:S(2)}) collective-permute-start(bf16[16,3456]{1,0:T(8,128)(2,1)S(1)} %get-tuple-element.45), channel_id=1, source_target_pairs={{0,16},{2,18},{4,20},{6,22},{8,24},{10,26},{12,28},{14,30},{16,0},... | collective-permute-start | bytes 331784 | tf_op jit(solution)/shard_map/ppermute | solution.py:307
  90.2 2.7 %copy-start.20 = (bf16[8,6912]{1,0:T(8,128)(2,1)S(1)}, bf16[8,6912]{1,0:T(8,128)(2,1)}, u32[]{:S(2)}) copy-start(bf16[8,6912]{1,0:T(8,128)(2,1)} %copy-done.19) | copy-start | bytes 331780
  90.2 3.6 %copy-start.17 = (f32[16,6912]{1,0:T(8,128)S(1)}, f32[16,6912]{1,0:T(8,128)}, u32[]{:S(2)}) copy-start(f32[16,6912]{1,0:T(8,128)} %refs_0_.3) | copy-start | bytes 1327108
  90.2 3.6 %copy-start.18 = (f32[16,6912]{1,0:T(8,128)S(1)}, f32[16,6912]{1,0:T(8,128)}, u32[]{:S(2)}) copy-start(f32[16,6912]{1,0:T(8,128)} %refs_1_.7) | copy-start | bytes 1327108
  92.9 7.3 %collective-permute-start.25 = (bf16[8,6912]{1,0:T(8,128)(2,1)S(1)}, bf16[8,6912]{1,0:T(8,128)(2,1)S(1)}, u32[]{:S(2)}, u32[]{:S(2)}) collective-permute-start(bf16[8,6912]{1,0:T(8,128)(2,1)S(1)} %fold2.7.refs_2_.refs_1_), channel_id=1, source_target_pairs={{0,1},{1,0},{2,3},{3,2},{4,5},{5,4},{6,7},{7,6},{8,9},{9,8},{10,11... | collective-permute-start | bytes 331784 | tf_op jit(solution)/shard_map/ppermute | solution.py:307
  95.8 7.9 %copy-start.3 = (f32[16,6912]{1,0:T(8,128)S(1)}, f32[16,6912]{1,0:T(8,128)}, u32[]{:S(2)}) copy-start(f32[16,6912]{1,0:T(8,128)} %copy-done.2) | copy-start | bytes 1327108
  95.8 1.1 %copy-start.4 = (bf16[8,128,256]{2,1,0:T(8,128)(2,1)S(1)}, bf16[8,128,256]{2,1,0:T(8,128)(2,1)}, u32[]{:S(2)}) copy-start(bf16[8,128,256]{2,1,0:T(8,128)(2,1)} %finish.2.refs_2_) | copy-start | bytes 1572868
  97.8 1.0 copy-start.5
  98.8 4.8 %collective-permute-start.24 = (bf16[16,3456]{1,0:T(8,128)(2,1)S(1)}, bf16[16,3456]{1,0:T(8,128)(2,1)S(1)}, u32[]{:S(2)}, u32[]{:S(2)}) collective-permute-start(bf16[16,3456]{1,0:T(8,128)(2,1)S(1)} %fold1.7.refs_4_.refs_1_), channel_id=1, source_target_pairs={{0,1},{1,0},{2,3},{3,2},{4,5},{5,4},{6,7},{7,6},{8,9},{9,8},{10,11... | collective-permute-start | bytes 331784 | tf_op jit(solution)/shard_map/ppermute | solution.py:307
  103.7 1.0 copy-start.8
